TPU v7x, 512 devices: a whole 4x4x16 slice. The times are simulated.
512 devices in a mesh: space: 128 (over x_lo, y, z), chan: 4 (over x_hi, core).
Axes of the slice: x: 4 (x_hi: 2, x_lo: 2; x = x_hi * 2 + x_lo), y: 4, z: 16, core: 2. Of those that a mesh axis runs over, the one named last changes fastest.
Arguments:
- inputs: bfloat16 [2, 512, 256, 128], P(None, 'space', 'chan'), may hold values from -6 to 6
- weights: bfloat16 [3, 3, 256, 256], P(None, None, 'chan'), may hold values from -0.125 to 0.125
- target: bfloat16 [2, 512, 256, 128], P(None, 'space', 'chan'), may hold values from -15 to 15
Outputs:
- loss: float32 [], replicated
- grad_input: bfloat16 [2, 512, 256, 128], P(None, 'space', 'chan')
- weight_grad: float32 [3, 3, 256, 256], P(None, None, 'chan')
All inputs are finite; a program needn't handle non-finite values.
Results may differ from a plain program's by a relative error of at most 0.0047.
Values may be sent and summed in bfloat16 or wider, within the bound.
No kernel may reach another device: no remote copies, remote signals or barrier semaphores. Data moves between devices by JAX's collectives and lax.ppermute only.
A program may use at most 64 MiB of HBM per device.

v0:
```python
import jax
import jax.numpy as jnp
from jax import lax
from jax.sharding import PartitionSpec as P

scale_factor = 64.0


def extended(block, sides, width):
    for axis, dim in sides:
        count = lax.axis_size(axis)
        forward = [(i, i + 1) for i in range(count - 1)]
        forward.append((count - 1, 0))
        backward = [(target, source) for source, target in forward]
        low = lax.ppermute(
            lax.slice_in_dim(block, block.shape[dim] - width, None, axis=dim), axis, forward
        )
        high = lax.ppermute(lax.slice_in_dim(block, 0, width, axis=dim), axis, backward)
        block = jnp.concatenate([low, block, high], axis=dim)
    return block


def tap_block(block, shift_lat, shift_lon, columns, rows):
    return block[
        :, 1 + shift_lon : 1 + shift_lon + columns, :, 1 + shift_lat : 1 + shift_lat + rows
    ]


def forward_terms(block, kernel, columns, rows):
    total = jnp.zeros((block.shape[0], columns, kernel.shape[3], rows), jnp.float32)
    for row_tap in range(3):
        for col_tap in range(3):
            moved = tap_block(block, row_tap - 1, col_tap - 1, columns, rows)
            total = total + jnp.einsum(
                "bjci,cd->bjdi", moved, kernel[row_tap, col_tap], preferred_element_type=jnp.float32
            )
    return total


def local(inputs, weights, target):
    batch_size, lon_cols, own_chan, lat_rows = inputs.shape
    channels = weights.shape[3]
    lon_total = lon_cols * lax.axis_size("space")
    rimmed = extended(inputs, (("space", 1),), 1)
    framed = jnp.pad(rimmed, ((0, 0), (0, 0), (0, 0), (1, 1)))
    predicted = lax.psum_scatter(
        forward_terms(framed, weights, lon_cols, lat_rows), "chan", scatter_dimension=2, tiled=True
    )
    coslat = jnp.cos(jnp.pi * ((jnp.arange(lat_rows, dtype=jnp.float32) + 0.5) / lat_rows - 0.5))
    weighting = coslat[None, None, None, :]
    diff = predicted - target.astype(jnp.float32)
    partial_loss = 0.5 * jnp.sum(weighting * diff * diff)
    loss = lax.psum(partial_loss, ("space", "chan")) / (
        batch_size * lat_rows * lon_total * channels
    )
    cotangent = (weighting * diff).astype(jnp.bfloat16)
    cot_rim = extended(cotangent, (("space", 1),), 1)
    cot_framed = jnp.pad(cot_rim, ((0, 0), (0, 0), (0, 0), (1, 1)))
    start_grad = jnp.zeros((batch_size, lon_cols, own_chan, lat_rows), jnp.float32)
    piece = lax.all_gather(cot_framed, "chan", axis=2, tiled=True)
    grad_sum = start_grad
    centre = tap_block(piece, 0, 0, lon_cols, lat_rows)
    kernel_rows = []
    for row_tap in range(3):
        kernel_list = []
        for col_tap in range(3):
            back = tap_block(piece, 1 - row_tap, 1 - col_tap, lon_cols, lat_rows)
            grad_sum = grad_sum + jnp.einsum(
                "bjdi,cd->bjci", back, weights[row_tap, col_tap], preferred_element_type=jnp.float32
            )
            moved = tap_block(framed, row_tap - 1, col_tap - 1, lon_cols, lat_rows)
            kernel_list.append(
                jnp.einsum("bjci,bjdi->cd", moved, centre, preferred_element_type=jnp.float32)
            )
        kernel_rows.append(jnp.stack(kernel_list))
    fresh = jnp.stack(kernel_rows)
    kernel_sum = fresh
    grad_sum, kernel_sum = (grad_sum, kernel_sum)
    weight_grad = lax.psum(kernel_sum, "space") * (
        scale_factor / (batch_size * lat_rows * lon_total)
    )
    grad_input = grad_sum.astype(jnp.bfloat16)
    return (loss, grad_input, weight_grad)


def solution(mesh):
    in_specs = (
        P(None, "space", "chan", None),
        P(None, None, "chan", None),
        P(None, "space", "chan", None),
    )
    out_specs = (P(), P(None, "space", "chan", None), P(None, None, "chan", None))
    return jax.shard_map(local, mesh=mesh, in_specs=in_specs, out_specs=out_specs, check_vma=False)
```

profile of v0, /device:TPU:6, one launch (start us, length us, event | category | flops | bytes accessed | tf_op | source)
XLA Modules:
  0.0 1336.4 jit_solution(7341413563788531224)
XLA Ops:
  7.2 0.8 fusion.86
  8.1 3.8 collective-permute-start
  11.9 12.2 collective-permute-start.1
  24.1 1.2 fusion.46
  25.3 0.3 collective-permute-done.1
  25.7 1.1 fusion.20
  26.8 1.2 fusion.25
  28.0 0.4 fusion.28
  28.4 0.3 fusion.33
  28.9 0.3 convolution_add_fusion.4
  29.2 0.3 convolution_add_fusion.3
  29.6 0.3 fusion.1
  29.9 0.3 fusion.3
  30.3 0.3 copy-done.3
  30.6 0.4 fusion
  31.0 1.3 copy.25
  32.4 1.3 dynamic-slice
  34.4 53.8 %all-reduce.8.cloned.1.call-done = f32[2,4,256,128]{3,1,0,2:T(4,128)} async-done(((f32[2,4,256,128]{3,1,0,2:T(4,128)}), f32[2,4,256,128]{3,1,0,2:T(4,128)}) %all-reduce.8.cloned.1.call-update) | async-done | bytes 1048592
  88.2 1.7 multiply_convert_fusion
  90.0 3.5 collective-permute-start.2
  93.4 6.9 collective-permute-start.3
  101.0 100.5 %psum.14 = f32[]{:T(128)} all-reduce(f32[]{:T(128)S(6)} %mul.39), channel_id=1, replica_groups=mesh['space'=128,'chan'=4] {'space','chan'}, use_global_device_ids=true, to_apply=%region_2.3 | all-reduce | flops 1 | bytes 8 | tf_op jit(solution)/shard_map/psum | solution.py:53
  202.6 0.5 pad.8.clone
  203.1 14.0 %all_gather.3 = bf16[2,6,256,130]{3,0,1,2:T(2,128)(2,1)S(1)} all-gather(bf16[2,6,64,130]{3,0,1,2:T(2,128)(2,1)S(1)} %pad.8.clone), channel_id=1, replica_groups=mesh['space'=128,'chan'=4] {'chan'}, dimensions={2}, use_global_device_ids=true | all-gather | bytes 998400 | tf_op jit(solution)/shard_map/all_gather | solution.py:60
  217.1 5.3 fusion.84
  224.4 0.3 convolution_bitcast_fusion.3
  225.1 0.9 pad_maximum_fusion
  226.0 1.3 fusion.14
  227.3 1.3 convolution_add_fusion.12
  229.8 0.9 fusion.5
  230.7 1095.8 %all-reduce.6.cloned.1.call-done = f32[3,3,64,256]{3,2,1,0:T(8,128)} async-done(((f32[3,3,64,256]{3,2,1,0:T(8,128)}), f32[3,3,64,256]{3,2,1,0:T(8,128)}) %all-reduce.6.cloned.1.call-update) | async-done | bytes 589840 | tf_op jit(solution)/shard_map/psum | solution.py:79
  1326.5 1.9 broadcast_multiply_fusion
  (49 shorter events, 4.3 us)
Async XLA Ops:
  7.2 81.0 %all-reduce.8.cloned.1.call-start = ((), (), s32[]{:S(2)}) async-start(), calls=%async_computation.1 | async-start | bytes 2097152
  7.2 20.8 %copy-start.5 = (bf16[3,3,64,256]{3,2,1,0:T(8,128)(2,1)S(1)}, bf16[3,3,64,256]{3,2,1,0:T(8,128)(2,1)}, u32[]{:S(2)}) copy-start(bf16[3,3,64,256]{3,2,1,0:T(8,128)(2,1)} %param.4) | copy-start | bytes 884740
  8.1 17.3 %collective-permute-start = (bf16[2,1,64,128]{3,2,1,0:T(8,128)(2,1)S(1)}, bf16[2,1,64,128]{3,2,1,0:T(8,128)(2,1)S(1)}, u32[]{:S(2)}, u32[]{:S(2)}) collective-permute-start(bf16[2,1,64,128]{3,2,1,0:T(8,128)(2,1)S(1)} %get-tuple-element.18), channel_id=1, source_target_pairs={{0,4},{4,8},{8,12},{12,16},{16,20},{20,24},{24,28},{28,32},{32,36}... | collective-permute-start | bytes 98312 | tf_op jit(solution)/shard_map/ppermute | solution.py:15
  11.9 13.8 %collective-permute-start.1 = (bf16[2,1,64,128]{3,2,1,0:T(8,128)(2,1)S(1)}, bf16[2,1,64,128]{3,2,1,0:T(8,128)(2,1)S(1)}, u32[]{:S(2)}, u32[]{:S(2)}) collective-permute-start(bf16[2,1,64,128]{3,2,1,0:T(8,128)(2,1)S(1)} %get-tuple-element.19), channel_id=1, source_target_pairs={{4,0},{8,4},{12,8},{16,12},{20,16},{24,20},{28,24},{32,28},{36,32}... | collective-permute-start | bytes 98312 | tf_op jit(solution)/shard_map/ppermute | solution.py:18
  26.8 2.0 copy-start.1
  28.9 0.7 copy-start.7
  29.9 0.7 copy-start.3
  31.0 57.2 %copy-start.9 = (bf16[2,4,64,128]{3,2,1,0:T(8,128)(2,1)S(1)}, bf16[2,4,64,128]{3,2,1,0:T(8,128)(2,1)}, u32[]{:S(2)}) copy-start(bf16[2,4,64,128]{3,2,1,0:T(8,128)(2,1)} %param.5) | copy-start | bytes 393220
  32.4 1294.1 %all-reduce.6.cloned.1.call-start = ((), (), s32[]{:S(2)}) async-start(), calls=%async_computation | async-start | bytes 1179648 | tf_op jit(solution)/shard_map/psum | solution.py:79
  90.0 112.2 %collective-permute-start.2 = (bf16[2,1,64,128]{3,1,0,2:T(2,128)(2,1)S(1)}, bf16[2,1,64,128]{3,1,0,2:T(2,128)(2,1)S(1)}, u32[]{:S(2)}, u32[]{:S(2)}) collective-permute-start(bf16[2,1,64,128]{3,1,0,2:T(2,128)(2,1)S(1)} %get-tuple-element.14), channel_id=1, source_target_pairs={{0,4},{4,8},{8,12},{12,16},{16,20},{20,24},{24,28},{28,32},{32,36}... | collective-permute-start | bytes 98312 | tf_op jit(solution)/shard_map/ppermute | solution.py:15
  93.4 108.7 %collective-permute-start.3 = (bf16[2,1,64,128]{3,1,0,2:T(2,128)(2,1)S(1)}, bf16[2,1,64,128]{3,1,0,2:T(2,128)(2,1)S(1)}, u32[]{:S(2)}, u32[]{:S(2)}) collective-permute-start(bf16[2,1,64,128]{3,1,0,2:T(2,128)(2,1)S(1)} %get-tuple-element.15), channel_id=1, source_target_pairs={{4,0},{8,4},{12,8},{16,12},{20,16},{24,20},{28,24},{32,28},{36,32}... | collective-permute-start | bytes 98312 | tf_op jit(solution)/shard_map/ppermute | solution.py:18
  217.1 5.3 copy-start.8
  217.1 5.6 copy-start.4
  222.7 1.1 copy-start.2
  225.0 1.0 copy-start.6
  225.9 2.6 copy-start
Sparse Core Ops, SparseCore 0:
  32.5 55.6 all-reduce.7
  226.1 1100.4 all-reduce.5
where the time goes:
time: 1340 us
  waiting for transfers between devices  1150 us (86%)
  blocking collectives  115 us (9%)
  starting transfers between devices  26.5 us (2%)
  between operations  17.5 us (1%)
    psum x1, waiting for transfers between devices, local(): lax.psum(kernel_sum, 'space')  1100 us
    psum x1, blocking collectives, local(): lax.psum(partial_loss, ('space', 'chan'))  100 us
    unnamed x3, waiting for transfers between devices  53.8 us
  transfers between devices with their start and end apart: 6, of which 3 were waited for; matrix products, arithmetic and copies ran while one was open for 1% of the time, Pallas kernels for 0%

commit v1 on v0

--- a/solution.py
+++ b/solution.py
@@ -43,16 +43,15 @@
     lon_total = lon_cols * lax.axis_size("space")
     rimmed = extended(inputs, (("space", 1),), 1)
     framed = jnp.pad(rimmed, ((0, 0), (0, 0), (0, 0), (1, 1)))
-    predicted = lax.psum_scatter(
-        forward_terms(framed, weights, lon_cols, lat_rows), "chan", scatter_dimension=2, tiled=True
-    )
+    partial = forward_terms(framed, weights, lon_cols, lat_rows)
+    partial = partial.reshape(batch_size, lon_cols, channels // own_chan, own_chan, lat_rows)
+    partial = jnp.moveaxis(partial, 2, 0)
+    predicted = jnp.sum(lax.all_to_all(partial, "chan", 0, 0, tiled=True), axis=0)
     coslat = jnp.cos(jnp.pi * ((jnp.arange(lat_rows, dtype=jnp.float32) + 0.5) / lat_rows - 0.5))
     weighting = coslat[None, None, None, :]
     diff = predicted - target.astype(jnp.float32)
     partial_loss = 0.5 * jnp.sum(weighting * diff * diff)
-    loss = lax.psum(partial_loss, ("space", "chan")) / (
-        batch_size * lat_rows * lon_total * channels
-    )
+    partial_loss = jnp.sum(lax.all_gather(jnp.full((8, 128), partial_loss), "chan")[:, 0, 0])
     cotangent = (weighting * diff).astype(jnp.bfloat16)
     cot_rim = extended(cotangent, (("space", 1),), 1)
     cot_framed = jnp.pad(cot_rim, ((0, 0), (0, 0), (0, 0), (1, 1)))
@@ -74,11 +73,18 @@
             )
         kernel_rows.append(jnp.stack(kernel_list))
     fresh = jnp.stack(kernel_rows)
-    kernel_sum = fresh
-    grad_sum, kernel_sum = (grad_sum, kernel_sum)
-    weight_grad = lax.psum(kernel_sum, "space") * (
-        scale_factor / (batch_size * lat_rows * lon_total)
-    )
+    count = lax.axis_size("space")
+    parts = fresh.astype(jnp.bfloat16).reshape(count, 8, fresh.size // (8 * count))
+    high = partial_loss.astype(jnp.bfloat16)
+    low = (partial_loss - high.astype(jnp.float32)).astype(jnp.bfloat16)
+    tail = jnp.broadcast_to(jnp.stack([high, low])[None, None, :], (count, 8, 2))
+    parts = jnp.concatenate([parts, tail], axis=2)
+    summed = jnp.sum(lax.all_to_all(parts, "space", 0, 0, tiled=True).astype(jnp.float32), axis=0)
+    loss = (summed[0, -2] + summed[0, -1]) / (batch_size * lat_rows * lon_total * channels)
+    own = (summed[:, :-2] * (scale_factor / (batch_size * lat_rows * lon_total))).astype(jnp.bfloat16)
+    everyone = jnp.broadcast_to(own[None], (count,) + own.shape)
+    weight_grad = lax.all_to_all(everyone, "space", 0, 0, tiled=True)
+    weight_grad = weight_grad.astype(jnp.float32).reshape(fresh.shape)
     grad_input = grad_sum.astype(jnp.bfloat16)
     return (loss, grad_input, weight_grad)
 

time: 1340 us -> 173 us (0.13)
  waiting for transfers between devices: 1150 us -> 70.7 us
  blocking collectives: 115 us -> 22.4 us
  starting transfers between devices: 26.5 us -> 48.2 us
    psum x1 -> x0, waiting for transfers between devices: 1100 us -> none  [local(): lax.psum(kernel_sum, 'space')]
    psum x1 -> x0, blocking collectives: 100 us -> none  [local(): lax.psum(partial_loss, ('space', 'chan'))]
    all_to_all x0 -> x3, waiting for transfers between devices: none -> 70.3 us  [the longest x1 30.9 us: local(): lax.all_to_all(parts, 'space', 0, 0, tiled=True).astype(jnp.float32)]
    unnamed x3 -> x0, waiting for transfers between devices: 53.8 us -> none
    all_to_all x0 -> x3, starting transfers between devices: none -> 21.8 us  [the longest x1 8.56 us: local(): weight_grad = lax.all_to_all(everyone, 'space', 0, 0, tiled=True)]
  transfers between devices with their start and end apart: 6 -> 7, of which waited for: 3 -> 4; matrix products, arithmetic and copies ran while one was open for 1% -> 5% of each run, Pallas kernels for 0% -> 0%
where the time goes in v1:
time: 173 us; the launch traced here: 171 us
  waiting for transfers between devices  70.7 us (41%)
  starting transfers between devices  48.2 us (28%)
  blocking collectives  22.4 us (13%)
  matrix products  11 us (6%)
  local copies, waits for them, and re-layouts  9.12 us (5%)
  between operations  5.27 us (3%)
  other arithmetic  3.91 us (2%)
    all_to_all x1, waiting for transfers between devices, local(): lax.all_to_all(parts, 'space', 0, 0, tiled=True).astype(jnp.float32)  30.9 us
    all_to_all x1, waiting for transfers between devices, local(): weight_grad = lax.all_to_all(everyone, 'space', 0, 0, tiled=True)  27.9 us
    ppermute x2, starting transfers between devices, extended(): lax.ppermute(lax.slice_in_dim(block, 0, width, axis=dim), axis, backward)  20.6 us
    all_gather x1, blocking collectives, local(): piece = lax.all_gather(cot_framed, 'chan', axis=2, tiled=True)  12.5 us
    all_to_all x1, waiting for transfers between devices, local(): lax.all_to_all(partial, 'chan', 0, 0, tiled=True)  11.5 us
    unnamed x1, blocking collectives  9.9 us
    all_to_all x1, starting transfers between devices, local(): weight_grad = lax.all_to_all(everyone, 'space', 0, 0, tiled=True)  8.56 us
    all_to_all x1, starting transfers between devices, local(): lax.all_to_all(parts, 'space', 0, 0, tiled=True).astype(jnp.float32)  8.34 us
  transfers between devices with their start and end apart: 7, of which 4 were waited for; matrix products, arithmetic and copies ran while one was open for 5% of the time, Pallas kernels for 0%

profile of v1, /device:TPU:6, one launch (start us, length us, event | category | flops | bytes accessed | tf_op | source)
XLA Modules:
  0.0 170.6 jit_solution(7269533694665472298)
XLA Ops:
  0.6 0.8 fusion.100
  1.5 3.8 %collective-permute-start = (bf16[2,1,64,128]{3,2,1,0:T(8,128)(2,1)S(1)}, bf16[2,1,64,128]{3,2,1,0:T(8,128)(2,1)S(1)}, u32[]{:S(2)}, u32[]{:S(2)}) collective-permute-start(bf16[2,1,64,128]{3,2,1,0:T(8,128)(2,1)S(1)} %get-tuple-element.9), channel_id=1, source_target_pairs={{0,4},{4,8},{8,12},{12,16},{16,20},{20,24},{24,28},{28,32},{32,36}... | collective-permute-start | bytes 98312 | tf_op jit(solution)/shard_map/ppermute | solution.py:15
  5.3 12.2 %collective-permute-start.1 = (bf16[2,1,64,128]{3,2,1,0:T(8,128)(2,1)S(1)}, bf16[2,1,64,128]{3,2,1,0:T(8,128)(2,1)S(1)}, u32[]{:S(2)}, u32[]{:S(2)}) collective-permute-start(bf16[2,1,64,128]{3,2,1,0:T(8,128)(2,1)S(1)} %get-tuple-element.10), channel_id=1, source_target_pairs={{4,0},{8,4},{12,8},{16,12},{20,16},{24,20},{28,24},{32,28},{36,32}... | collective-permute-start | bytes 98312 | tf_op jit(solution)/shard_map/ppermute | solution.py:18
  17.5 1.2 fusion.60
  19.1 1.1 select_maximum_fusion.2
  20.5 0.4 fusion.39
  21.0 0.4 fusion.42
  22.1 0.5 copy-done
  23.4 0.4 fusion
  24.2 1.0 copy.8
  25.2 4.9 %all-to-all-start = ((f32[4,2,4,64,128]{4,3,2,1,0:T(8,128)}), f32[4,2,4,64,128]{4,3,2,1,0:T(8,128)S(1)}, u32[]{:S(2)}, u32[]{:S(2)}) async-start(f32[4,2,4,64,128]{4,3,2,1,0:T(8,128)} %copy.8), calls=%async_computation | async-start | bytes 2097152 | tf_op jit(solution)/shard_map/all_to_all | solution.py:49
  30.1 1.3 dynamic-slice
  31.4 11.5 %all-to-all-done = f32[4,2,4,64,128]{4,3,2,1,0:T(8,128)S(1)} async-done(((f32[4,2,4,64,128]{4,3,2,1,0:T(8,128)}), f32[4,2,4,64,128]{4,3,2,1,0:T(8,128)S(1)}, u32[]{:S(2)}, u32[]{:S(2)}) %all-to-all-start) | async-done | bytes 1048608 | tf_op jit(solution)/shard_map/all_to_all | solution.py:49
  43.0 0.7 fusion.35
  43.7 1.9 %collective-permute-start.2 = (bf16[2,1,64,128]{3,2,1,0:T(8,128)(2,1)S(1)}, bf16[2,1,64,128]{3,2,1,0:T(8,128)(2,1)S(1)}, u32[]{:S(2)}, u32[]{:S(2)}) collective-permute-start(bf16[2,1,64,128]{3,2,1,0:T(8,128)(2,1)S(1)} %get-tuple-element.5), channel_id=1, source_target_pairs={{0,4},{4,8},{8,12},{12,16},{16,20},{20,24},{24,28},{28,32},{32,36}... | collective-permute-start | bytes 98312 | tf_op jit(solution)/shard_map/ppermute | solution.py:15
  46.3 0.8 dynamic-update-slice
  47.0 8.4 %collective-permute-start.3 = (bf16[2,1,64,128]{3,2,1,0:T(8,128)(2,1)S(1)}, bf16[2,1,64,128]{3,2,1,0:T(8,128)(2,1)S(1)}, u32[]{:S(2)}, u32[]{:S(2)}) collective-permute-start(bf16[2,1,64,128]{3,2,1,0:T(8,128)(2,1)S(1)} %get-tuple-element.6), channel_id=1, source_target_pairs={{4,0},{8,4},{12,8},{16,12},{20,16},{24,20},{28,24},{32,28},{36,32}... | collective-permute-start | bytes 98312 | tf_op jit(solution)/shard_map/ppermute | solution.py:18
  55.5 9.9 %all-reduce.2 = f32[4]{0:T(128)S(1)} all-reduce(f32[4]{0:T(128)S(1)} %dynamic-update-slice), channel_id=2, replica_groups=mesh['space'=128,'chan'=4] {'chan'}, use_global_device_ids=true, to_apply=%add.2 | all-reduce | flops 4 | bytes 32
  65.4 0.6 reduce_sum.38
  67.6 12.5 %all_gather.6 = bf16[2,6,256,130]{3,2,1,0:T(8,128)(2,1)S(1)} all-gather(bf16[2,6,64,130]{3,2,1,0:T(8,128)(2,1)S(1)} %select_maximum_fusion), channel_id=1, replica_groups=mesh['space'=128,'chan'=4] {'chan'}, dimensions={2}, use_global_device_ids=true | all-gather | bytes 998400 | tf_op jit(solution)/shard_map/all_gather | solution.py:59
  82.3 0.4 fusion.19
  82.7 0.4 fusion.18
  83.6 1.0 convert_element_type.35
  84.6 0.9 pad_maximum_fusion
  85.5 8.3 %all-to-all-start.1 = ((bf16[128,8,146]{2,1,0:T(8,128)(2,1)}), bf16[128,8,146]{2,1,0:T(8,128)(2,1)S(1)}, u32[]{:S(2)}, u32[]{:S(2)}) async-start(bf16[128,8,146]{2,1,0:T(8,128)(2,1)} %pad_maximum_fusion), calls=%async_computation.1 | async-start | bytes 1048576 | tf_op jit(solution)/shard_map/all_to_all | solution.py:82
  95.3 30.9 %all-to-all-done.1 = bf16[128,8,146]{2,1,0:T(8,128)(2,1)S(1)} async-done(((bf16[128,8,146]{2,1,0:T(8,128)(2,1)}), bf16[128,8,146]{2,1,0:T(8,128)(2,1)S(1)}, u32[]{:S(2)}, u32[]{:S(2)}) %all-to-all-start.1) | async-done | bytes 299040 | tf_op jit(solution)/shard_map/all_to_all | solution.py:82
  126.4 0.8 broadcast_in_dim.5
  127.3 8.6 %all-to-all-start.2 = ((bf16[128,8,144]{2,1,0:T(8,128)(2,1)}), bf16[128,8,144]{2,1,0:T(8,128)(2,1)S(1)}, u32[]{:S(2)}, u32[]{:S(2)}) async-start(bf16[128,8,144]{2,1,0:T(8,128)(2,1)} %broadcast_in_dim.5), calls=%async_computation.2 | async-start | bytes 1048576 | tf_op jit(solution)/shard_map/all_to_all | solution.py:86
  137.0 0.9 fusion.5
  137.9 0.6 fusion.101
  139.7 27.9 %all-to-all-done.2 = bf16[128,8,144]{2,1,0:T(8,128)(2,1)S(1)} async-done(((bf16[128,8,144]{2,1,0:T(8,128)(2,1)}), bf16[128,8,144]{2,1,0:T(8,128)(2,1)S(1)}, u32[]{:S(2)}, u32[]{:S(2)}) %all-to-all-start.2) | async-done | bytes 294944 | tf_op jit(solution)/shard_map/all_to_all | solution.py:86
  167.6 1.8 %reshape.35 = f32[3,3,64,256]{3,2,1,0:T(8,128)} reshape(bf16[128,8,144]{2,1,0:T(8,128)(2,1)S(1)} %all-to-all-done.2) | data formatting | bytes 884736 | tf_op jit(solution)/shard_map/reshape | solution.py:87
  (44 shorter events, 8.2 us)
Async XLA Ops:
  0.6 19.6 %copy-start.1 = (bf16[3,3,64,256]{3,2,1,0:T(8,128)(2,1)S(1)}, bf16[3,3,64,256]{3,2,1,0:T(8,128)(2,1)}, u32[]{:S(2)}) copy-start(bf16[3,3,64,256]{3,2,1,0:T(8,128)(2,1)} %param.4) | copy-start | bytes 884740
  1.5 17.3 %collective-permute-start = (bf16[2,1,64,128]{3,2,1,0:T(8,128)(2,1)S(1)}, bf16[2,1,64,128]{3,2,1,0:T(8,128)(2,1)S(1)}, u32[]{:S(2)}, u32[]{:S(2)}) collective-permute-start(bf16[2,1,64,128]{3,2,1,0:T(8,128)(2,1)S(1)} %get-tuple-element.9), channel_id=1, source_target_pairs={{0,4},{4,8},{8,12},{12,16},{16,20},{20,24},{24,28},{28,32},{32,36}... | collective-permute-start | bytes 98312 | tf_op jit(solution)/shard_map/ppermute | solution.py:15
  5.3 13.8 %collective-permute-start.1 = (bf16[2,1,64,128]{3,2,1,0:T(8,128)(2,1)S(1)}, bf16[2,1,64,128]{3,2,1,0:T(8,128)(2,1)S(1)}, u32[]{:S(2)}, u32[]{:S(2)}) collective-permute-start(bf16[2,1,64,128]{3,2,1,0:T(8,128)(2,1)S(1)} %get-tuple-element.10), channel_id=1, source_target_pairs={{4,0},{8,4},{12,8},{16,12},{20,16},{24,20},{28,24},{32,28},{36,32}... | collective-permute-start | bytes 98312 | tf_op jit(solution)/shard_map/ppermute | solution.py:18
  21.7 0.9 copy-start
  25.2 17.8 %copy-start.2 = (bf16[2,4,64,128]{3,2,1,0:T(8,128)(2,1)S(1)}, bf16[2,4,64,128]{3,2,1,0:T(8,128)(2,1)}, u32[]{:S(2)}) copy-start(bf16[2,4,64,128]{3,2,1,0:T(8,128)(2,1)} %param.5) | copy-start | bytes 393220
  25.2 17.7 %all-to-all-start = ((f32[4,2,4,64,128]{4,3,2,1,0:T(8,128)}), f32[4,2,4,64,128]{4,3,2,1,0:T(8,128)S(1)}, u32[]{:S(2)}, u32[]{:S(2)}) async-start(f32[4,2,4,64,128]{4,3,2,1,0:T(8,128)} %copy.8), calls=%async_computation | async-start | bytes 2097152 | tf_op jit(solution)/shard_map/all_to_all | solution.py:49
  43.7 23.7 %collective-permute-start.2 = (bf16[2,1,64,128]{3,2,1,0:T(8,128)(2,1)S(1)}, bf16[2,1,64,128]{3,2,1,0:T(8,128)(2,1)S(1)}, u32[]{:S(2)}, u32[]{:S(2)}) collective-permute-start(bf16[2,1,64,128]{3,2,1,0:T(8,128)(2,1)S(1)} %get-tuple-element.5), channel_id=1, source_target_pairs={{0,4},{4,8},{8,12},{12,16},{16,20},{20,24},{24,28},{28,32},{32,36}... | collective-permute-start | bytes 98312 | tf_op jit(solution)/shard_map/ppermute | solution.py:15
  47.0 20.3 %collective-permute-start.3 = (bf16[2,1,64,128]{3,2,1,0:T(8,128)(2,1)S(1)}, bf16[2,1,64,128]{3,2,1,0:T(8,128)(2,1)S(1)}, u32[]{:S(2)}, u32[]{:S(2)}) collective-permute-start(bf16[2,1,64,128]{3,2,1,0:T(8,128)(2,1)S(1)} %get-tuple-element.6), channel_id=1, source_target_pairs={{4,0},{8,4},{12,8},{16,12},{20,16},{24,20},{28,24},{32,28},{36,32}... | collective-permute-start | bytes 98312 | tf_op jit(solution)/shard_map/ppermute | solution.py:18
  85.5 40.8 %all-to-all-start.1 = ((bf16[128,8,146]{2,1,0:T(8,128)(2,1)}), bf16[128,8,146]{2,1,0:T(8,128)(2,1)S(1)}, u32[]{:S(2)}, u32[]{:S(2)}) async-start(bf16[128,8,146]{2,1,0:T(8,128)(2,1)} %pad_maximum_fusion), calls=%async_computation.1 | async-start | bytes 1048576 | tf_op jit(solution)/shard_map/all_to_all | solution.py:82
  127.3 40.4 %all-to-all-start.2 = ((bf16[128,8,144]{2,1,0:T(8,128)(2,1)}), bf16[128,8,144]{2,1,0:T(8,128)(2,1)S(1)}, u32[]{:S(2)}, u32[]{:S(2)}) async-start(bf16[128,8,144]{2,1,0:T(8,128)(2,1)} %broadcast_in_dim.5), calls=%async_computation.2 | async-start | bytes 1048576 | tf_op jit(solution)/shard_map/all_to_all | solution.py:86

commit v2 on v0

v2 whole, which is shorter than its diff:
```python
import jax
import jax.numpy as jnp
from jax import lax
from jax.experimental import pallas as pl
from jax.experimental.pallas import tpu as pltpu
from jax.sharding import Mesh
from jax.sharding import PartitionSpec as P

scale_factor = 64.0
SPACE = ("xlo", "y", "zhi", "zlo")
CHAN = ("xhi", "core")
NEAR = ("xlo", "y", "zlo")
BF16, F32 = jnp.bfloat16, jnp.float32


def shift_lanes(x, step):
    rows, lat = x.shape
    lane = lax.broadcasted_iota(jnp.int32, (rows, lat), 1)
    if step == 1:
        return jnp.where(lane == lat - 1, 0.0, pltpu.roll(x, lat - 1, 1))
    return jnp.where(lane == 0, 0.0, pltpu.roll(x, 1, 1))


def kernel(
    where_ref, own_ref, oth_ref, left_ref, right_ref, wt_ref, wown_ref, cos_ref,
    gi_ref, wg_ref, loss_ref, xs_ref, tg_ref, cot_ref,
):
    xhi, core = where_ref[0], where_ref[1]
    batch, cols, chans, lat = gi_ref.shape
    wide = batch * lat
    count = 2 * batch * cols
    rim = 3 * batch

    for chip in range(2):
        main = own_ref if chip == 0 else oth_ref
        for unit in range(2):
            block = chip * 2 + unit
            row = block * 3 * chans
            trow = pl.multiple_of(((chip ^ xhi) * 2 + unit) * chans, chans)
            base, edge = unit * count, (unit * 2 + chip) * rim
            for b in range(batch):
                for e in range(cols + 4):
                    if e < 2:
                        x = left_ref[edge + b * 2 + e]
                    elif e < cols + 2:
                        x = main[base + b * cols + e - 2]
                    else:
                        x = right_ref[edge + b * 2 + e - cols - 2]
                    at = pl.ds(e * wide + b * lat, lat)
                    x32 = x.astype(F32)
                    xs_ref[row : row + chans, at] = shift_lanes(x32, -1).astype(BF16)
                    xs_ref[row + chans : row + 2 * chans, at] = x
                    xs_ref[row + 2 * chans : row + 3 * chans, at] = shift_lanes(x32, 1).astype(BF16)
                for f in range(cols + 2):
                    if f < 1:
                        t = left_ref[edge + 2 * batch + b]
                    elif f < cols + 1:
                        t = main[base + (batch + b) * cols + f - 1]
                    else:
                        t = right_ref[edge + 2 * batch + b]
                    tg_ref[pl.ds(trow, chans), pl.ds(f * wide + b * lat, lat)] = t

    weighting = cos_ref[0:1, :]
    loss = jnp.zeros((8, wide), F32)
    for f in range(cols + 2):
        at = pl.ds(f * wide, wide)
        total = jnp.dot(wt_ref[0], xs_ref[:, at], preferred_element_type=F32)
        for q in (1, 2):
            total += jnp.dot(
                wt_ref[q], xs_ref[:, pl.ds((f + q) * wide, wide)], preferred_element_type=F32
            )
        diff = total - tg_ref[:, at].astype(F32)
        cot = weighting * diff
        cot_ref[:, at] = cot.astype(BF16)
        if 1 <= f <= cols:
            loss += jnp.sum((cot * diff).reshape(-1, 8, wide), axis=0)
    loss_ref[...] = jnp.full(loss_ref.shape, jnp.sum(loss), F32)

    for j in range(cols):
        total = jnp.zeros((3 * chans, wide), F32)
        for q in range(3):
            total += jnp.dot(
                wown_ref[q], cot_ref[:, pl.ds((j + 2 - q) * wide, wide)], preferred_element_type=F32
            )
        for b in range(batch):
            part = total[:, b * lat : (b + 1) * lat]
            grad = (
                shift_lanes(part[:chans], 1)
                + part[chans : 2 * chans]
                + shift_lanes(part[2 * chans :], -1)
            )
            gi_ref[b, j] = grad.astype(BF16)

    centre = cot_ref[:, wide : (cols + 1) * wide]
    mine = pl.ds(pl.multiple_of(core * 3 * chans, chans), 3 * chans)
    for q in range(3):
        wg_ref[q] = lax.dot_general(
            xs_ref[mine, pl.ds((q + 1) * wide, cols * wide)],
            centre,
            (((1,), (1,)), ((), ())),
            preferred_element_type=F32,
        )


def exchange(a, axes, count, to):
    return lax.ppermute(a, axes, [(i, to(i)) for i in range(count)])


def local(inputs, weights, target):
    batch, cols, chans, lat = inputs.shape
    channels = weights.shape[3]
    tiles = lax.axis_size(SPACE)
    lon = cols * tiles
    near, far = lax.axis_size(NEAR), lax.axis_size("zhi")
    xhi, core = lax.axis_index("xhi"), lax.axis_index("core")

    def gathered(a):
        return lax.all_gather(a, "core", axis=0, tiled=True)

    own = jnp.concatenate(
        [inputs.reshape(-1, chans, lat), target.reshape(-1, chans, lat)], axis=0
    )
    other = exchange(own, "xhi", 2, lambda i: 1 - i)
    w_other = exchange(weights, ("xlo", "xhi"), 4, lambda i: 3 - i)

    def edge(pack, side):
        both = pack.reshape(2, batch, cols, chans, lat)
        if side > 0:
            x, t = both[0, :, cols - 2 :], both[1, :, cols - 1 :]
        else:
            x, t = both[0, :, :2], both[1, :, :1]
        return [x.reshape(-1, chans, lat), t.reshape(-1, chans, lat)]

    to_right = jnp.concatenate(edge(own, 1) + edge(other, 1), axis=0)
    to_left = jnp.concatenate(edge(own, -1) + edge(other, -1), axis=0)
    left = exchange(to_right, SPACE, tiles, lambda i: (i + 1) % tiles)
    right = exchange(to_left, SPACE, tiles, lambda i: (i - 1) % tiles)

    w_mine, w_far = gathered(weights[None]), gathered(w_other[None])
    w_all = jnp.concatenate([w_mine, w_far], axis=0)
    wt = jnp.transpose(w_all, (2, 4, 0, 1, 3)).reshape(3, channels, 3 * channels)
    wown = jnp.transpose(weights, (1, 0, 2, 3)).reshape(3, 3 * chans, channels)

    coslat = jnp.cos(jnp.pi * ((jnp.arange(lat, dtype=F32) + 0.5) / lat - 0.5))
    cos_rows = jnp.broadcast_to(jnp.tile(coslat, batch)[None], (8, batch * lat))
    place = jnp.stack([xhi, core]).astype(jnp.int32)

    wide = batch * lat
    vmem = pl.BlockSpec(memory_space=pltpu.VMEM)
    grad_input, wg, loss_part = pl.pallas_call(
        kernel,
        out_shape=(
            jax.ShapeDtypeStruct((batch, cols, chans, lat), BF16),
            jax.ShapeDtypeStruct((3, 3 * chans, channels), F32),
            jax.ShapeDtypeStruct((8, 128), F32),
        ),
        in_specs=[pl.BlockSpec(memory_space=pltpu.SMEM)] + [vmem] * 7,
        out_specs=(vmem, vmem, vmem),
        scratch_shapes=[
            pltpu.VMEM((3 * channels, (cols + 4) * wide), BF16),
            pltpu.VMEM((channels, (cols + 2) * wide), BF16),
            pltpu.VMEM((channels, (cols + 2) * wide), BF16),
        ],
        compiler_params=pltpu.CompilerParams(vmem_limit_bytes=40 * 1024 * 1024),
        name="conv_all",
    )(place, gathered(own), gathered(other), gathered(left), gathered(right), wt, wown, cos_rows)

    half = channels // 2
    rows = 9 * chans * 2 // near
    parts = jnp.concatenate([wg[:, :, :half], wg[:, :, half:]], axis=0).reshape(near, rows, half)

    def with_loss(data, value):
        high = value.astype(BF16)
        low = (value - high.astype(F32)).astype(BF16)
        row = lax.broadcasted_iota(jnp.int32, (8, half), 0)
        block = jnp.where(row == 0, high, jnp.where(row == 1, low, jnp.zeros((), BF16)))
        block = jnp.broadcast_to(block, data.shape[:1] + block.shape)
        return jnp.concatenate([data.astype(BF16), block], axis=1)

    def everyone(a, axes):
        return lax.all_to_all(a, axes, 0, 0, tiled=True)

    first = everyone(with_loss(parts, loss_part[0, 0]), NEAR)
    total = jnp.sum(first.astype(F32), axis=0)
    value = total[rows, 0] + total[rows + 1, 0]
    second = everyone(
        with_loss(jnp.broadcast_to(total[None, :rows], (far, rows, half)), value), "zhi"
    )
    total = jnp.sum(second.astype(F32), axis=0)
    value = total[rows, 0] + total[rows + 1, 0]
    loss = 0.5 * value / (batch * lat * lon * channels)
    mine = (total[:rows] * (scale_factor / (batch * lat * lon))).astype(BF16)
    third = everyone(jnp.broadcast_to(mine[None], (near, rows, half)), NEAR)
    halves = third.reshape(2, 3, 3, chans, half).astype(F32)
    weight_grad = jnp.swapaxes(jnp.concatenate([halves[0], halves[1]], axis=-1), 0, 1)
    return (loss, grad_input, weight_grad)


def solution(mesh):
    grid = Mesh(mesh.devices.reshape(2, 4, 8, 2, 2, 2), SPACE + CHAN)
    in_specs = (
        P(None, SPACE, CHAN, None),
        P(None, None, CHAN, None),
        P(None, SPACE, CHAN, None),
    )
    out_specs = (P(), P(None, SPACE, CHAN, None), P(None, None, CHAN, None))
    return jax.shard_map(local, mesh=grid, in_specs=in_specs, out_specs=out_specs, check_vma=False)
```

time: 1340 us -> 99.3 us (0.07)
  waiting for transfers between devices: 1150 us -> 6.34 us
  blocking collectives: 115 us -> 47.6 us
    psum x1 -> x0, waiting for transfers between devices: 1100 us -> none  [local(): lax.psum(kernel_sum, 'space')]
    psum x1 -> x0, blocking collectives: 100 us -> none  [local(): lax.psum(partial_loss, ('space', 'chan'))]
    unnamed x3 -> x0, waiting for transfers between devices: 53.8 us -> none
    all_to_all x0 -> x2, blocking collectives: none -> 34.4 us  [everyone(): return lax.all_to_all(a, axes, 0, 0, tiled=True)]
  transfers between devices with their start and end apart: 6 -> 5, of which waited for: 3 -> 2; matrix products, arithmetic and copies ran while one was open for 1% -> 4% of each run, Pallas kernels for 0% -> 0%
where the time goes in v2:
time: 99.3 us; the launch traced here: 98.8 us
  blocking collectives  47.6 us (48%)
  starting transfers between devices  26.9 us (27%)
  waiting for transfers between devices  6.34 us (6%)
  between operations  5.93 us (6%)
  local copies, waits for them, and re-layouts  5.01 us (5%)
  Pallas kernels  4.26 us (4%)
  other arithmetic  2.74 us (3%)
    all_to_all x2, blocking collectives, everyone(): return lax.all_to_all(a, axes, 0, 0, tiled=True)  34.4 us
    ppermute x4, starting transfers between devices, exchange(): return lax.ppermute(a, axes, [(i, to(i)) for i in range(count)])  22.9 us
    all_gather x6, blocking collectives, gathered(): return lax.all_gather(a, 'core', axis=0, tiled=True)  13.2 us
    all_to_all x1, waiting for transfers between devices, everyone(): return lax.all_to_all(a, axes, 0, 0, tiled=True)  5 us
    pallas_call x1, Pallas kernels, local(): pl.pallas_call(kernel, out_shape=(jax.ShapeDtypeStruct((batch, cols, chan...  4.26 us
    all_to_all x1, starting transfers between devices, everyone(): return lax.all_to_all(a, axes, 0, 0, tiled=True)  4.01 us
  transfers between devices with their start and end apart: 5, of which 2 were waited for; matrix products, arithmetic and copies ran while one was open for 4% of the time, Pallas kernels for 0%

profile of v2, /device:TPU:6, one launch (start us, length us, event | category | flops | bytes accessed | tf_op | source)
XLA Modules:
  0.0 98.8 jit_solution(3412986741274485158)
XLA Ops:
  0.6 0.0 copy-start
  0.6 1.0 %pad_maximum_fusion.3 = bf16[16,64,128]{2,1,0:T(8,128)(2,1)S(1)} fusion(bf16[8,64,128]{2,1,0:T(8,128)(2,1)} %bitcast.53, bf16[8,64,128]{2,1,0:T(8,128)(2,1)} %bitcast.54), kind=kLoop, calls=%fused_computation.6 | loop fusion | flops 131072 | bytes 524288 | tf_op jit(solution)/shard_map/concatenate | solution.py:120
  1.7 3.3 %collective-permute-start = (bf16[16,64,128]{2,1,0:T(8,128)(2,1)S(1)}, bf16[16,64,128]{2,1,0:T(8,128)(2,1)S(1)}, u32[]{:S(2)}, u32[]{:S(2)}) collective-permute-start(bf16[16,64,128]{2,1,0:T(8,128)(2,1)S(1)} %pad_maximum_fusion.3), channel_id=1, source_target_pairs={{0,2},{2,0},{1,3},{3,1},{4,6},{6,4},{5,7},{7,5},{8,10},{10,8},{9,1... | collective-permute-start | bytes 786440 | tf_op jit(solution)/shard_map/ppermute | solution.py:106
  5.0 6.4 %collective-permute-start.3 = (bf16[3,3,64,256]{3,2,1,0:T(8,128)(2,1)}, bf16[3,3,64,256]{3,2,1,0:T(8,128)(2,1)S(1)}, u32[]{:S(2)}, u32[]{:S(2)}) collective-permute-start(bf16[3,3,64,256]{3,2,1,0:T(8,128)(2,1)} %param.4), channel_id=1, source_target_pairs={{0,258},{2,256},{256,2},{258,0},{1,259},{3,257},{257,3},{259,1},{4... | collective-permute-start | bytes 884744 | tf_op jit(solution)/shard_map/ppermute | solution.py:106
  11.4 2.2 %all_gather.18.own_ref = bf16[32,64,128]{2,1,0:T(8,128)(2,1)S(1)} all-gather(bf16[16,64,128]{2,1,0:T(8,128)(2,1)S(1)} %pad_maximum_fusion.3), channel_id=1, replica_groups=mesh['xlo'=2,'y'=4,'zhi'=8,'zlo'=2,'xhi'=2,'core'=2] {'core'}, dimensions={0}, use_global_device_ids=true | all-gather | bytes 786432 | tf_op jit(solution)/shard_map/all_gather | solution.py:118
  13.6 2.2 %all-gather = bf16[6,3,64,256]{3,2,1,0:T(8,128)(2,1)S(1)} all-gather(bf16[3,3,64,256]{3,2,1,0:T(8,128)(2,1)S(1)} %copy-done), channel_id=2, replica_groups=mesh['xlo'=2,'y'=4,'zhi'=8,'zlo'=2,'xhi'=2,'core'=2] {'core'}, dimensions={0}, use_global_device_ids=true | all-gather | bytes 884736 | tf_op jit(solution)/shard_map/all_gather | solution.py:118
  15.9 0.1 pad_add_fusion.where_ref
  16.0 0.0 collective-permute-done
  16.1 11.3 %collective-permute-start.2 = (bf16[12,64,128]{2,1,0:T(8,128)(2,1)S(1)}, bf16[12,64,128]{2,1,0:T(8,128)(2,1)S(1)}, u32[]{:S(2)}, u32[]{:S(2)}) collective-permute-start(bf16[12,64,128]{2,1,0:T(8,128)(2,1)S(1)} %pad_maximum_fusion.5), channel_id=1, source_target_pairs={{0,508},{4,0},{8,4},{12,8},{16,12},{20,16},{24,20},{28,24},{32,28}... | collective-permute-start | bytes 589832 | tf_op jit(solution)/shard_map/ppermute | solution.py:106
  27.5 1.9 %collective-permute-start.1 = (bf16[12,64,128]{2,1,0:T(8,128)(2,1)S(1)}, bf16[12,64,128]{2,1,0:T(8,128)(2,1)}, u32[]{:S(2)}, u32[]{:S(2)}) collective-permute-start(bf16[12,64,128]{2,1,0:T(8,128)(2,1)S(1)} %pad_maximum_fusion.4), channel_id=1, source_target_pairs={{0,4},{4,8},{8,12},{12,16},{16,20},{20,24},{24,28},{28,32},{32,36}... | collective-permute-start | bytes 589832 | tf_op jit(solution)/shard_map/ppermute | solution.py:106
  29.4 2.2 %all_gather.19.oth_ref = bf16[32,64,128]{2,1,0:T(8,128)(2,1)S(1)} all-gather(bf16[16,64,128]{2,1,0:T(8,128)(2,1)S(1)} %collective-permute-done), channel_id=1, replica_groups=mesh['xlo'=2,'y'=4,'zhi'=8,'zlo'=2,'xhi'=2,'core'=2] {'core'}, dimensions={0}, use_global_device_ids=true | all-gather | bytes 786432 | tf_op jit(solution)/shard_map/all_gather | solution.py:118
  31.6 0.0 collective-permute-done.3
  31.6 2.2 %all-gather.1 = bf16[6,3,64,256]{3,2,1,0:T(8,128)(2,1)S(1)} all-gather(bf16[3,3,64,256]{3,2,1,0:T(8,128)(2,1)S(1)} %collective-permute-done.3), channel_id=3, replica_groups=mesh['xlo'=2,'y'=4,'zhi'=8,'zlo'=2,'xhi'=2,'core'=2] {'core'}, dimensions={0}, use_global_device_ids=true | all-gather | bytes 884736 | tf_op jit(solution)/shard_map/all_gather | solution.py:118
  33.8 1.1 %pad_maximum_fusion = bf16[4,3,3,64,256]{4,3,1,0,2:T(8,128)(2,1)} fusion(bf16[2,3,3,64,256]{4,3,1,0,2:T(8,128)(2,1)S(1)} %bitcast.40, bf16[2,3,3,64,256]{4,3,1,0,2:T(8,128)(2,1)S(1)} %bitcast.39), kind=kLoop, calls=%fused_computation | loop fusion | flops 589824 | bytes 2359296 | tf_op jit(solution)/shard_map/concatenate | solution.py:140
  35.0 1.6 %copy.28.wt_ref = bf16[3,256,768]{2,1,0:T(8,128)(2,1)S(1)} copy(bf16[3,256,768]{1,2,0:T(8,128)(2,1)} %bitcast.38) | data formatting | bytes 2359296 | tf_op jit(solution)/shard_map/reshape | solution.py:141
  36.5 2.1 %all_gather.21.right_ref = bf16[24,64,128]{2,1,0:T(8,128)(2,1)S(1)} all-gather(bf16[12,64,128]{2,1,0:T(8,128)(2,1)S(1)} %collective-permute-done.2), channel_id=1, replica_groups=mesh['xlo'=2,'y'=4,'zhi'=8,'zlo'=2,'xhi'=2,'core'=2] {'core'}, dimensions={0}, use_global_device_ids=true | all-gather | bytes 589824 | tf_op jit(solution)/shard_map/all_gather | solution.py:118
  38.6 1.3 %collective-permute-done.1 = bf16[12,64,128]{2,1,0:T(8,128)(2,1)} collective-permute-done((bf16[12,64,128]{2,1,0:T(8,128)(2,1)S(1)}, bf16[12,64,128]{2,1,0:T(8,128)(2,1)}, u32[]{:S(2)}, u32[]{:S(2)}) %collective-permute-start.1) | collective-permute-done | bytes 196640 | tf_op jit(solution)/shard_map/ppermute | solution.py:106
  40.0 2.3 %all_gather.20.left_ref = bf16[24,64,128]{2,1,0:T(8,128)(2,1)S(1)} all-gather(bf16[12,64,128]{2,1,0:T(8,128)(2,1)} %collective-permute-done.1), channel_id=1, replica_groups=mesh['xlo'=2,'y'=4,'zhi'=8,'zlo'=2,'xhi'=2,'core'=2] {'core'}, dimensions={0}, use_global_device_ids=true | all-gather | bytes 589824 | tf_op jit(solution)/shard_map/all_gather | solution.py:118
  42.3 4.3 %conv_all.1 = (bf16[2,4,64,128]{3,2,1,0:T(8,128)(2,1)}, f32[3,192,256]{2,1,0:T(8,128)S(1)}, f32[8,128]{1,0:T(8,128)S(1)}) custom-call(s32[2]{0:T(128)S(1)} %pad_add_fusion.where_ref, bf16[32,64,128]{2,1,0:T(8,128)(2,1)S(1)} %all_gather.18.own_ref, bf16[32,64,128]{2,1,0:T(8,128)(2,1)S(1)} %all_gather.19.oth_ref, ...), custom_call_target="tpu_custom_call" | custom-call | tf_op jit(solution)/shard_map/conv_all/pallas_call | solution.py:150
  46.5 0.5 slice.72
  48.4 0.1 fusion.2
  48.4 0.1 broadcast_select_fusion.1
  48.6 12.4 %all_to_all.15 = bf16[16,80,128]{2,1,0:T(8,128)(2,1)S(1)} all-to-all(bf16[16,80,128]{2,1,0:T(8,128)(2,1)S(1)} %pad_maximum_fusion.1), channel_id=1, replica_groups=mesh['xlo'=2,'y'=4,'zhi'=8,'zlo'=2,'xhi'=2,'core'=2] {'xlo','y','zlo'}, dimensions={0} | all-to-all | bytes 655360 | tf_op jit(solution)/shard_map/all_to_all | solution.py:181
  61.0 0.1 convert_reduce_fusion
  61.1 0.5 fusion.6
  62.9 0.1 broadcast_select_fusion
  63.0 22.0 %all_to_all.16 = bf16[8,80,128]{2,1,0:T(8,128)(2,1)S(1)} all-to-all(bf16[8,80,128]{2,1,0:T(8,128)(2,1)S(1)} %pad_maximum_fusion.6), channel_id=1, replica_groups=mesh['xlo'=2,'y'=4,'zhi'=8,'zlo'=2,'xhi'=2,'core'=2] {'zhi'}, dimensions={0} | all-to-all | bytes 327680 | tf_op jit(solution)/shard_map/all_to_all | solution.py:181
  85.1 0.8 broadcast_in_dim.62
  85.9 4.0 %all-to-all-start.2 = ((bf16[16,72,128]{2,1,0:T(8,128)(2,1)}), bf16[16,72,128]{2,1,0:T(8,128)(2,1)S(1)}, u32[]{:S(2)}, u32[]{:S(2)}) async-start(bf16[16,72,128]{2,1,0:T(8,128)(2,1)} %broadcast_in_dim.62), calls=%async_computation.2 | async-start | bytes 589824 | tf_op jit(solution)/shard_map/all_to_all | solution.py:181
  89.9 0.5 fusion.5
  91.7 5.0 %all-to-all-done.2 = bf16[16,72,128]{2,1,0:T(8,128)(2,1)S(1)} async-done(((bf16[16,72,128]{2,1,0:T(8,128)(2,1)}), bf16[16,72,128]{2,1,0:T(8,128)(2,1)S(1)}, u32[]{:S(2)}, u32[]{:S(2)}) %all-to-all-start.2) | async-done | bytes 294944 | tf_op jit(solution)/shard_map/all_to_all | solution.py:181
  96.8 0.9 copy.29
  (29 shorter events, 0.5 us)
Async XLA Ops:
  0.6 12.9 %copy-start = (bf16[3,3,64,256]{3,2,1,0:T(8,128)(2,1)S(1)}, bf16[3,3,64,256]{3,2,1,0:T(8,128)(2,1)}, u32[]{:S(2)}) copy-start(bf16[3,3,64,256]{3,2,1,0:T(8,128)(2,1)} %param.4) | copy-start | bytes 884740
  1.7 14.4 %collective-permute-start = (bf16[16,64,128]{2,1,0:T(8,128)(2,1)S(1)}, bf16[16,64,128]{2,1,0:T(8,128)(2,1)S(1)}, u32[]{:S(2)}, u32[]{:S(2)}) collective-permute-start(bf16[16,64,128]{2,1,0:T(8,128)(2,1)S(1)} %pad_maximum_fusion.3), channel_id=1, source_target_pairs={{0,2},{2,0},{1,3},{3,1},{4,6},{6,4},{5,7},{7,5},{8,10},{10,8},{9,1... | collective-permute-start | bytes 786440 | tf_op jit(solution)/shard_map/ppermute | solution.py:106
  5.0 26.6 %collective-permute-start.3 = (bf16[3,3,64,256]{3,2,1,0:T(8,128)(2,1)}, bf16[3,3,64,256]{3,2,1,0:T(8,128)(2,1)S(1)}, u32[]{:S(2)}, u32[]{:S(2)}) collective-permute-start(bf16[3,3,64,256]{3,2,1,0:T(8,128)(2,1)} %param.4), channel_id=1, source_target_pairs={{0,258},{2,256},{256,2},{258,0},{1,259},{3,257},{257,3},{259,1},{4... | collective-permute-start | bytes 884744 | tf_op jit(solution)/shard_map/ppermute | solution.py:106
  16.1 20.4 %collective-permute-start.2 = (bf16[12,64,128]{2,1,0:T(8,128)(2,1)S(1)}, bf16[12,64,128]{2,1,0:T(8,128)(2,1)S(1)}, u32[]{:S(2)}, u32[]{:S(2)}) collective-permute-start(bf16[12,64,128]{2,1,0:T(8,128)(2,1)S(1)} %pad_maximum_fusion.5), channel_id=1, source_target_pairs={{0,508},{4,0},{8,4},{12,8},{16,12},{20,16},{24,20},{28,24},{32,28}... | collective-permute-start | bytes 589832 | tf_op jit(solution)/shard_map/ppermute | solution.py:106
  27.5 12.5 %collective-permute-start.1 = (bf16[12,64,128]{2,1,0:T(8,128)(2,1)S(1)}, bf16[12,64,128]{2,1,0:T(8,128)(2,1)}, u32[]{:S(2)}, u32[]{:S(2)}) collective-permute-start(bf16[12,64,128]{2,1,0:T(8,128)(2,1)S(1)} %pad_maximum_fusion.4), channel_id=1, source_target_pairs={{0,4},{4,8},{8,12},{12,16},{16,20},{20,24},{24,28},{28,32},{32,36}... | collective-permute-start | bytes 589832 | tf_op jit(solution)/shard_map/ppermute | solution.py:106
  85.9 10.8 %all-to-all-start.2 = ((bf16[16,72,128]{2,1,0:T(8,128)(2,1)}), bf16[16,72,128]{2,1,0:T(8,128)(2,1)S(1)}, u32[]{:S(2)}, u32[]{:S(2)}) async-start(bf16[16,72,128]{2,1,0:T(8,128)(2,1)} %broadcast_in_dim.62), calls=%async_computation.2 | async-start | bytes 589824 | tf_op jit(solution)/shard_map/all_to_all | solution.py:181

commit v3 on v2

--- a/solution.py
+++ b/solution.py
@@ -22,13 +22,13 @@
 
 
 def kernel(
-    where_ref, own_ref, oth_ref, left_ref, right_ref, wt_ref, wown_ref, cos_ref,
+    where_ref, own_ref, oth_ref, rim_ref, wt_ref, wown_ref, cos_ref,
     gi_ref, wg_ref, loss_ref, xs_ref, tg_ref, cot_ref,
 ):
     xhi, core = where_ref[0], where_ref[1]
     batch, cols, chans, lat = gi_ref.shape
     wide = batch * lat
-    count = 2 * batch * cols
+    count = own_ref.shape[0] // 2
     rim = 3 * batch
 
     for chip in range(2):
@@ -37,15 +37,17 @@
             block = chip * 2 + unit
             row = block * 3 * chans
             trow = pl.multiple_of(((chip ^ xhi) * 2 + unit) * chans, chans)
-            base, edge = unit * count, (unit * 2 + chip) * rim
+            base = unit * count
+            left = (unit * 4 + chip) * rim
+            right = left + 2 * rim
             for b in range(batch):
                 for e in range(cols + 4):
                     if e < 2:
-                        x = left_ref[edge + b * 2 + e]
+                        x = rim_ref[left + b * 2 + e]
                     elif e < cols + 2:
                         x = main[base + b * cols + e - 2]
                     else:
-                        x = right_ref[edge + b * 2 + e - cols - 2]
+                        x = rim_ref[right + b * 2 + e - cols - 2]
                     at = pl.ds(e * wide + b * lat, lat)
                     x32 = x.astype(F32)
                     xs_ref[row : row + chans, at] = shift_lanes(x32, -1).astype(BF16)
@@ -53,11 +55,11 @@
                     xs_ref[row + 2 * chans : row + 3 * chans, at] = shift_lanes(x32, 1).astype(BF16)
                 for f in range(cols + 2):
                     if f < 1:
-                        t = left_ref[edge + 2 * batch + b]
+                        t = rim_ref[left + 2 * batch + b]
                     elif f < cols + 1:
                         t = main[base + (batch + b) * cols + f - 1]
                     else:
-                        t = right_ref[edge + 2 * batch + b]
+                        t = rim_ref[right + 2 * batch + b]
                     tg_ref[pl.ds(trow, chans), pl.ds(f * wide + b * lat, lat)] = t
 
     weighting = cos_ref[0:1, :]
@@ -94,12 +96,16 @@
     centre = cot_ref[:, wide : (cols + 1) * wide]
     mine = pl.ds(pl.multiple_of(core * 3 * chans, chans), 3 * chans)
     for q in range(3):
-        wg_ref[q] = lax.dot_general(
+        fresh = lax.dot_general(
             xs_ref[mine, pl.ds((q + 1) * wide, cols * wide)],
             centre,
             (((1,), (1,)), ((), ())),
             preferred_element_type=F32,
-        )
+        ).astype(BF16)
+        half = wg_ref.shape[-1]
+        for p in range(3):
+            for h in range(2):
+                wg_ref[h, p, q] = fresh[p * chans : (p + 1) * chans, h * half : (h + 1) * half]
 
 
 def exchange(a, axes, count, to):
@@ -136,9 +142,11 @@
     left = exchange(to_right, SPACE, tiles, lambda i: (i + 1) % tiles)
     right = exchange(to_left, SPACE, tiles, lambda i: (i - 1) % tiles)
 
-    w_mine, w_far = gathered(weights[None]), gathered(w_other[None])
-    w_all = jnp.concatenate([w_mine, w_far], axis=0)
+    half = channels // 2
+    near_pack, far_pack = gathered(own), gathered(other)
+    w_all = jnp.concatenate([gathered(weights[None]), gathered(w_other[None])], axis=0)
     wt = jnp.transpose(w_all, (2, 4, 0, 1, 3)).reshape(3, channels, 3 * channels)
+    rim = gathered(jnp.concatenate([left, right], axis=0))
     wown = jnp.transpose(weights, (1, 0, 2, 3)).reshape(3, 3 * chans, channels)
 
     coslat = jnp.cos(jnp.pi * ((jnp.arange(lat, dtype=F32) + 0.5) / lat - 0.5))
@@ -151,48 +159,49 @@
         kernel,
         out_shape=(
             jax.ShapeDtypeStruct((batch, cols, chans, lat), BF16),
-            jax.ShapeDtypeStruct((3, 3 * chans, channels), F32),
+            jax.ShapeDtypeStruct((2, 3, 3, chans, half), BF16),
             jax.ShapeDtypeStruct((8, 128), F32),
         ),
-        in_specs=[pl.BlockSpec(memory_space=pltpu.SMEM)] + [vmem] * 7,
+        in_specs=[pl.BlockSpec(memory_space=pltpu.SMEM)] + [vmem] * 6,
         out_specs=(vmem, vmem, vmem),
         scratch_shapes=[
             pltpu.VMEM((3 * channels, (cols + 4) * wide), BF16),
             pltpu.VMEM((channels, (cols + 2) * wide), BF16),
             pltpu.VMEM((channels, (cols + 2) * wide), BF16),
         ],
-        compiler_params=pltpu.CompilerParams(vmem_limit_bytes=40 * 1024 * 1024),
+        compiler_params=pltpu.CompilerParams(vmem_limit_bytes=16 * 1024 * 1024),
         name="conv_all",
-    )(place, gathered(own), gathered(other), gathered(left), gathered(right), wt, wown, cos_rows)
-
-    half = channels // 2
+    )(place, near_pack, far_pack, rim, wt, wown, cos_rows)
+
     rows = 9 * chans * 2 // near
-    parts = jnp.concatenate([wg[:, :, :half], wg[:, :, half:]], axis=0).reshape(near, rows, half)
+    parts = wg.reshape(near, rows, half)
 
     def with_loss(data, value):
         high = value.astype(BF16)
         low = (value - high.astype(F32)).astype(BF16)
-        row = lax.broadcasted_iota(jnp.int32, (8, half), 0)
-        block = jnp.where(row == 0, high, jnp.where(row == 1, low, jnp.zeros((), BF16)))
+        row = lax.broadcasted_iota(jnp.int32, value.shape, 0)
+        block = jnp.where(row < 4, high, low)
         block = jnp.broadcast_to(block, data.shape[:1] + block.shape)
         return jnp.concatenate([data.astype(BF16), block], axis=1)
 
     def everyone(a, axes):
         return lax.all_to_all(a, axes, 0, 0, tiled=True)
 
-    first = everyone(with_loss(parts, loss_part[0, 0]), NEAR)
-    total = jnp.sum(first.astype(F32), axis=0)
-    value = total[rows, 0] + total[rows + 1, 0]
-    second = everyone(
-        with_loss(jnp.broadcast_to(total[None, :rows], (far, rows, half)), value), "zhi"
+    def summed(a):
+        total = jnp.sum(a.astype(F32), axis=0)
+        value = total[rows : rows + 4] + total[rows + 4 :]
+        return total[:rows], value
+
+    total, value = summed(everyone(with_loss(parts, loss_part), NEAR))
+    spread = jnp.broadcast_to(total[None], (far, rows, half))
+    total, value = summed(
+        everyone(with_loss(spread, jnp.concatenate([value, value], axis=0)), "zhi")
     )
-    total = jnp.sum(second.astype(F32), axis=0)
-    value = total[rows, 0] + total[rows + 1, 0]
-    loss = 0.5 * value / (batch * lat * lon * channels)
-    mine = (total[:rows] * (scale_factor / (batch * lat * lon))).astype(BF16)
+    loss = 0.5 * value[0, 0] / (batch * lat * lon * channels)
+    mine = (total * (scale_factor / (batch * lat * lon))).astype(BF16)
     third = everyone(jnp.broadcast_to(mine[None], (near, rows, half)), NEAR)
     halves = third.reshape(2, 3, 3, chans, half).astype(F32)
-    weight_grad = jnp.swapaxes(jnp.concatenate([halves[0], halves[1]], axis=-1), 0, 1)
+    weight_grad = jnp.concatenate([halves[0], halves[1]], axis=-1)
     return (loss, grad_input, weight_grad)
 
 

time: 99.3 us -> 93.9 us (0.946)
  between operations: 5.93 us -> 2.63 us
  local copies, waits for them, and re-layouts: 5.01 us -> 3.06 us
    all_gather x6 -> x5, blocking collectives: 13.2 us -> 11.2 us  [gathered(): return lax.all_gather(a, 'core', axis=0, tiled=True)]
    all_to_all x2, blocking collectives: 34.4 us -> 36.2 us  [everyone(): return lax.all_to_all(a, axes, 0, 0, tiled=True)]
    ppermute x4, waiting for transfers between devices: 1.34 us -> 0.01 us  [exchange(): return lax.ppermute(a, axes, [(i, to(i)) for i in range(count)])]
    slice x8 -> x5, local copies, waits for them, and re-layouts: 1.69 us -> 0.58 us  [the longest x1 0.51 us: local(): loss = 0.5 * value[0, 0] / (batch * lat * lon * channels)]
    concatenate x2 -> x3, other arithmetic: 1.15 us -> 2.02 us  [the longest x1 1.12 us: local(): jnp.concatenate([gathered(weights[None]), gathered(w_other[None])], axis=0)]
  transfers between devices with their start and end apart: 5 -> 5, of which waited for: 2 -> 1; matrix products, arithmetic and copies ran while one was open for 4% -> 4% of each run, Pallas kernels for 0% -> 0%
where the time goes in v3:
time: 93.9 us; the launch traced here: 93.4 us
  blocking collectives  47.3 us (50%)
  starting transfers between devices  26.9 us (29%)
  waiting for transfers between devices  5.67 us (6%)
  Pallas kernels  4.26 us (5%)
  other arithmetic  3.53 us (4%)
  local copies, waits for them, and re-layouts  3.06 us (3%)
  between operations  2.63 us (3%)
    all_to_all x2, blocking collectives, everyone(): return lax.all_to_all(a, axes, 0, 0, tiled=True)  36.2 us
    ppermute x4, starting transfers between devices, exchange(): return lax.ppermute(a, axes, [(i, to(i)) for i in range(count)])  22.9 us
    all_gather x5, blocking collectives, gathered(): return lax.all_gather(a, 'core', axis=0, tiled=True)  11.2 us
    all_to_all x1, waiting for transfers between devices, everyone(): return lax.all_to_all(a, axes, 0, 0, tiled=True)  5.66 us
    pallas_call x1, Pallas kernels, local(): pl.pallas_call(kernel, out_shape=(jax.ShapeDtypeStruct((batch, cols, chan...  4.26 us
    all_to_all x1, starting transfers between devices, everyone(): return lax.all_to_all(a, axes, 0, 0, tiled=True)  4.01 us
  transfers between devices with their start and end apart: 5, of which 1 were waited for; matrix products, arithmetic and copies ran while one was open for 4% of the time, Pallas kernels for 0%

profile of v3, /device:TPU:6, one launch (start us, length us, event | category | flops | bytes accessed | tf_op | source)
XLA Modules:
  0.0 93.4 jit_solution(2065358744740434346)
XLA Ops:
  0.6 0.0 copy-start
  0.6 1.0 %pad_maximum_fusion.4 = bf16[16,64,128]{2,1,0:T(8,128)(2,1)S(1)} fusion(bf16[8,64,128]{2,1,0:T(8,128)(2,1)} %bitcast.51, bf16[8,64,128]{2,1,0:T(8,128)(2,1)} %bitcast.52), kind=kLoop, calls=%fused_computation.6 | loop fusion | flops 131072 | bytes 524288 | tf_op jit(solution)/shard_map/concatenate | solution.py:126
  1.7 3.3 %collective-permute-start = (bf16[16,64,128]{2,1,0:T(8,128)(2,1)S(1)}, bf16[16,64,128]{2,1,0:T(8,128)(2,1)S(1)}, u32[]{:S(2)}, u32[]{:S(2)}) collective-permute-start(bf16[16,64,128]{2,1,0:T(8,128)(2,1)S(1)} %pad_maximum_fusion.4), channel_id=1, source_target_pairs={{0,2},{2,0},{1,3},{3,1},{4,6},{6,4},{5,7},{7,5},{8,10},{10,8},{9,1... | collective-permute-start | bytes 786440 | tf_op jit(solution)/shard_map/ppermute | solution.py:112
  5.0 6.4 %collective-permute-start.3 = (bf16[3,3,64,256]{3,2,1,0:T(8,128)(2,1)}, bf16[3,3,64,256]{3,2,1,0:T(8,128)(2,1)S(1)}, u32[]{:S(2)}, u32[]{:S(2)}) collective-permute-start(bf16[3,3,64,256]{3,2,1,0:T(8,128)(2,1)} %param.4), channel_id=1, source_target_pairs={{0,258},{2,256},{256,2},{258,0},{1,259},{3,257},{257,3},{259,1},{4... | collective-permute-start | bytes 884744 | tf_op jit(solution)/shard_map/ppermute | solution.py:112
  11.4 2.2 %all_gather.15.own_ref = bf16[32,64,128]{2,1,0:T(8,128)(2,1)S(1)} all-gather(bf16[16,64,128]{2,1,0:T(8,128)(2,1)S(1)} %pad_maximum_fusion.4), channel_id=1, replica_groups=mesh['xlo'=2,'y'=4,'zhi'=8,'zlo'=2,'xhi'=2,'core'=2] {'core'}, dimensions={0}, use_global_device_ids=true | all-gather | bytes 786432 | tf_op jit(solution)/shard_map/all_gather | solution.py:124
  13.6 0.0 copy-done
  13.6 2.2 %all-gather = bf16[6,3,64,256]{3,2,1,0:T(8,128)(2,1)S(1)} all-gather(bf16[3,3,64,256]{3,2,1,0:T(8,128)(2,1)S(1)} %copy-done), channel_id=2, replica_groups=mesh['xlo'=2,'y'=4,'zhi'=8,'zlo'=2,'xhi'=2,'core'=2] {'core'}, dimensions={0}, use_global_device_ids=true | all-gather | bytes 884736 | tf_op jit(solution)/shard_map/all_gather | solution.py:124
  15.9 0.1 pad_add_fusion.where_ref
  16.0 0.0 collective-permute-done
  16.1 1.9 %collective-permute-start.1 = (bf16[12,64,128]{2,1,0:T(8,128)(2,1)S(1)}, bf16[12,64,128]{2,1,0:T(8,128)(2,1)S(1)}, u32[]{:S(2)}, u32[]{:S(2)}) collective-permute-start(bf16[12,64,128]{2,1,0:T(8,128)(2,1)S(1)} %pad_maximum_fusion.5), channel_id=1, source_target_pairs={{0,4},{4,8},{8,12},{12,16},{16,20},{20,24},{24,28},{28,32},{32,36}... | collective-permute-start | bytes 589832 | tf_op jit(solution)/shard_map/ppermute | solution.py:112
  18.1 11.3 %collective-permute-start.2 = (bf16[12,64,128]{2,1,0:T(8,128)(2,1)S(1)}, bf16[12,64,128]{2,1,0:T(8,128)(2,1)S(1)}, u32[]{:S(2)}, u32[]{:S(2)}) collective-permute-start(bf16[12,64,128]{2,1,0:T(8,128)(2,1)S(1)} %pad_maximum_fusion.6), channel_id=1, source_target_pairs={{0,508},{4,0},{8,4},{12,8},{16,12},{20,16},{24,20},{28,24},{32,28}... | collective-permute-start | bytes 589832 | tf_op jit(solution)/shard_map/ppermute | solution.py:112
  29.4 2.2 %all_gather.16.oth_ref = bf16[32,64,128]{2,1,0:T(8,128)(2,1)S(1)} all-gather(bf16[16,64,128]{2,1,0:T(8,128)(2,1)S(1)} %collective-permute-done), channel_id=1, replica_groups=mesh['xlo'=2,'y'=4,'zhi'=8,'zlo'=2,'xhi'=2,'core'=2] {'core'}, dimensions={0}, use_global_device_ids=true | all-gather | bytes 786432 | tf_op jit(solution)/shard_map/all_gather | solution.py:124
  31.6 0.0 collective-permute-done.3
  31.6 2.2 %all-gather.1 = bf16[6,3,64,256]{3,2,1,0:T(8,128)(2,1)S(1)} all-gather(bf16[3,3,64,256]{3,2,1,0:T(8,128)(2,1)S(1)} %collective-permute-done.3), channel_id=3, replica_groups=mesh['xlo'=2,'y'=4,'zhi'=8,'zlo'=2,'xhi'=2,'core'=2] {'core'}, dimensions={0}, use_global_device_ids=true | all-gather | bytes 884736 | tf_op jit(solution)/shard_map/all_gather | solution.py:124
  33.8 1.1 %pad_maximum_fusion = bf16[4,3,3,64,256]{4,3,1,0,2:T(8,128)(2,1)} fusion(bf16[2,3,3,64,256]{4,3,1,0,2:T(8,128)(2,1)S(1)} %bitcast.39, bf16[2,3,3,64,256]{4,3,1,0,2:T(8,128)(2,1)S(1)} %bitcast.38), kind=kLoop, calls=%fused_computation | loop fusion | flops 589824 | bytes 2359296 | tf_op jit(solution)/shard_map/concatenate | solution.py:147
  35.0 1.6 %copy.28.wt_ref = bf16[3,256,768]{2,1,0:T(8,128)(2,1)S(1)} copy(bf16[3,256,768]{1,2,0:T(8,128)(2,1)} %bitcast.37) | data formatting | bytes 2359296 | tf_op jit(solution)/shard_map/reshape | solution.py:148
  36.5 0.0 collective-permute-done.1
  36.5 0.0 collective-permute-done.2
  36.6 2.4 %all_gather.17.rim_ref = bf16[48,64,128]{2,1,0:T(8,128)(2,1)S(1)} all-gather(bf16[24,64,128]{2,1,0:T(8,128)(2,1)S(1)} %pad_maximum_fusion.2), channel_id=1, replica_groups=mesh['xlo'=2,'y'=4,'zhi'=8,'zlo'=2,'xhi'=2,'core'=2] {'core'}, dimensions={0}, use_global_device_ids=true | all-gather | bytes 1179648 | tf_op jit(solution)/shard_map/all_gather | solution.py:124
  39.0 4.3 %conv_all.1 = (bf16[2,4,64,128]{3,2,1,0:T(8,128)(2,1)}, bf16[2,3,3,64,128]{4,3,2,1,0:T(8,128)(2,1)S(1)}, f32[8,128]{1,0:T(8,128)S(1)}) custom-call(s32[2]{0:T(128)S(1)} %pad_add_fusion.where_ref, bf16[32,64,128]{2,1,0:T(8,128)(2,1)S(1)} %all_gather.15.own_ref, bf16[32,64,128]{2,1,0:T(8,128)(2,1)S(1)} %all_gather.16.oth_ref, ...), custom_call_target="tpu_custom_call" | custom-call | tf_op jit(solution)/shard_map/conv_all/pallas_call | solution.py:158
  43.2 0.1 fusion.4
  43.3 12.0 %all_to_all.15 = bf16[16,80,128]{2,1,0:T(8,128)(2,1)S(1)} all-to-all(bf16[16,80,128]{2,1,0:T(8,128)(2,1)S(1)} %pad_maximum_fusion.3), channel_id=1, replica_groups=mesh['xlo'=2,'y'=4,'zhi'=8,'zlo'=2,'xhi'=2,'core'=2] {'xlo','y','zlo'}, dimensions={0} | all-to-all | bytes 655360 | tf_op jit(solution)/shard_map/all_to_all | solution.py:188
  55.4 0.1 convert_reduce_fusion
  55.4 0.1 fusion.5
  55.6 24.2 %all_to_all.16 = bf16[8,80,128]{2,1,0:T(8,128)(2,1)S(1)} all-to-all(bf16[8,80,128]{2,1,0:T(8,128)(2,1)S(1)} %pad_maximum_fusion.7), channel_id=1, replica_groups=mesh['xlo'=2,'y'=4,'zhi'=8,'zlo'=2,'xhi'=2,'core'=2] {'zhi'}, dimensions={0} | all-to-all | bytes 327680 | tf_op jit(solution)/shard_map/all_to_all | solution.py:188
  79.8 0.8 broadcast_in_dim.38
  80.5 4.0 %all-to-all-start.2 = ((bf16[16,72,128]{2,1,0:T(8,128)(2,1)}), bf16[16,72,128]{2,1,0:T(8,128)(2,1)S(1)}, u32[]{:S(2)}, u32[]{:S(2)}) async-start(bf16[16,72,128]{2,1,0:T(8,128)(2,1)} %broadcast_in_dim.38), calls=%async_computation.2 | async-start | bytes 589824 | tf_op jit(solution)/shard_map/all_to_all | solution.py:188
  84.5 0.5 slice.67
  85.7 5.7 %all-to-all-done.2 = bf16[16,72,128]{2,1,0:T(8,128)(2,1)S(1)} async-done(((bf16[16,72,128]{2,1,0:T(8,128)(2,1)}), bf16[16,72,128]{2,1,0:T(8,128)(2,1)S(1)}, u32[]{:S(2)}, u32[]{:S(2)}) %all-to-all-start.2) | async-done | bytes 294944 | tf_op jit(solution)/shard_map/all_to_all | solution.py:188
  91.4 0.9 pad_maximum_fusion.1
  (25 shorter events, 0.5 us)
Async XLA Ops:
  0.6 12.9 %copy-start = (bf16[3,3,64,256]{3,2,1,0:T(8,128)(2,1)S(1)}, bf16[3,3,64,256]{3,2,1,0:T(8,128)(2,1)}, u32[]{:S(2)}) copy-start(bf16[3,3,64,256]{3,2,1,0:T(8,128)(2,1)} %param.4) | copy-start | bytes 884740
  1.7 14.4 %collective-permute-start = (bf16[16,64,128]{2,1,0:T(8,128)(2,1)S(1)}, bf16[16,64,128]{2,1,0:T(8,128)(2,1)S(1)}, u32[]{:S(2)}, u32[]{:S(2)}) collective-permute-start(bf16[16,64,128]{2,1,0:T(8,128)(2,1)S(1)} %pad_maximum_fusion.4), channel_id=1, source_target_pairs={{0,2},{2,0},{1,3},{3,1},{4,6},{6,4},{5,7},{7,5},{8,10},{10,8},{9,1... | collective-permute-start | bytes 786440 | tf_op jit(solution)/shard_map/ppermute | solution.py:112
  5.0 26.6 %collective-permute-start.3 = (bf16[3,3,64,256]{3,2,1,0:T(8,128)(2,1)}, bf16[3,3,64,256]{3,2,1,0:T(8,128)(2,1)S(1)}, u32[]{:S(2)}, u32[]{:S(2)}) collective-permute-start(bf16[3,3,64,256]{3,2,1,0:T(8,128)(2,1)} %param.4), channel_id=1, source_target_pairs={{0,258},{2,256},{256,2},{258,0},{1,259},{3,257},{257,3},{259,1},{4... | collective-permute-start | bytes 884744 | tf_op jit(solution)/shard_map/ppermute | solution.py:112
  16.1 20.4 %collective-permute-start.1 = (bf16[12,64,128]{2,1,0:T(8,128)(2,1)S(1)}, bf16[12,64,128]{2,1,0:T(8,128)(2,1)S(1)}, u32[]{:S(2)}, u32[]{:S(2)}) collective-permute-start(bf16[12,64,128]{2,1,0:T(8,128)(2,1)S(1)} %pad_maximum_fusion.5), channel_id=1, source_target_pairs={{0,4},{4,8},{8,12},{12,16},{16,20},{20,24},{24,28},{28,32},{32,36}... | collective-permute-start | bytes 589832 | tf_op jit(solution)/shard_map/ppermute | solution.py:112
  18.1 18.5 %collective-permute-start.2 = (bf16[12,64,128]{2,1,0:T(8,128)(2,1)S(1)}, bf16[12,64,128]{2,1,0:T(8,128)(2,1)S(1)}, u32[]{:S(2)}, u32[]{:S(2)}) collective-permute-start(bf16[12,64,128]{2,1,0:T(8,128)(2,1)S(1)} %pad_maximum_fusion.6), channel_id=1, source_target_pairs={{0,508},{4,0},{8,4},{12,8},{16,12},{20,16},{24,20},{28,24},{32,28}... | collective-permute-start | bytes 589832 | tf_op jit(solution)/shard_map/ppermute | solution.py:112
  80.5 10.8 %all-to-all-start.2 = ((bf16[16,72,128]{2,1,0:T(8,128)(2,1)}), bf16[16,72,128]{2,1,0:T(8,128)(2,1)S(1)}, u32[]{:S(2)}, u32[]{:S(2)}) async-start(bf16[16,72,128]{2,1,0:T(8,128)(2,1)} %broadcast_in_dim.38), calls=%async_computation.2 | async-start | bytes 589824 | tf_op jit(solution)/shard_map/all_to_all | solution.py:188

commit v4 on v3

--- a/solution.py
+++ b/solution.py
@@ -1,3 +1,5 @@
+import functools
+
 import jax
 import jax.numpy as jnp
 from jax import lax
@@ -21,56 +23,106 @@
     return jnp.where(lane == 0, 0.0, pltpu.roll(x, 1, 1))
 
 
-def kernel(
-    where_ref, own_ref, oth_ref, rim_ref, wt_ref, wown_ref, cos_ref,
-    gi_ref, wg_ref, loss_ref, xs_ref, tg_ref, cot_ref,
+def place_block(xs_ref, row, at, x):
+    chans = x.shape[0]
+    wide = x.astype(F32)
+    xs_ref[row : row + chans, at] = shift_lanes(wide, -1).astype(BF16)
+    xs_ref[row + chans : row + 2 * chans, at] = x
+    xs_ref[row + 2 * chans : row + 3 * chans, at] = shift_lanes(wide, 1).astype(BF16)
+
+
+def early_kernel(early, near_ref, far_ref, w_ref, wt_ref, xs_ref, part_ref):
+    chans, lat = near_ref.shape[1:]
+    half = far_ref.shape[2]
+    wide = part_ref.shape[1] // 6
+    batch, cols = wide // lat, xs_ref.shape[1] // wide
+    pack = (near_ref.shape[0] // 2, far_ref.shape[0] // 2)
+    weights_at = batch * cols + early
+
+    for q in range(3):
+        blocks = []
+        for block in range(4):
+            unit = block % 2
+            for p in range(3):
+                if block < 2:
+                    blocks.append(w_ref[unit * 3 + p, q])
+                else:
+                    first = unit * pack[1] + weights_at + p * 3 + q
+                    blocks.append(jnp.concatenate([far_ref[first], far_ref[first + 9]], axis=1))
+        for t in range(0, 12, 2):
+            pair = jnp.concatenate(blocks[t : t + 2], axis=0)
+            wt_ref[q, :, t * chans : (t + 2) * chans] = pair.T
+
+    for block in range(4):
+        unit, ref = block % 2, near_ref if block < 2 else far_ref
+        for b in range(batch):
+            for j in range(cols):
+                x = ref[unit * pack[block // 2] + b * cols + j]
+                place_block(xs_ref, block * 3 * chans, pl.ds(j * wide + b * lat, lat), x)
+
+    for f in range(cols + 2):
+        total = None
+        for q in range(3):
+            j = f + q - 2
+            if 0 <= j < cols:
+                term = jnp.dot(
+                    wt_ref[q], xs_ref[:, j * wide : (j + 1) * wide], preferred_element_type=F32
+                )
+                total = term if total is None else total + term
+        part_ref[:, f * wide : (f + 1) * wide] = total
+
+
+def late_kernel(
+    early, where_ref, near_ref, far_ref, rim_ref, wt_ref, xs_ref, part_ref, wown_ref, cos_ref,
+    gi_ref, wg_ref, loss_ref, xh_ref, tg_ref, cot_ref,
 ):
     xhi, core = where_ref[0], where_ref[1]
     batch, cols, chans, lat = gi_ref.shape
     wide = batch * lat
-    count = own_ref.shape[0] // 2
+    tile = batch * cols
     rim = 3 * batch
+    pack = (near_ref.shape[0] // 2, far_ref.shape[0] // 2, rim_ref.shape[0] // 2)
+
+    def outer(e):
+        return e if e < 2 else e - cols
 
     for chip in range(2):
-        main = own_ref if chip == 0 else oth_ref
         for unit in range(2):
-            block = chip * 2 + unit
-            row = block * 3 * chans
+            row = (chip * 2 + unit) * 3 * chans
             trow = pl.multiple_of(((chip ^ xhi) * 2 + unit) * chans, chans)
-            base = unit * count
-            left = (unit * 4 + chip) * rim
+            left = unit * pack[2] + chip * rim
             right = left + 2 * rim
             for b in range(batch):
-                for e in range(cols + 4):
-                    if e < 2:
-                        x = rim_ref[left + b * 2 + e]
-                    elif e < cols + 2:
-                        x = main[base + b * cols + e - 2]
-                    else:
-                        x = rim_ref[right + b * 2 + e - cols - 2]
-                    at = pl.ds(e * wide + b * lat, lat)
-                    x32 = x.astype(F32)
-                    xs_ref[row : row + chans, at] = shift_lanes(x32, -1).astype(BF16)
-                    xs_ref[row + chans : row + 2 * chans, at] = x
-                    xs_ref[row + 2 * chans : row + 3 * chans, at] = shift_lanes(x32, 1).astype(BF16)
+                for e in (0, 1, cols + 2, cols + 3):
+                    x = rim_ref[left + b * 2 + e] if e < 2 else rim_ref[right + b * 2 + e - cols - 2]
+                    place_block(xh_ref, row, pl.ds(outer(e) * wide + b * lat, lat), x)
                 for f in range(cols + 2):
+                    own = b * cols + f - 1
                     if f < 1:
                         t = rim_ref[left + 2 * batch + b]
-                    elif f < cols + 1:
-                        t = main[base + (batch + b) * cols + f - 1]
+                    elif f > cols:
+                        t = rim_ref[right + 2 * batch + b]
+                    elif chip == 0:
+                        t = near_ref[unit * pack[0] + tile + own]
+                    elif own < early:
+                        t = far_ref[unit * pack[1] + tile + own]
                     else:
-                        t = rim_ref[right + 2 * batch + b]
+                        t = rim_ref[unit * pack[2] + 4 * rim + own - early]
                     tg_ref[pl.ds(trow, chans), pl.ds(f * wide + b * lat, lat)] = t
+
+    def column(e, rows):
+        if 2 <= e < cols + 2:
+            return xs_ref[rows, pl.ds((e - 2) * wide, wide)]
+        return xh_ref[rows, pl.ds(outer(e) * wide, wide)]
 
     weighting = cos_ref[0:1, :]
     loss = jnp.zeros((8, wide), F32)
     for f in range(cols + 2):
         at = pl.ds(f * wide, wide)
-        total = jnp.dot(wt_ref[0], xs_ref[:, at], preferred_element_type=F32)
-        for q in (1, 2):
-            total += jnp.dot(
-                wt_ref[q], xs_ref[:, pl.ds((f + q) * wide, wide)], preferred_element_type=F32
-            )
+        total = part_ref[:, at]
+        for q in range(3):
+            if not 2 <= f + q < cols + 2:
+                total += jnp.dot(wt_ref[q], column(f + q, slice(None)), preferred_element_type=F32)
         diff = total - tg_ref[:, at].astype(F32)
         cot = weighting * diff
         cot_ref[:, at] = cot.astype(BF16)
@@ -93,16 +145,18 @@
             )
             gi_ref[b, j] = grad.astype(BF16)
 
-    centre = cot_ref[:, wide : (cols + 1) * wide]
     mine = pl.ds(pl.multiple_of(core * 3 * chans, chans), 3 * chans)
+    half = wg_ref.shape[-1]
     for q in range(3):
-        fresh = lax.dot_general(
-            xs_ref[mine, pl.ds((q + 1) * wide, cols * wide)],
-            centre,
-            (((1,), (1,)), ((), ())),
-            preferred_element_type=F32,
-        ).astype(BF16)
-        half = wg_ref.shape[-1]
+        fresh = jnp.zeros((3 * chans, 2 * half), F32)
+        for j in range(cols):
+            fresh += lax.dot_general(
+                column(q + j + 1, mine),
+                cot_ref[:, pl.ds((j + 1) * wide, wide)],
+                (((1,), (1,)), ((), ())),
+                preferred_element_type=F32,
+            )
+        fresh = fresh.astype(BF16)
         for p in range(3):
             for h in range(2):
                 wg_ref[h, p, q] = fresh[p * chans : (p + 1) * chans, h * half : (h + 1) * half]
@@ -143,10 +197,14 @@
     right = exchange(to_left, SPACE, tiles, lambda i: (i - 1) % tiles)
 
     half = channels // 2
-    near_pack, far_pack = gathered(own), gathered(other)
-    w_all = jnp.concatenate([gathered(weights[None]), gathered(w_other[None])], axis=0)
-    wt = jnp.transpose(w_all, (2, 4, 0, 1, 3)).reshape(3, channels, 3 * channels)
-    rim = gathered(jnp.concatenate([left, right], axis=0))
+    tile, early = batch * cols, 2
+    near_pack = gathered(own)
+    w_near = gathered(weights)
+    w_far = w_other.reshape(9, chans, channels)
+    far_pack = gathered(
+        jnp.concatenate([other[: tile + early], w_far[:, :, :half], w_far[:, :, half:]], axis=0)
+    )
+    rim = gathered(jnp.concatenate([left, right, other[tile + early :]], axis=0))
     wown = jnp.transpose(weights, (1, 0, 2, 3)).reshape(3, 3 * chans, channels)
 
     coslat = jnp.cos(jnp.pi * ((jnp.arange(lat, dtype=F32) + 0.5) / lat - 0.5))
@@ -155,23 +213,38 @@
 
     wide = batch * lat
     vmem = pl.BlockSpec(memory_space=pltpu.VMEM)
+    wt, xs, part = pl.pallas_call(
+        functools.partial(early_kernel, early),
+        out_shape=(
+            jax.ShapeDtypeStruct((3, channels, 3 * channels), BF16),
+            jax.ShapeDtypeStruct((3 * channels, cols * wide), BF16),
+            jax.ShapeDtypeStruct((channels, (cols + 2) * wide), F32),
+        ),
+        in_specs=[vmem] * 3,
+        out_specs=(vmem, vmem, vmem),
+        compiler_params=pltpu.CompilerParams(vmem_limit_bytes=16 * 1024 * 1024),
+        cost_estimate=pl.CostEstimate(
+            flops=24 * channels * channels * 3 * wide, bytes_accessed=6 << 20, transcendentals=0
+        ),
+        name="conv_tile",
+    )(near_pack, far_pack, w_near)
     grad_input, wg, loss_part = pl.pallas_call(
-        kernel,
+        functools.partial(late_kernel, early),
         out_shape=(
             jax.ShapeDtypeStruct((batch, cols, chans, lat), BF16),
             jax.ShapeDtypeStruct((2, 3, 3, chans, half), BF16),
             jax.ShapeDtypeStruct((8, 128), F32),
         ),
-        in_specs=[pl.BlockSpec(memory_space=pltpu.SMEM)] + [vmem] * 6,
+        in_specs=[pl.BlockSpec(memory_space=pltpu.SMEM)] + [vmem] * 8,
         out_specs=(vmem, vmem, vmem),
         scratch_shapes=[
-            pltpu.VMEM((3 * channels, (cols + 4) * wide), BF16),
+            pltpu.VMEM((3 * channels, 4 * wide), BF16),
             pltpu.VMEM((channels, (cols + 2) * wide), BF16),
             pltpu.VMEM((channels, (cols + 2) * wide), BF16),
         ],
         compiler_params=pltpu.CompilerParams(vmem_limit_bytes=16 * 1024 * 1024),
-        name="conv_all",
-    )(place, near_pack, far_pack, rim, wt, wown, cos_rows)
+        name="conv_rim",
+    )(place, near_pack, far_pack, rim, wt, xs, part, wown, cos_rows)
 
     rows = 9 * chans * 2 // near
     parts = wg.reshape(near, rows, half)

time: 93.9 us -> 90.9 us (0.968)
  local copies, waits for them, and re-layouts: 3.06 us -> 1.5 us
  other arithmetic: 3.53 us -> 2.49 us
    all_gather x5 -> x4, blocking collectives: 11.2 us -> 9.58 us  [gathered(): return lax.all_gather(a, 'core', axis=0, tiled=True)]
    reshape x1 -> x0, local copies, waits for them, and re-layouts: 1.57 us -> none  [local(): jnp.transpose(w_all, (2, 4, 0, 1, 3)).reshape(3, channels, 3 * channels)]
    all_to_all x2, blocking collectives: 36.2 us -> 37.3 us  [everyone(): return lax.all_to_all(a, axes, 0, 0, tiled=True)]
    concatenate x2, other arithmetic: 1.16 us -> 0.11 us  [the longest x1 0.06 us: local(): rim = gathered(jnp.concatenate([left, right, other[tile + early:]], axis=0))]
    pallas_call x1 -> x2, Pallas kernels: 4.26 us -> 4.54 us  [the longest x1 2.94 us: local(): pl.pallas_call(functools.partial(late_kernel, early), out_shape=(jax.Shap...]
  transfers between devices with their start and end apart: 5 -> 5, of which waited for: 1 -> 1; matrix products, arithmetic and copies ran while one was open for 4% -> 1% of each run, Pallas kernels for 0% -> 2%
where the time goes in v4:
time: 90.9 us; the launch traced here: 90.5 us
  blocking collectives  46.8 us (51%)
  starting transfers between devices  26.8 us (29%)
  waiting for transfers between devices  5.67 us (6%)
  Pallas kernels  4.54 us (5%)
  between operations  2.67 us (3%)
  other arithmetic  2.49 us (3%)
  local copies, waits for them, and re-layouts  1.5 us (2%)
    all_to_all x2, blocking collectives, everyone(): return lax.all_to_all(a, axes, 0, 0, tiled=True)  37.3 us
    ppermute x4, starting transfers between devices, exchange(): return lax.ppermute(a, axes, [(i, to(i)) for i in range(count)])  22.7 us
    all_gather x4, blocking collectives, gathered(): return lax.all_gather(a, 'core', axis=0, tiled=True)  9.58 us
    all_to_all x1, waiting for transfers between devices, everyone(): return lax.all_to_all(a, axes, 0, 0, tiled=True)  5.66 us
    all_to_all x1, starting transfers between devices, everyone(): return lax.all_to_all(a, axes, 0, 0, tiled=True)  4.02 us
    pallas_call x1, Pallas kernels, local(): pl.pallas_call(functools.partial(late_kernel, early), out_shape=(jax.Shap...  2.94 us
  transfers between devices with their start and end apart: 5, of which 1 were waited for; matrix products, arithmetic and copies ran while one was open for 1% of the time, Pallas kernels for 2%

profile of v4, /device:TPU:6, one launch (start us, length us, event | category | flops | bytes accessed | tf_op | source)
XLA Modules:
  0.0 90.5 jit_solution(18425502961642062053)
XLA Ops:
  0.6 0.0 copy-start
  0.6 1.0 %pad_maximum_fusion.4 = bf16[16,64,128]{2,1,0:T(8,128)(2,1)S(1)} fusion(bf16[8,64,128]{2,1,0:T(8,128)(2,1)} %bitcast.49, bf16[8,64,128]{2,1,0:T(8,128)(2,1)} %bitcast.50), kind=kLoop, calls=%fused_computation.6 | loop fusion | flops 131072 | bytes 524288 | tf_op jit(solution)/shard_map/concatenate | solution.py:180
  1.7 3.3 %collective-permute-start = (bf16[16,64,128]{2,1,0:T(8,128)(2,1)S(1)}, bf16[16,64,128]{2,1,0:T(8,128)(2,1)S(1)}, u32[]{:S(2)}, u32[]{:S(2)}) collective-permute-start(bf16[16,64,128]{2,1,0:T(8,128)(2,1)S(1)} %pad_maximum_fusion.4), channel_id=1, source_target_pairs={{0,2},{2,0},{1,3},{3,1},{4,6},{6,4},{5,7},{7,5},{8,10},{10,8},{9,1... | collective-permute-start | bytes 786440 | tf_op jit(solution)/shard_map/ppermute | solution.py:166
  5.0 6.4 %collective-permute-start.1 = (bf16[3,3,64,256]{3,2,1,0:T(8,128)(2,1)}, bf16[3,3,64,256]{3,2,1,0:T(8,128)(2,1)S(1)}, u32[]{:S(2)}, u32[]{:S(2)}) collective-permute-start(bf16[3,3,64,256]{3,2,1,0:T(8,128)(2,1)} %param.4), channel_id=1, source_target_pairs={{0,258},{2,256},{256,2},{258,0},{1,259},{3,257},{257,3},{259,1},{4... | collective-permute-start | bytes 884744 | tf_op jit(solution)/shard_map/ppermute | solution.py:166
  11.4 2.2 %all_gather.12.near_ref = bf16[32,64,128]{2,1,0:T(8,128)(2,1)S(1)} all-gather(bf16[16,64,128]{2,1,0:T(8,128)(2,1)S(1)} %pad_maximum_fusion.4), channel_id=1, replica_groups=mesh['xlo'=2,'y'=4,'zhi'=8,'zlo'=2,'xhi'=2,'core'=2] {'core'}, dimensions={0}, use_global_device_ids=true | all-gather | bytes 786432 | tf_op jit(solution)/shard_map/all_gather | solution.py:178
  13.6 2.4 %all_gather.15.w_ref = bf16[6,3,64,256]{3,2,1,0:T(8,128)(2,1)S(1)} all-gather(bf16[3,3,64,256]{3,2,1,0:T(8,128)(2,1)} %param.4), channel_id=1, replica_groups=mesh['xlo'=2,'y'=4,'zhi'=8,'zlo'=2,'xhi'=2,'core'=2] {'core'}, dimensions={0}, use_global_device_ids=true | all-gather | bytes 884736 | tf_op jit(solution)/shard_map/all_gather | solution.py:178
  16.1 0.1 pad_add_fusion.where_ref
  16.2 0.0 copy-done
  16.2 0.0 collective-permute-done
  16.3 1.9 %collective-permute-start.2 = (bf16[12,64,128]{2,1,0:T(8,128)(2,1)S(1)}, bf16[12,64,128]{2,1,0:T(8,128)(2,1)S(1)}, u32[]{:S(2)}, u32[]{:S(2)}) collective-permute-start(bf16[12,64,128]{2,1,0:T(8,128)(2,1)S(1)} %pad_maximum_fusion.5), channel_id=1, source_target_pairs={{0,4},{4,8},{8,12},{12,16},{16,20},{20,24},{24,28},{28,32},{32,36}... | collective-permute-start | bytes 589832 | tf_op jit(solution)/shard_map/ppermute | solution.py:166
  18.3 11.1 %collective-permute-start.3 = (bf16[12,64,128]{2,1,0:T(8,128)(2,1)S(1)}, bf16[12,64,128]{2,1,0:T(8,128)(2,1)S(1)}, u32[]{:S(2)}, u32[]{:S(2)}) collective-permute-start(bf16[12,64,128]{2,1,0:T(8,128)(2,1)S(1)} %pad_maximum_fusion.6), channel_id=1, source_target_pairs={{0,508},{4,0},{8,4},{12,8},{16,12},{20,16},{24,20},{28,24},{32,28}... | collective-permute-start | bytes 589832 | tf_op jit(solution)/shard_map/ppermute | solution.py:166
  29.4 0.0 collective-permute-done.1
  29.4 0.1 fusion.7
  29.5 0.1 pad_maximum_fusion.2
  29.6 2.5 %all_gather.13.far_ref = bf16[56,64,128]{2,1,0:T(8,128)(2,1)S(1)} all-gather(bf16[28,64,128]{2,1,0:T(8,128)(2,1)S(1)} %pad_maximum_fusion.2), channel_id=1, replica_groups=mesh['xlo'=2,'y'=4,'zhi'=8,'zlo'=2,'xhi'=2,'core'=2] {'core'}, dimensions={0}, use_global_device_ids=true | all-gather | bytes 1376256 | tf_op jit(solution)/shard_map/all_gather | solution.py:178
  32.0 1.6 %conv_tile.1 = (bf16[3,256,768]{2,1,0:T(8,128)(2,1)S(1)}, bf16[768,1024]{1,0:T(8,128)(2,1)S(1)}, f32[256,1536]{1,0:T(8,128)S(1)}) custom-call(bf16[32,64,128]{2,1,0:T(8,128)(2,1)S(1)} %all_gather.12.near_ref, bf16[56,64,128]{2,1,0:T(8,128)(2,1)S(1)} %all_gather.13.far_ref, bf16[6,3,64,256]{3,2,1,0:T(8,128)(2,1)S(1)} %all_gather.15.w_ref), custom_call_target="tpu_custom_call" | custom-call | flops 1207959552 | bytes 6291456 | tf_op jit(solution)/shard_map/conv_tile/pallas_call | solution.py:216
  33.6 0.0 collective-permute-done.2
  33.7 0.0 collective-permute-done.3
  33.7 0.1 pad_maximum_fusion.1
  33.7 2.5 %all_gather.14.rim_ref = bf16[60,64,128]{2,1,0:T(8,128)(2,1)S(1)} all-gather(bf16[30,64,128]{2,1,0:T(8,128)(2,1)S(1)} %pad_maximum_fusion.1), channel_id=1, replica_groups=mesh['xlo'=2,'y'=4,'zhi'=8,'zlo'=2,'xhi'=2,'core'=2] {'core'}, dimensions={0}, use_global_device_ids=true | all-gather | bytes 1474560 | tf_op jit(solution)/shard_map/all_gather | solution.py:178
  36.2 2.9 %conv_rim.1 = (bf16[2,4,64,128]{3,2,1,0:T(8,128)(2,1)}, bf16[2,3,3,64,128]{4,3,2,1,0:T(8,128)(2,1)S(1)}, f32[8,128]{1,0:T(8,128)S(1)}) custom-call(s32[2]{0:T(128)S(1)} %pad_add_fusion.where_ref, bf16[32,64,128]{2,1,0:T(8,128)(2,1)S(1)} %all_gather.12.near_ref, bf16[56,64,128]{2,1,0:T(8,128)(2,1)S(1)} %all_gather.13.far_ref, ...), custom_call_target="tpu_custom_call" | custom-call | tf_op jit(solution)/shard_map/conv_rim/pallas_call | solution.py:231
  39.2 0.1 fusion.4
  39.3 12.3 %all_to_all.15 = bf16[16,80,128]{2,1,0:T(8,128)(2,1)S(1)} all-to-all(bf16[16,80,128]{2,1,0:T(8,128)(2,1)S(1)} %pad_maximum_fusion.3), channel_id=1, replica_groups=mesh['xlo'=2,'y'=4,'zhi'=8,'zlo'=2,'xhi'=2,'core'=2] {'xlo','y','zlo'}, dimensions={0} | all-to-all | bytes 655360 | tf_op jit(solution)/shard_map/all_to_all | solution.py:261
  51.6 0.1 convert_reduce_fusion
  51.7 0.1 fusion.5
  51.8 24.9 %all_to_all.16 = bf16[8,80,128]{2,1,0:T(8,128)(2,1)S(1)} all-to-all(bf16[8,80,128]{2,1,0:T(8,128)(2,1)S(1)} %pad_maximum_fusion.7), channel_id=1, replica_groups=mesh['xlo'=2,'y'=4,'zhi'=8,'zlo'=2,'xhi'=2,'core'=2] {'zhi'}, dimensions={0} | all-to-all | bytes 327680 | tf_op jit(solution)/shard_map/all_to_all | solution.py:261
  76.8 0.8 broadcast_in_dim.30
  77.6 4.0 %all-to-all-start.2 = ((bf16[16,72,128]{2,1,0:T(8,128)(2,1)}), bf16[16,72,128]{2,1,0:T(8,128)(2,1)S(1)}, u32[]{:S(2)}, u32[]{:S(2)}) async-start(bf16[16,72,128]{2,1,0:T(8,128)(2,1)} %broadcast_in_dim.30), calls=%async_computation.2 | async-start | bytes 589824 | tf_op jit(solution)/shard_map/all_to_all | solution.py:261
  81.6 0.5 slice.83
  82.8 5.7 %all-to-all-done.2 = bf16[16,72,128]{2,1,0:T(8,128)(2,1)S(1)} async-done(((bf16[16,72,128]{2,1,0:T(8,128)(2,1)}), bf16[16,72,128]{2,1,0:T(8,128)(2,1)S(1)}, u32[]{:S(2)}, u32[]{:S(2)}) %all-to-all-start.2) | async-done | bytes 294944 | tf_op jit(solution)/shard_map/all_to_all | solution.py:261
  88.5 0.9 pad_maximum_fusion
  (24 shorter events, 0.4 us)
Async XLA Ops:
  0.6 15.5 %copy-start = (bf16[3,3,64,256]{3,2,1,0:T(8,128)(2,1)S(1)}, bf16[3,3,64,256]{3,2,1,0:T(8,128)(2,1)}, u32[]{:S(2)}) copy-start(bf16[3,3,64,256]{3,2,1,0:T(8,128)(2,1)} %param.4) | copy-start | bytes 884740
  1.7 14.5 %collective-permute-start = (bf16[16,64,128]{2,1,0:T(8,128)(2,1)S(1)}, bf16[16,64,128]{2,1,0:T(8,128)(2,1)S(1)}, u32[]{:S(2)}, u32[]{:S(2)}) collective-permute-start(bf16[16,64,128]{2,1,0:T(8,128)(2,1)S(1)} %pad_maximum_fusion.4), channel_id=1, source_target_pairs={{0,2},{2,0},{1,3},{3,1},{4,6},{6,4},{5,7},{7,5},{8,10},{10,8},{9,1... | collective-permute-start | bytes 786440 | tf_op jit(solution)/shard_map/ppermute | solution.py:166
  5.0 24.4 %collective-permute-start.1 = (bf16[3,3,64,256]{3,2,1,0:T(8,128)(2,1)}, bf16[3,3,64,256]{3,2,1,0:T(8,128)(2,1)S(1)}, u32[]{:S(2)}, u32[]{:S(2)}) collective-permute-start(bf16[3,3,64,256]{3,2,1,0:T(8,128)(2,1)} %param.4), channel_id=1, source_target_pairs={{0,258},{2,256},{256,2},{258,0},{1,259},{3,257},{257,3},{259,1},{4... | collective-permute-start | bytes 884744 | tf_op jit(solution)/shard_map/ppermute | solution.py:166
  16.3 17.4 %collective-permute-start.2 = (bf16[12,64,128]{2,1,0:T(8,128)(2,1)S(1)}, bf16[12,64,128]{2,1,0:T(8,128)(2,1)S(1)}, u32[]{:S(2)}, u32[]{:S(2)}) collective-permute-start(bf16[12,64,128]{2,1,0:T(8,128)(2,1)S(1)} %pad_maximum_fusion.5), channel_id=1, source_target_pairs={{0,4},{4,8},{8,12},{12,16},{16,20},{20,24},{24,28},{28,32},{32,36}... | collective-permute-start | bytes 589832 | tf_op jit(solution)/shard_map/ppermute | solution.py:166
  18.3 15.4 %collective-permute-start.3 = (bf16[12,64,128]{2,1,0:T(8,128)(2,1)S(1)}, bf16[12,64,128]{2,1,0:T(8,128)(2,1)S(1)}, u32[]{:S(2)}, u32[]{:S(2)}) collective-permute-start(bf16[12,64,128]{2,1,0:T(8,128)(2,1)S(1)} %pad_maximum_fusion.6), channel_id=1, source_target_pairs={{0,508},{4,0},{8,4},{12,8},{16,12},{20,16},{24,20},{28,24},{32,28}... | collective-permute-start | bytes 589832 | tf_op jit(solution)/shard_map/ppermute | solution.py:166
  77.6 10.9 %all-to-all-start.2 = ((bf16[16,72,128]{2,1,0:T(8,128)(2,1)}), bf16[16,72,128]{2,1,0:T(8,128)(2,1)S(1)}, u32[]{:S(2)}, u32[]{:S(2)}) async-start(bf16[16,72,128]{2,1,0:T(8,128)(2,1)} %broadcast_in_dim.30), calls=%async_computation.2 | async-start | bytes 589824 | tf_op jit(solution)/shard_map/all_to_all | solution.py:261

commit v5 on v4

--- a/solution.py
+++ b/solution.py
@@ -31,24 +31,30 @@
     xs_ref[row + 2 * chans : row + 3 * chans, at] = shift_lanes(wide, 1).astype(BF16)
 
 
-def early_kernel(early, near_ref, far_ref, w_ref, wt_ref, xs_ref, part_ref):
+def pack_kernel(keep, pack_ref, w_ref, out_ref, rest_ref):
+    half = out_ref.shape[2]
+    out_ref[:keep] = pack_ref[:keep]
+    rest_ref[...] = pack_ref[keep:]
+    for p in range(3):
+        for q in range(3):
+            for h in range(2):
+                out_ref[keep + h * 9 + p * 3 + q] = w_ref[p, q, :, h * half : (h + 1) * half]
+
+
+def early_kernel(early, near_ref, far_ref, wt_ref, xs_ref, part_ref):
     chans, lat = near_ref.shape[1:]
-    half = far_ref.shape[2]
     wide = part_ref.shape[1] // 6
     batch, cols = wide // lat, xs_ref.shape[1] // wide
-    pack = (near_ref.shape[0] // 2, far_ref.shape[0] // 2)
+    pack = near_ref.shape[0] // 2
     weights_at = batch * cols + early
 
     for q in range(3):
         blocks = []
         for block in range(4):
-            unit = block % 2
+            unit, ref = block % 2, near_ref if block < 2 else far_ref
             for p in range(3):
-                if block < 2:
-                    blocks.append(w_ref[unit * 3 + p, q])
-                else:
-                    first = unit * pack[1] + weights_at + p * 3 + q
-                    blocks.append(jnp.concatenate([far_ref[first], far_ref[first + 9]], axis=1))
+                first = unit * pack + weights_at + p * 3 + q
+                blocks.append(jnp.concatenate([ref[first], ref[first + 9]], axis=1))
         for t in range(0, 12, 2):
             pair = jnp.concatenate(blocks[t : t + 2], axis=0)
             wt_ref[q, :, t * chans : (t + 2) * chans] = pair.T
@@ -57,7 +63,7 @@
         unit, ref = block % 2, near_ref if block < 2 else far_ref
         for b in range(batch):
             for j in range(cols):
-                x = ref[unit * pack[block // 2] + b * cols + j]
+                x = ref[unit * pack + b * cols + j]
                 place_block(xs_ref, block * 3 * chans, pl.ds(j * wide + b * lat, lat), x)
 
     for f in range(cols + 2):
@@ -81,7 +87,8 @@
     wide = batch * lat
     tile = batch * cols
     rim = 3 * batch
-    pack = (near_ref.shape[0] // 2, far_ref.shape[0] // 2, rim_ref.shape[0] // 2)
+    pack, rims = near_ref.shape[0] // 2, rim_ref.shape[0] // 2
+    later = tile - early
 
     def outer(e):
         return e if e < 2 else e - cols
@@ -90,7 +97,8 @@
         for unit in range(2):
             row = (chip * 2 + unit) * 3 * chans
             trow = pl.multiple_of(((chip ^ xhi) * 2 + unit) * chans, chans)
-            left = unit * pack[2] + chip * rim
+            left = unit * rims + chip * rim
+            main = near_ref if chip == 0 else far_ref
             right = left + 2 * rim
             for b in range(batch):
                 for e in (0, 1, cols + 2, cols + 3):
@@ -102,12 +110,10 @@
                         t = rim_ref[left + 2 * batch + b]
                     elif f > cols:
                         t = rim_ref[right + 2 * batch + b]
-                    elif chip == 0:
-                        t = near_ref[unit * pack[0] + tile + own]
                     elif own < early:
-                        t = far_ref[unit * pack[1] + tile + own]
+                        t = main[unit * pack + tile + own]
                     else:
-                        t = rim_ref[unit * pack[2] + 4 * rim + own - early]
+                        t = rim_ref[unit * rims + 4 * rim + chip * later + own - early]
                     tg_ref[pl.ds(trow, chans), pl.ds(f * wide + b * lat, lat)] = t
 
     def column(e, rows):
@@ -162,6 +168,13 @@
                 wg_ref[h, p, q] = fresh[p * chans : (p + 1) * chans, h * half : (h + 1) * half]
 
 
+def last_kernel(scale, halves_ref, value_ref, wg_ref, loss_ref):
+    half = halves_ref.shape[-1]
+    for h in range(2):
+        wg_ref[:, :, :, h * half : (h + 1) * half] = halves_ref[h].astype(F32)
+    loss_ref[0, 0] = jnp.max(value_ref[...]) * scale
+
+
 def exchange(a, axes, count, to):
     return lax.ppermute(a, axes, [(i, to(i)) for i in range(count)])
 
@@ -197,14 +210,29 @@
     right = exchange(to_left, SPACE, tiles, lambda i: (i - 1) % tiles)
 
     half = channels // 2
-    tile, early = batch * cols, 2
-    near_pack = gathered(own)
-    w_near = gathered(weights)
-    w_far = w_other.reshape(9, chans, channels)
-    far_pack = gathered(
-        jnp.concatenate([other[: tile + early], w_far[:, :, :half], w_far[:, :, half:]], axis=0)
-    )
-    rim = gathered(jnp.concatenate([left, right, other[tile + early :]], axis=0))
+    tile, early = batch * cols, 5
+
+    keep = tile + early
+    vmem = pl.BlockSpec(memory_space=pltpu.VMEM)
+
+    def with_weights(pack, w):
+        return pl.pallas_call(
+            functools.partial(pack_kernel, keep),
+            out_shape=(
+                jax.ShapeDtypeStruct((keep + 18, chans, half), BF16),
+                jax.ShapeDtypeStruct((2 * tile - keep, chans, half), BF16),
+            ),
+            in_specs=[vmem] * 2,
+            out_specs=(vmem, vmem),
+            compiler_params=pltpu.CompilerParams(vmem_limit_bytes=8 * 1024 * 1024),
+            cost_estimate=pl.CostEstimate(flops=0, bytes_accessed=1 << 20, transcendentals=0),
+            name="pack",
+        )(pack, w)
+
+    near_part, near_rest = with_weights(own, weights)
+    far_part, far_rest = with_weights(other, w_other)
+    near_pack, far_pack = gathered(near_part), gathered(far_part)
+    rim = gathered(jnp.concatenate([left, right, near_rest, far_rest], axis=0))
     wown = jnp.transpose(weights, (1, 0, 2, 3)).reshape(3, 3 * chans, channels)
 
     coslat = jnp.cos(jnp.pi * ((jnp.arange(lat, dtype=F32) + 0.5) / lat - 0.5))
@@ -212,7 +240,6 @@
     place = jnp.stack([xhi, core]).astype(jnp.int32)
 
     wide = batch * lat
-    vmem = pl.BlockSpec(memory_space=pltpu.VMEM)
     wt, xs, part = pl.pallas_call(
         functools.partial(early_kernel, early),
         out_shape=(
@@ -220,14 +247,14 @@
             jax.ShapeDtypeStruct((3 * channels, cols * wide), BF16),
             jax.ShapeDtypeStruct((channels, (cols + 2) * wide), F32),
         ),
-        in_specs=[vmem] * 3,
+        in_specs=[vmem] * 2,
         out_specs=(vmem, vmem, vmem),
         compiler_params=pltpu.CompilerParams(vmem_limit_bytes=16 * 1024 * 1024),
         cost_estimate=pl.CostEstimate(
             flops=24 * channels * channels * 3 * wide, bytes_accessed=6 << 20, transcendentals=0
         ),
         name="conv_tile",
-    )(near_pack, far_pack, w_near)
+    )(near_pack, far_pack)
     grad_input, wg, loss_part = pl.pallas_call(
         functools.partial(late_kernel, early),
         out_shape=(
@@ -270,12 +297,20 @@
     total, value = summed(
         everyone(with_loss(spread, jnp.concatenate([value, value], axis=0)), "zhi")
     )
-    loss = 0.5 * value[0, 0] / (batch * lat * lon * channels)
     mine = (total * (scale_factor / (batch * lat * lon))).astype(BF16)
     third = everyone(jnp.broadcast_to(mine[None], (near, rows, half)), NEAR)
-    halves = third.reshape(2, 3, 3, chans, half).astype(F32)
-    weight_grad = jnp.concatenate([halves[0], halves[1]], axis=-1)
-    return (loss, grad_input, weight_grad)
+    weight_grad, loss = pl.pallas_call(
+        functools.partial(last_kernel, 0.5 / (batch * lat * lon * channels)),
+        out_shape=(
+            jax.ShapeDtypeStruct(weights.shape, F32),
+            jax.ShapeDtypeStruct((1, 1), F32),
+        ),
+        in_specs=[vmem] * 2,
+        out_specs=(vmem, pl.BlockSpec(memory_space=pltpu.SMEM)),
+        compiler_params=pltpu.CompilerParams(vmem_limit_bytes=8 * 1024 * 1024),
+        name="widen",
+    )(third.reshape(2, 3, 3, chans, half), value)
+    return (loss[0, 0], grad_input, weight_grad)
 
 
 def solution(mesh):

time: 90.9 us -> 88.7 us (0.976)
  blocking collectives: 46.8 us -> 43.8 us
  between operations: 2.67 us -> 0.86 us
  waiting for transfers between devices: 5.67 us -> 6.83 us
  starting transfers between devices: 26.8 us -> 27.8 us
  Pallas kernels: 4.54 us -> 5.53 us
    all_gather x4 -> x3, blocking collectives: 9.58 us -> 7.58 us  [gathered(): return lax.all_gather(a, 'core', axis=0, tiled=True)]
    all_to_all x1, waiting for transfers between devices: 5.66 us -> 6.82 us  [everyone(): return lax.all_to_all(a, axes, 0, 0, tiled=True)]
    ppermute x4, starting transfers between devices: 22.7 us -> 23.8 us  [exchange(): return lax.ppermute(a, axes, [(i, to(i)) for i in range(count)])]
    all_to_all x2, blocking collectives: 37.3 us -> 36.3 us  [everyone(): return lax.all_to_all(a, axes, 0, 0, tiled=True)]
    pallas_call x0 -> x3, Pallas kernels: none -> 1 us  [the longest x1 0.86 us: local(): pl.pallas_call(functools.partial(last_kernel, 0.5 / (batch * lat * lon *...]
    unnamed x2 -> x4, local copies, waits for them, and re-layouts: 0.01 us -> 0.97 us
  transfers between devices with their start and end apart: 5 -> 5, of which waited for: 1 -> 1; matrix products, arithmetic and copies ran while one was open for 1% -> 0% of each run, Pallas kernels for 2% -> 2%
where the time goes in v5:
time: 88.7 us; the launch traced here: 88.3 us
  blocking collectives  43.8 us (49%)
  starting transfers between devices  27.8 us (31%)
  waiting for transfers between devices  6.83 us (8%)
  Pallas kernels  5.53 us (6%)
  local copies, waits for them, and re-layouts  1.82 us (2%)
  other arithmetic  1.59 us (2%)
    all_to_all x2, blocking collectives, everyone(): return lax.all_to_all(a, axes, 0, 0, tiled=True)  36.3 us
    ppermute x4, starting transfers between devices, exchange(): return lax.ppermute(a, axes, [(i, to(i)) for i in range(count)])  23.8 us
    all_gather x3, blocking collectives, gathered(): return lax.all_gather(a, 'core', axis=0, tiled=True)  7.58 us
    all_to_all x1, waiting for transfers between devices, everyone(): return lax.all_to_all(a, axes, 0, 0, tiled=True)  6.82 us
    all_to_all x1, starting transfers between devices, everyone(): return lax.all_to_all(a, axes, 0, 0, tiled=True)  4.02 us
    pallas_call x1, Pallas kernels, local(): pl.pallas_call(functools.partial(late_kernel, early), out_shape=(jax.Shap...  2.94 us
  transfers between devices with their start and end apart: 5, of which 1 were waited for; matrix products, arithmetic and copies ran while one was open for 0% of the time, Pallas kernels for 2%

profile of v5, /device:TPU:6, one launch (start us, length us, event | category | flops | bytes accessed | tf_op | source)
XLA Modules:
  0.0 88.3 jit_solution(60051502593256683)
XLA Ops:
  0.6 0.0 copy-start.1
  0.6 1.0 %pad_maximum_fusion.2.pack_ref = bf16[16,64,128]{2,1,0:T(8,128)(2,1)S(1)} fusion(bf16[8,64,128]{2,1,0:T(8,128)(2,1)} %bitcast.41, bf16[8,64,128]{2,1,0:T(8,128)(2,1)} %bitcast.42), kind=kLoop, calls=%fused_computation.4 | loop fusion | flops 131072 | bytes 524288 | tf_op jit(solution)/shard_map/concatenate | solution.py:193
  1.7 3.3 %collective-permute-start = (bf16[16,64,128]{2,1,0:T(8,128)(2,1)S(1)}, bf16[16,64,128]{2,1,0:T(8,128)(2,1)S(1)}, u32[]{:S(2)}, u32[]{:S(2)}) collective-permute-start(bf16[16,64,128]{2,1,0:T(8,128)(2,1)S(1)} %pad_maximum_fusion.2.pack_ref), channel_id=1, source_target_pairs={{0,2},{2,0},{1,3},{3,1},{4,6},{6,4},{5,7},{7,5},{8,10},{10,8},{9,1... | collective-permute-start | bytes 786440 | tf_op jit(solution)/shard_map/ppermute | solution.py:179
  5.0 6.4 %collective-permute-start.1 = (bf16[3,3,64,256]{3,2,1,0:T(8,128)(2,1)}, bf16[3,3,64,256]{3,2,1,0:T(8,128)(2,1)S(1)}, u32[]{:S(2)}, u32[]{:S(2)}) collective-permute-start(bf16[3,3,64,256]{3,2,1,0:T(8,128)(2,1)} %w_ref.1), channel_id=1, source_target_pairs={{0,258},{2,256},{256,2},{258,0},{1,259},{3,257},{257,3},{259,1},{4... | collective-permute-start | bytes 884744 | tf_op jit(solution)/shard_map/ppermute | solution.py:179
  11.5 0.1 pad_add_fusion.where_ref
  11.6 0.0 copy-start
  11.6 1.0 %copy-done = bf16[3,3,64,256]{3,2,1,0:T(8,128)(2,1)S(1)} copy-done((bf16[3,3,64,256]{3,2,1,0:T(8,128)(2,1)S(1)}, bf16[3,3,64,256]{3,2,1,0:T(8,128)(2,1)}, u32[]{:S(2)}) %copy-start) | copy-done | bytes 294936
  12.5 0.1 pack.2
  12.6 0.0 copy-done.1
  12.6 2.5 %all_gather.9.near_ref = bf16[62,64,128]{2,1,0:T(8,128)(2,1)S(1)} all-gather(bf16[31,64,128]{2,1,0:T(8,128)(2,1)S(1)} %get-tuple-element.15), channel_id=1, replica_groups=mesh['xlo'=2,'y'=4,'zhi'=8,'zlo'=2,'xhi'=2,'core'=2] {'core'}, dimensions={0}, use_global_device_ids=true | all-gather | bytes 1523712 | tf_op jit(solution)/shard_map/all_gather | solution.py:191
  15.2 0.0 collective-permute-done.pack_ref
  15.2 1.9 %collective-permute-start.2 = (bf16[12,64,128]{2,1,0:T(8,128)(2,1)S(1)}, bf16[12,64,128]{2,1,0:T(8,128)(2,1)S(1)}, u32[]{:S(2)}, u32[]{:S(2)}) collective-permute-start(bf16[12,64,128]{2,1,0:T(8,128)(2,1)S(1)} %pad_maximum_fusion.3), channel_id=1, source_target_pairs={{0,4},{4,8},{8,12},{12,16},{16,20},{20,24},{24,28},{28,32},{32,36}... | collective-permute-start | bytes 589832 | tf_op jit(solution)/shard_map/ppermute | solution.py:179
  17.2 12.2 %collective-permute-start.3 = (bf16[12,64,128]{2,1,0:T(8,128)(2,1)S(1)}, bf16[12,64,128]{2,1,0:T(8,128)(2,1)S(1)}, u32[]{:S(2)}, u32[]{:S(2)}) collective-permute-start(bf16[12,64,128]{2,1,0:T(8,128)(2,1)S(1)} %pad_maximum_fusion.4), channel_id=1, source_target_pairs={{0,508},{4,0},{8,4},{12,8},{16,12},{20,16},{24,20},{28,24},{32,28}... | collective-permute-start | bytes 589832 | tf_op jit(solution)/shard_map/ppermute | solution.py:179
  29.4 0.0 collective-permute-done.1.w_ref
  29.4 0.1 pack.3
  29.5 2.5 %all_gather.10.far_ref = bf16[62,64,128]{2,1,0:T(8,128)(2,1)S(1)} all-gather(bf16[31,64,128]{2,1,0:T(8,128)(2,1)S(1)} %get-tuple-element.16), channel_id=1, replica_groups=mesh['xlo'=2,'y'=4,'zhi'=8,'zlo'=2,'xhi'=2,'core'=2] {'core'}, dimensions={0}, use_global_device_ids=true | all-gather | bytes 1523712 | tf_op jit(solution)/shard_map/all_gather | solution.py:191
  32.0 1.6 %conv_tile.1 = (bf16[3,256,768]{2,1,0:T(8,128)(2,1)S(1)}, bf16[768,1024]{1,0:T(8,128)(2,1)S(1)}, f32[256,1536]{1,0:T(8,128)S(1)}) custom-call(bf16[62,64,128]{2,1,0:T(8,128)(2,1)S(1)} %all_gather.9.near_ref, bf16[62,64,128]{2,1,0:T(8,128)(2,1)S(1)} %all_gather.10.far_ref), custom_call_target="tpu_custom_call" | custom-call | flops 1207959552 | bytes 6291456 | tf_op jit(solution)/shard_map/conv_tile/pallas_call | solution.py:243
  33.6 0.0 collective-permute-done.2
  33.6 0.0 collective-permute-done.3
  33.6 0.1 pad_maximum_fusion
  33.7 2.5 %all_gather.11.rim_ref = bf16[60,64,128]{2,1,0:T(8,128)(2,1)S(1)} all-gather(bf16[30,64,128]{2,1,0:T(8,128)(2,1)S(1)} %pad_maximum_fusion), channel_id=1, replica_groups=mesh['xlo'=2,'y'=4,'zhi'=8,'zlo'=2,'xhi'=2,'core'=2] {'core'}, dimensions={0}, use_global_device_ids=true | all-gather | bytes 1474560 | tf_op jit(solution)/shard_map/all_gather | solution.py:191
  36.2 2.9 %conv_rim.1 = (bf16[2,4,64,128]{3,2,1,0:T(8,128)(2,1)}, bf16[2,3,3,64,128]{4,3,2,1,0:T(8,128)(2,1)S(1)}, f32[8,128]{1,0:T(8,128)S(1)}) custom-call(s32[2]{0:T(128)S(1)} %pad_add_fusion.where_ref, bf16[62,64,128]{2,1,0:T(8,128)(2,1)S(1)} %all_gather.9.near_ref, bf16[62,64,128]{2,1,0:T(8,128)(2,1)S(1)} %all_gather.10.far_ref, ...), custom_call_target="tpu_custom_call" | custom-call | tf_op jit(solution)/shard_map/conv_rim/pallas_call | solution.py:258
  39.2 0.1 fusion.4
  39.3 11.6 %all_to_all.15 = bf16[16,80,128]{2,1,0:T(8,128)(2,1)S(1)} all-to-all(bf16[16,80,128]{2,1,0:T(8,128)(2,1)S(1)} %pad_maximum_fusion.1), channel_id=1, replica_groups=mesh['xlo'=2,'y'=4,'zhi'=8,'zlo'=2,'xhi'=2,'core'=2] {'xlo','y','zlo'}, dimensions={0} | all-to-all | bytes 655360 | tf_op jit(solution)/shard_map/all_to_all | solution.py:288
  50.8 0.1 convert_reduce_fusion
  50.9 0.1 fusion.5
  51.0 24.7 %all_to_all.16 = bf16[8,80,128]{2,1,0:T(8,128)(2,1)S(1)} all-to-all(bf16[8,80,128]{2,1,0:T(8,128)(2,1)S(1)} %pad_maximum_fusion.5), channel_id=1, replica_groups=mesh['xlo'=2,'y'=4,'zhi'=8,'zlo'=2,'xhi'=2,'core'=2] {'zhi'}, dimensions={0} | all-to-all | bytes 327680 | tf_op jit(solution)/shard_map/all_to_all | solution.py:288
  75.8 0.8 broadcast_in_dim.30
  76.5 4.0 %all-to-all-start.2 = ((bf16[16,72,128]{2,1,0:T(8,128)(2,1)}), bf16[16,72,128]{2,1,0:T(8,128)(2,1)S(1)}, u32[]{:S(2)}, u32[]{:S(2)}) async-start(bf16[16,72,128]{2,1,0:T(8,128)(2,1)} %broadcast_in_dim.30), calls=%async_computation.2 | async-start | bytes 589824 | tf_op jit(solution)/shard_map/all_to_all | solution.py:288
  80.6 6.8 %all-to-all-done.2 = bf16[16,72,128]{2,1,0:T(8,128)(2,1)S(1)} async-done(((bf16[16,72,128]{2,1,0:T(8,128)(2,1)}), bf16[16,72,128]{2,1,0:T(8,128)(2,1)S(1)}, u32[]{:S(2)}, u32[]{:S(2)}) %all-to-all-start.2) | async-done | bytes 294944 | tf_op jit(solution)/shard_map/all_to_all | solution.py:288
  87.4 0.9 widen.1
  (21 shorter events, 0.3 us)
Async XLA Ops:
  0.6 12.0 %copy-start.1 = (bf16[3,3,64,256]{3,2,1,0:T(8,128)(2,1)S(1)}, bf16[3,3,64,256]{3,2,1,0:T(8,128)(2,1)}, u32[]{:S(2)}) copy-start(bf16[3,3,64,256]{3,2,1,0:T(8,128)(2,1)} %w_ref.1) | copy-start | bytes 884740
  1.7 13.5 %collective-permute-start = (bf16[16,64,128]{2,1,0:T(8,128)(2,1)S(1)}, bf16[16,64,128]{2,1,0:T(8,128)(2,1)S(1)}, u32[]{:S(2)}, u32[]{:S(2)}) collective-permute-start(bf16[16,64,128]{2,1,0:T(8,128)(2,1)S(1)} %pad_maximum_fusion.2.pack_ref), channel_id=1, source_target_pairs={{0,2},{2,0},{1,3},{3,1},{4,6},{6,4},{5,7},{7,5},{8,10},{10,8},{9,1... | collective-permute-start | bytes 786440 | tf_op jit(solution)/shard_map/ppermute | solution.py:179
  5.0 24.4 %collective-permute-start.1 = (bf16[3,3,64,256]{3,2,1,0:T(8,128)(2,1)}, bf16[3,3,64,256]{3,2,1,0:T(8,128)(2,1)S(1)}, u32[]{:S(2)}, u32[]{:S(2)}) collective-permute-start(bf16[3,3,64,256]{3,2,1,0:T(8,128)(2,1)} %w_ref.1), channel_id=1, source_target_pairs={{0,258},{2,256},{256,2},{258,0},{1,259},{3,257},{257,3},{259,1},{4... | collective-permute-start | bytes 884744 | tf_op jit(solution)/shard_map/ppermute | solution.py:179
  11.6 1.0 %copy-start = (bf16[3,3,64,256]{3,2,1,0:T(8,128)(2,1)S(1)}, bf16[3,3,64,256]{3,2,1,0:T(8,128)(2,1)}, u32[]{:S(2)}) copy-start(bf16[3,3,64,256]{3,2,1,0:T(8,128)(2,1)} %w_ref.1) | copy-start | bytes 884740
  15.2 18.4 %collective-permute-start.2 = (bf16[12,64,128]{2,1,0:T(8,128)(2,1)S(1)}, bf16[12,64,128]{2,1,0:T(8,128)(2,1)S(1)}, u32[]{:S(2)}, u32[]{:S(2)}) collective-permute-start(bf16[12,64,128]{2,1,0:T(8,128)(2,1)S(1)} %pad_maximum_fusion.3), channel_id=1, source_target_pairs={{0,4},{4,8},{8,12},{12,16},{16,20},{20,24},{24,28},{28,32},{32,36}... | collective-permute-start | bytes 589832 | tf_op jit(solution)/shard_map/ppermute | solution.py:179
  17.2 16.4 %collective-permute-start.3 = (bf16[12,64,128]{2,1,0:T(8,128)(2,1)S(1)}, bf16[12,64,128]{2,1,0:T(8,128)(2,1)S(1)}, u32[]{:S(2)}, u32[]{:S(2)}) collective-permute-start(bf16[12,64,128]{2,1,0:T(8,128)(2,1)S(1)} %pad_maximum_fusion.4), channel_id=1, source_target_pairs={{0,508},{4,0},{8,4},{12,8},{16,12},{20,16},{24,20},{28,24},{32,28}... | collective-permute-start | bytes 589832 | tf_op jit(solution)/shard_map/ppermute | solution.py:179
  76.5 10.9 %all-to-all-start.2 = ((bf16[16,72,128]{2,1,0:T(8,128)(2,1)}), bf16[16,72,128]{2,1,0:T(8,128)(2,1)S(1)}, u32[]{:S(2)}, u32[]{:S(2)}) async-start(bf16[16,72,128]{2,1,0:T(8,128)(2,1)} %broadcast_in_dim.30), calls=%async_computation.2 | async-start | bytes 589824 | tf_op jit(solution)/shard_map/all_to_all | solution.py:288

commit v6 on v5

--- a/solution.py
+++ b/solution.py
@@ -80,7 +80,7 @@
 
 def late_kernel(
     early, where_ref, near_ref, far_ref, rim_ref, wt_ref, xs_ref, part_ref, wown_ref, cos_ref,
-    gi_ref, wg_ref, loss_ref, xh_ref, tg_ref, cot_ref,
+    gi_ref, wg_ref, loss_ref, xh_ref, tg_ref, cot_ref, grad_ref, sem,
 ):
     xhi, core = where_ref[0], where_ref[1]
     batch, cols, chans, lat = gi_ref.shape
@@ -149,7 +149,9 @@
                 + part[chans : 2 * chans]
                 + shift_lanes(part[2 * chans :], -1)
             )
-            gi_ref[b, j] = grad.astype(BF16)
+            grad_ref[b, j] = grad.astype(BF16)
+    leaving = pltpu.make_async_copy(grad_ref, gi_ref, sem)
+    leaving.start()
 
     mine = pl.ds(pl.multiple_of(core * 3 * chans, chans), 3 * chans)
     half = wg_ref.shape[-1]
@@ -166,6 +168,7 @@
         for p in range(3):
             for h in range(2):
                 wg_ref[h, p, q] = fresh[p * chans : (p + 1) * chans, h * half : (h + 1) * half]
+    leaving.wait()
 
 
 def last_kernel(scale, halves_ref, value_ref, wg_ref, loss_ref):
@@ -263,11 +266,13 @@
             jax.ShapeDtypeStruct((8, 128), F32),
         ),
         in_specs=[pl.BlockSpec(memory_space=pltpu.SMEM)] + [vmem] * 8,
-        out_specs=(vmem, vmem, vmem),
+        out_specs=(pl.BlockSpec(memory_space=pl.ANY), vmem, vmem),
         scratch_shapes=[
             pltpu.VMEM((3 * channels, 4 * wide), BF16),
             pltpu.VMEM((channels, (cols + 2) * wide), BF16),
             pltpu.VMEM((channels, (cols + 2) * wide), BF16),
+            pltpu.VMEM((batch, cols, chans, lat), BF16),
+            pltpu.SemaphoreType.DMA,
         ],
         compiler_params=pltpu.CompilerParams(vmem_limit_bytes=16 * 1024 * 1024),
         name="conv_rim",
@@ -297,6 +302,7 @@
     total, value = summed(
         everyone(with_loss(spread, jnp.concatenate([value, value], axis=0)), "zhi")
     )
+    total, value = lax.optimization_barrier((total, value))
     mine = (total * (scale_factor / (batch * lat * lon))).astype(BF16)
     third = everyone(jnp.broadcast_to(mine[None], (near, rows, half)), NEAR)
     weight_grad, loss = pl.pallas_call(

time: 88.7 us -> 87.6 us (0.988)
  blocking collectives: 43.8 us -> 54.3 us
  waiting for transfers between devices: 6.83 us -> 0.01 us
  starting transfers between devices: 27.8 us -> 23.8 us
    all_to_all x2 -> x3, blocking collectives: 36.3 us -> 46.7 us  [everyone(): return lax.all_to_all(a, axes, 0, 0, tiled=True)]
    all_to_all x1 -> x0, waiting for transfers between devices: 6.82 us -> none  [everyone(): return lax.all_to_all(a, axes, 0, 0, tiled=True)]
    all_to_all x1 -> x0, starting transfers between devices: 4.02 us -> none  [everyone(): return lax.all_to_all(a, axes, 0, 0, tiled=True)]
  transfers between devices with their start and end apart: 5 -> 4, of which waited for: 1 -> 0; matrix products, arithmetic and copies ran while one was open for 0% -> 0% of each run, Pallas kernels for 2% -> 2%
where the time goes in v6:
time: 87.6 us; the launch traced here: 87.2 us
  blocking collectives  54.3 us (62%)
  starting transfers between devices  23.8 us (27%)
  Pallas kernels  5.54 us (6%)
  other arithmetic  1.59 us (2%)
  local copies, waits for them, and re-layouts  1.11 us (1%)
  between operations  0.89 us (1%)
    all_to_all x3, blocking collectives, everyone(): return lax.all_to_all(a, axes, 0, 0, tiled=True)  46.7 us
    ppermute x4, starting transfers between devices, exchange(): return lax.ppermute(a, axes, [(i, to(i)) for i in range(count)])  23.8 us
    all_gather x3, blocking collectives, gathered(): return lax.all_gather(a, 'core', axis=0, tiled=True)  7.58 us
    pallas_call x1, Pallas kernels, local(): pl.pallas_call(functools.partial(late_kernel, early), out_shape=(jax.Shap...  2.94 us
  transfers between devices with their start and end apart: 4, of which 0 were waited for; matrix products, arithmetic and copies ran while one was open for 0% of the time, Pallas kernels for 2%

profile of v6, /device:TPU:6, one launch (start us, length us, event | category | flops | bytes accessed | tf_op | source)
XLA Modules:
  0.0 87.2 jit_solution(2666951073373195704)
XLA Ops:
  0.6 0.0 copy-start.1
  0.6 1.0 %pad_maximum_fusion.2.pack_ref = bf16[16,64,128]{2,1,0:T(8,128)(2,1)S(1)} fusion(bf16[8,64,128]{2,1,0:T(8,128)(2,1)} %bitcast.41, bf16[8,64,128]{2,1,0:T(8,128)(2,1)} %bitcast.42), kind=kLoop, calls=%fused_computation.4 | loop fusion | flops 131072 | bytes 524288 | tf_op jit(solution)/shard_map/concatenate | solution.py:196
  1.7 3.3 %collective-permute-start = (bf16[16,64,128]{2,1,0:T(8,128)(2,1)S(1)}, bf16[16,64,128]{2,1,0:T(8,128)(2,1)S(1)}, u32[]{:S(2)}, u32[]{:S(2)}) collective-permute-start(bf16[16,64,128]{2,1,0:T(8,128)(2,1)S(1)} %pad_maximum_fusion.2.pack_ref), channel_id=1, source_target_pairs={{0,2},{2,0},{1,3},{3,1},{4,6},{6,4},{5,7},{7,5},{8,10},{10,8},{9,1... | collective-permute-start | bytes 786440 | tf_op jit(solution)/shard_map/ppermute | solution.py:182
  5.0 6.4 %collective-permute-start.1 = (bf16[3,3,64,256]{3,2,1,0:T(8,128)(2,1)}, bf16[3,3,64,256]{3,2,1,0:T(8,128)(2,1)S(1)}, u32[]{:S(2)}, u32[]{:S(2)}) collective-permute-start(bf16[3,3,64,256]{3,2,1,0:T(8,128)(2,1)} %w_ref.1), channel_id=1, source_target_pairs={{0,258},{2,256},{256,2},{258,0},{1,259},{3,257},{257,3},{259,1},{4... | collective-permute-start | bytes 884744 | tf_op jit(solution)/shard_map/ppermute | solution.py:182
  11.5 0.1 pad_add_fusion.where_ref
  11.6 0.0 copy-start
  11.6 1.0 %copy-done = bf16[3,3,64,256]{3,2,1,0:T(8,128)(2,1)S(1)} copy-done((bf16[3,3,64,256]{3,2,1,0:T(8,128)(2,1)S(1)}, bf16[3,3,64,256]{3,2,1,0:T(8,128)(2,1)}, u32[]{:S(2)}) %copy-start) | copy-done | bytes 294936
  12.5 0.1 pack.2
  12.6 0.0 copy-done.1
  12.6 2.5 %all_gather.9.near_ref = bf16[62,64,128]{2,1,0:T(8,128)(2,1)S(1)} all-gather(bf16[31,64,128]{2,1,0:T(8,128)(2,1)S(1)} %get-tuple-element.17), channel_id=1, replica_groups=mesh['xlo'=2,'y'=4,'zhi'=8,'zlo'=2,'xhi'=2,'core'=2] {'core'}, dimensions={0}, use_global_device_ids=true | all-gather | bytes 1523712 | tf_op jit(solution)/shard_map/all_gather | solution.py:194
  15.2 0.0 collective-permute-done.pack_ref
  15.2 1.9 %collective-permute-start.2 = (bf16[12,64,128]{2,1,0:T(8,128)(2,1)S(1)}, bf16[12,64,128]{2,1,0:T(8,128)(2,1)S(1)}, u32[]{:S(2)}, u32[]{:S(2)}) collective-permute-start(bf16[12,64,128]{2,1,0:T(8,128)(2,1)S(1)} %pad_maximum_fusion.3), channel_id=1, source_target_pairs={{0,4},{4,8},{8,12},{12,16},{16,20},{20,24},{24,28},{28,32},{32,36}... | collective-permute-start | bytes 589832 | tf_op jit(solution)/shard_map/ppermute | solution.py:182
  17.2 12.2 %collective-permute-start.3 = (bf16[12,64,128]{2,1,0:T(8,128)(2,1)S(1)}, bf16[12,64,128]{2,1,0:T(8,128)(2,1)S(1)}, u32[]{:S(2)}, u32[]{:S(2)}) collective-permute-start(bf16[12,64,128]{2,1,0:T(8,128)(2,1)S(1)} %pad_maximum_fusion.4), channel_id=1, source_target_pairs={{0,508},{4,0},{8,4},{12,8},{16,12},{20,16},{24,20},{28,24},{32,28}... | collective-permute-start | bytes 589832 | tf_op jit(solution)/shard_map/ppermute | solution.py:182
  29.4 0.0 collective-permute-done.1.w_ref
  29.4 0.1 pack.3
  29.5 2.5 %all_gather.10.far_ref = bf16[62,64,128]{2,1,0:T(8,128)(2,1)S(1)} all-gather(bf16[31,64,128]{2,1,0:T(8,128)(2,1)S(1)} %get-tuple-element.18), channel_id=1, replica_groups=mesh['xlo'=2,'y'=4,'zhi'=8,'zlo'=2,'xhi'=2,'core'=2] {'core'}, dimensions={0}, use_global_device_ids=true | all-gather | bytes 1523712 | tf_op jit(solution)/shard_map/all_gather | solution.py:194
  32.0 1.6 %conv_tile.1 = (bf16[3,256,768]{2,1,0:T(8,128)(2,1)S(1)}, bf16[768,1024]{1,0:T(8,128)(2,1)S(1)}, f32[256,1536]{1,0:T(8,128)S(1)}) custom-call(bf16[62,64,128]{2,1,0:T(8,128)(2,1)S(1)} %all_gather.9.near_ref, bf16[62,64,128]{2,1,0:T(8,128)(2,1)S(1)} %all_gather.10.far_ref), custom_call_target="tpu_custom_call" | custom-call | flops 1207959552 | bytes 6291456 | tf_op jit(solution)/shard_map/conv_tile/pallas_call | solution.py:246
  33.6 0.0 collective-permute-done.2
  33.6 0.0 collective-permute-done.3
  33.6 0.1 pad_maximum_fusion
  33.7 2.5 %all_gather.11.rim_ref = bf16[60,64,128]{2,1,0:T(8,128)(2,1)S(1)} all-gather(bf16[30,64,128]{2,1,0:T(8,128)(2,1)S(1)} %pad_maximum_fusion), channel_id=1, replica_groups=mesh['xlo'=2,'y'=4,'zhi'=8,'zlo'=2,'xhi'=2,'core'=2] {'core'}, dimensions={0}, use_global_device_ids=true | all-gather | bytes 1474560 | tf_op jit(solution)/shard_map/all_gather | solution.py:194
  36.2 2.9 %conv_rim.1 = (bf16[2,4,64,128]{3,2,1,0:T(8,128)(2,1)}, bf16[2,3,3,64,128]{4,3,2,1,0:T(8,128)(2,1)S(1)}, f32[8,128]{1,0:T(8,128)S(1)}) custom-call(s32[2]{0:T(128)S(1)} %pad_add_fusion.where_ref, bf16[62,64,128]{2,1,0:T(8,128)(2,1)S(1)} %all_gather.9.near_ref, bf16[62,64,128]{2,1,0:T(8,128)(2,1)S(1)} %all_gather.10.far_ref, ...), custom_call_target="tpu_custom_call" | custom-call | tf_op jit(solution)/shard_map/conv_rim/pallas_call | solution.py:261
  39.2 0.1 fusion.3
  39.3 11.5 %all_to_all.15 = bf16[16,80,128]{2,1,0:T(8,128)(2,1)S(1)} all-to-all(bf16[16,80,128]{2,1,0:T(8,128)(2,1)S(1)} %pad_maximum_fusion.1), channel_id=1, replica_groups=mesh['xlo'=2,'y'=4,'zhi'=8,'zlo'=2,'xhi'=2,'core'=2] {'xlo','y','zlo'}, dimensions={0} | all-to-all | bytes 655360 | tf_op jit(solution)/shard_map/all_to_all | solution.py:293
  50.8 0.1 convert_reduce_fusion
  50.9 0.1 fusion.4
  51.1 24.7 %all_to_all.16 = bf16[8,80,128]{2,1,0:T(8,128)(2,1)S(1)} all-to-all(bf16[8,80,128]{2,1,0:T(8,128)(2,1)S(1)} %pad_maximum_fusion.5), channel_id=1, replica_groups=mesh['xlo'=2,'y'=4,'zhi'=8,'zlo'=2,'xhi'=2,'core'=2] {'zhi'}, dimensions={0} | all-to-all | bytes 327680 | tf_op jit(solution)/shard_map/all_to_all | solution.py:293
  75.9 10.4 %all_to_all.17 = bf16[16,72,128]{2,1,0:T(8,128)(2,1)S(1)} all-to-all(bf16[16,72,128]{2,1,0:T(8,128)(2,1)S(1)} %broadcast_in_dim.30), channel_id=1, replica_groups=mesh['xlo'=2,'y'=4,'zhi'=8,'zlo'=2,'xhi'=2,'core'=2] {'xlo','y','zlo'}, dimensions={0} | all-to-all | bytes 589824 | tf_op jit(solution)/shard_map/all_to_all | solution.py:293
  86.3 0.9 widen.1
  (23 shorter events, 0.3 us)
Async XLA Ops:
  0.6 12.0 %copy-start.1 = (bf16[3,3,64,256]{3,2,1,0:T(8,128)(2,1)S(1)}, bf16[3,3,64,256]{3,2,1,0:T(8,128)(2,1)}, u32[]{:S(2)}) copy-start(bf16[3,3,64,256]{3,2,1,0:T(8,128)(2,1)} %w_ref.1) | copy-start | bytes 884740
  1.7 13.5 %collective-permute-start = (bf16[16,64,128]{2,1,0:T(8,128)(2,1)S(1)}, bf16[16,64,128]{2,1,0:T(8,128)(2,1)S(1)}, u32[]{:S(2)}, u32[]{:S(2)}) collective-permute-start(bf16[16,64,128]{2,1,0:T(8,128)(2,1)S(1)} %pad_maximum_fusion.2.pack_ref), channel_id=1, source_target_pairs={{0,2},{2,0},{1,3},{3,1},{4,6},{6,4},{5,7},{7,5},{8,10},{10,8},{9,1... | collective-permute-start | bytes 786440 | tf_op jit(solution)/shard_map/ppermute | solution.py:182
  5.0 24.4 %collective-permute-start.1 = (bf16[3,3,64,256]{3,2,1,0:T(8,128)(2,1)}, bf16[3,3,64,256]{3,2,1,0:T(8,128)(2,1)S(1)}, u32[]{:S(2)}, u32[]{:S(2)}) collective-permute-start(bf16[3,3,64,256]{3,2,1,0:T(8,128)(2,1)} %w_ref.1), channel_id=1, source_target_pairs={{0,258},{2,256},{256,2},{258,0},{1,259},{3,257},{257,3},{259,1},{4... | collective-permute-start | bytes 884744 | tf_op jit(solution)/shard_map/ppermute | solution.py:182
  11.6 1.0 %copy-start = (bf16[3,3,64,256]{3,2,1,0:T(8,128)(2,1)S(1)}, bf16[3,3,64,256]{3,2,1,0:T(8,128)(2,1)}, u32[]{:S(2)}) copy-start(bf16[3,3,64,256]{3,2,1,0:T(8,128)(2,1)} %w_ref.1) | copy-start | bytes 884740
  15.2 18.4 %collective-permute-start.2 = (bf16[12,64,128]{2,1,0:T(8,128)(2,1)S(1)}, bf16[12,64,128]{2,1,0:T(8,128)(2,1)S(1)}, u32[]{:S(2)}, u32[]{:S(2)}) collective-permute-start(bf16[12,64,128]{2,1,0:T(8,128)(2,1)S(1)} %pad_maximum_fusion.3), channel_id=1, source_target_pairs={{0,4},{4,8},{8,12},{12,16},{16,20},{20,24},{24,28},{28,32},{32,36}... | collective-permute-start | bytes 589832 | tf_op jit(solution)/shard_map/ppermute | solution.py:182
  17.2 16.4 %collective-permute-start.3 = (bf16[12,64,128]{2,1,0:T(8,128)(2,1)S(1)}, bf16[12,64,128]{2,1,0:T(8,128)(2,1)S(1)}, u32[]{:S(2)}, u32[]{:S(2)}) collective-permute-start(bf16[12,64,128]{2,1,0:T(8,128)(2,1)S(1)} %pad_maximum_fusion.4), channel_id=1, source_target_pairs={{0,508},{4,0},{8,4},{12,8},{16,12},{20,16},{24,20},{28,24},{32,28}... | collective-permute-start | bytes 589832 | tf_op jit(solution)/shard_map/ppermute | solution.py:182

commit v7 on v6

--- a/solution.py
+++ b/solution.py
@@ -79,10 +79,10 @@
 
 
 def late_kernel(
-    early, where_ref, near_ref, far_ref, rim_ref, wt_ref, xs_ref, part_ref, wown_ref, cos_ref,
+    early, near_ref, far_ref, rim_ref, wt_ref, xs_ref, part_ref, wown_ref, cos_ref,
     gi_ref, wg_ref, loss_ref, xh_ref, tg_ref, cot_ref, grad_ref, sem,
 ):
-    xhi, core = where_ref[0], where_ref[1]
+    xhi, core = lax.axis_index("xhi"), lax.axis_index("core")
     batch, cols, chans, lat = gi_ref.shape
     wide = batch * lat
     tile = batch * cols
@@ -134,7 +134,8 @@
         cot_ref[:, at] = cot.astype(BF16)
         if 1 <= f <= cols:
             loss += jnp.sum((cot * diff).reshape(-1, 8, wide), axis=0)
-    loss_ref[...] = jnp.full(loss_ref.shape, jnp.sum(loss), F32)
+    loss = jnp.sum(jnp.sum(loss, axis=1, keepdims=True), axis=0, keepdims=True)
+    loss_ref[...] = jnp.broadcast_to(loss, loss_ref.shape)
 
     for j in range(cols):
         total = jnp.zeros((3 * chans, wide), F32)
@@ -155,19 +156,21 @@
 
     mine = pl.ds(pl.multiple_of(core * 3 * chans, chans), 3 * chans)
     half = wg_ref.shape[-1]
+    total = None
+    for j in range(cols):
+        stack = jnp.concatenate([column(q + j + 1, mine) for q in range(3)], axis=0)
+        term = lax.dot_general(
+            stack,
+            cot_ref[:, pl.ds((j + 1) * wide, wide)],
+            (((1,), (1,)), ((), ())),
+            preferred_element_type=F32,
+        )
+        total = term if total is None else total + term
     for q in range(3):
-        fresh = jnp.zeros((3 * chans, 2 * half), F32)
-        for j in range(cols):
-            fresh += lax.dot_general(
-                column(q + j + 1, mine),
-                cot_ref[:, pl.ds((j + 1) * wide, wide)],
-                (((1,), (1,)), ((), ())),
-                preferred_element_type=F32,
-            )
-        fresh = fresh.astype(BF16)
         for p in range(3):
+            at = (q * 3 + p) * chans
             for h in range(2):
-                wg_ref[h, p, q] = fresh[p * chans : (p + 1) * chans, h * half : (h + 1) * half]
+                wg_ref[h, p, q] = total[at : at + chans, h * half : (h + 1) * half].astype(BF16)
     leaving.wait()
 
 
@@ -188,7 +191,6 @@
     tiles = lax.axis_size(SPACE)
     lon = cols * tiles
     near, far = lax.axis_size(NEAR), lax.axis_size("zhi")
-    xhi, core = lax.axis_index("xhi"), lax.axis_index("core")
 
     def gathered(a):
         return lax.all_gather(a, "core", axis=0, tiled=True)
@@ -240,7 +242,6 @@
 
     coslat = jnp.cos(jnp.pi * ((jnp.arange(lat, dtype=F32) + 0.5) / lat - 0.5))
     cos_rows = jnp.broadcast_to(jnp.tile(coslat, batch)[None], (8, batch * lat))
-    place = jnp.stack([xhi, core]).astype(jnp.int32)
 
     wide = batch * lat
     wt, xs, part = pl.pallas_call(
@@ -265,7 +266,7 @@
             jax.ShapeDtypeStruct((2, 3, 3, chans, half), BF16),
             jax.ShapeDtypeStruct((8, 128), F32),
         ),
-        in_specs=[pl.BlockSpec(memory_space=pltpu.SMEM)] + [vmem] * 8,
+        in_specs=[vmem] * 8,
         out_specs=(pl.BlockSpec(memory_space=pl.ANY), vmem, vmem),
         scratch_shapes=[
             pltpu.VMEM((3 * channels, 4 * wide), BF16),
@@ -276,7 +277,7 @@
         ],
         compiler_params=pltpu.CompilerParams(vmem_limit_bytes=16 * 1024 * 1024),
         name="conv_rim",
-    )(place, near_pack, far_pack, rim, wt, xs, part, wown, cos_rows)
+    )(near_pack, far_pack, rim, wt, xs, part, wown, cos_rows)
 
     rows = 9 * chans * 2 // near
     parts = wg.reshape(near, rows, half)

time: 87.6 us -> 86.8 us (level)
  no operation moved by 1% of the time
where the time goes in v7:
time: 86.8 us; the launch traced here: 86.4 us
  blocking collectives  54.2 us (62%)
  starting transfers between devices  23.9 us (28%)
  Pallas kernels  4.91 us (6%)
  other arithmetic  1.52 us (2%)
  local copies, waits for them, and re-layouts  1.11 us (1%)
  between operations  0.89 us (1%)
    all_to_all x3, blocking collectives, everyone(): return lax.all_to_all(a, axes, 0, 0, tiled=True)  46.6 us
    ppermute x4, starting transfers between devices, exchange(): return lax.ppermute(a, axes, [(i, to(i)) for i in range(count)])  23.9 us
    all_gather x3, blocking collectives, gathered(): return lax.all_gather(a, 'core', axis=0, tiled=True)  7.58 us
    pallas_call x1, Pallas kernels, local(): pl.pallas_call(functools.partial(late_kernel, early), out_shape=(jax.Shap...  2.29 us
  transfers between devices with their start and end apart: 4, of which 0 were waited for; matrix products, arithmetic and copies ran while one was open for 0% of the time, Pallas kernels for 2%

profile of v7, /device:TPU:6, one launch (start us, length us, event | category | flops | bytes accessed | tf_op | source)
XLA Modules:
  0.0 86.4 jit_solution(4897423259501419650)
XLA Ops:
  0.6 0.0 copy-start.1
  0.6 1.0 %pad_maximum_fusion.2.pack_ref = bf16[16,64,128]{2,1,0:T(8,128)(2,1)S(1)} fusion(bf16[8,64,128]{2,1,0:T(8,128)(2,1)} %bitcast.39, bf16[8,64,128]{2,1,0:T(8,128)(2,1)} %bitcast.40), kind=kLoop, calls=%fused_computation.4 | loop fusion | flops 131072 | bytes 524288 | tf_op jit(solution)/shard_map/concatenate | solution.py:198
  1.7 3.3 %collective-permute-start = (bf16[16,64,128]{2,1,0:T(8,128)(2,1)S(1)}, bf16[16,64,128]{2,1,0:T(8,128)(2,1)S(1)}, u32[]{:S(2)}, u32[]{:S(2)}) collective-permute-start(bf16[16,64,128]{2,1,0:T(8,128)(2,1)S(1)} %pad_maximum_fusion.2.pack_ref), channel_id=1, source_target_pairs={{0,2},{2,0},{1,3},{3,1},{4,6},{6,4},{5,7},{7,5},{8,10},{10,8},{9,1... | collective-permute-start | bytes 786440 | tf_op jit(solution)/shard_map/ppermute | solution.py:185
  5.0 6.4 %collective-permute-start.1 = (bf16[3,3,64,256]{3,2,1,0:T(8,128)(2,1)}, bf16[3,3,64,256]{3,2,1,0:T(8,128)(2,1)S(1)}, u32[]{:S(2)}, u32[]{:S(2)}) collective-permute-start(bf16[3,3,64,256]{3,2,1,0:T(8,128)(2,1)} %w_ref.1), channel_id=1, source_target_pairs={{0,258},{2,256},{256,2},{258,0},{1,259},{3,257},{257,3},{259,1},{4... | collective-permute-start | bytes 884744 | tf_op jit(solution)/shard_map/ppermute | solution.py:185
  11.5 0.0 copy-start
  11.5 1.0 %copy-done = bf16[3,3,64,256]{3,2,1,0:T(8,128)(2,1)S(1)} copy-done((bf16[3,3,64,256]{3,2,1,0:T(8,128)(2,1)S(1)}, bf16[3,3,64,256]{3,2,1,0:T(8,128)(2,1)}, u32[]{:S(2)}) %copy-start) | copy-done | bytes 294936
  12.5 0.1 pack.2
  12.5 0.0 copy-done.1
  12.6 2.5 %all_gather.9.near_ref = bf16[62,64,128]{2,1,0:T(8,128)(2,1)S(1)} all-gather(bf16[31,64,128]{2,1,0:T(8,128)(2,1)S(1)} %get-tuple-element.17), channel_id=1, replica_groups=mesh['xlo'=2,'y'=4,'zhi'=8,'zlo'=2,'xhi'=2,'core'=2] {'core'}, dimensions={0}, use_global_device_ids=true | all-gather | bytes 1523712 | tf_op jit(solution)/shard_map/all_gather | solution.py:196
  15.1 0.0 collective-permute-done.pack_ref
  15.2 2.0 %collective-permute-start.2 = (bf16[12,64,128]{2,1,0:T(8,128)(2,1)S(1)}, bf16[12,64,128]{2,1,0:T(8,128)(2,1)S(1)}, u32[]{:S(2)}, u32[]{:S(2)}) collective-permute-start(bf16[12,64,128]{2,1,0:T(8,128)(2,1)S(1)} %pad_maximum_fusion.3), channel_id=1, source_target_pairs={{0,4},{4,8},{8,12},{12,16},{16,20},{20,24},{24,28},{28,32},{32,36}... | collective-permute-start | bytes 589832 | tf_op jit(solution)/shard_map/ppermute | solution.py:185
  17.2 12.2 %collective-permute-start.3 = (bf16[12,64,128]{2,1,0:T(8,128)(2,1)S(1)}, bf16[12,64,128]{2,1,0:T(8,128)(2,1)S(1)}, u32[]{:S(2)}, u32[]{:S(2)}) collective-permute-start(bf16[12,64,128]{2,1,0:T(8,128)(2,1)S(1)} %pad_maximum_fusion.4), channel_id=1, source_target_pairs={{0,508},{4,0},{8,4},{12,8},{16,12},{20,16},{24,20},{28,24},{32,28}... | collective-permute-start | bytes 589832 | tf_op jit(solution)/shard_map/ppermute | solution.py:185
  29.4 0.0 collective-permute-done.1.w_ref
  29.4 0.1 pack.3
  29.5 2.5 %all_gather.10.far_ref = bf16[62,64,128]{2,1,0:T(8,128)(2,1)S(1)} all-gather(bf16[31,64,128]{2,1,0:T(8,128)(2,1)S(1)} %get-tuple-element.18), channel_id=1, replica_groups=mesh['xlo'=2,'y'=4,'zhi'=8,'zlo'=2,'xhi'=2,'core'=2] {'core'}, dimensions={0}, use_global_device_ids=true | all-gather | bytes 1523712 | tf_op jit(solution)/shard_map/all_gather | solution.py:196
  32.0 1.6 %conv_tile.1 = (bf16[3,256,768]{2,1,0:T(8,128)(2,1)S(1)}, bf16[768,1024]{1,0:T(8,128)(2,1)S(1)}, f32[256,1536]{1,0:T(8,128)S(1)}) custom-call(bf16[62,64,128]{2,1,0:T(8,128)(2,1)S(1)} %all_gather.9.near_ref, bf16[62,64,128]{2,1,0:T(8,128)(2,1)S(1)} %all_gather.10.far_ref), custom_call_target="tpu_custom_call" | custom-call | flops 1207959552 | bytes 6291456 | tf_op jit(solution)/shard_map/conv_tile/pallas_call | solution.py:247
  33.6 0.0 collective-permute-done.2
  33.6 0.0 collective-permute-done.3
  33.7 0.1 pad_maximum_fusion
  33.7 2.5 %all_gather.11.rim_ref = bf16[60,64,128]{2,1,0:T(8,128)(2,1)S(1)} all-gather(bf16[30,64,128]{2,1,0:T(8,128)(2,1)S(1)} %pad_maximum_fusion), channel_id=1, replica_groups=mesh['xlo'=2,'y'=4,'zhi'=8,'zlo'=2,'xhi'=2,'core'=2] {'core'}, dimensions={0}, use_global_device_ids=true | all-gather | bytes 1474560 | tf_op jit(solution)/shard_map/all_gather | solution.py:196
  36.3 2.3 %conv_rim.1 = (bf16[2,4,64,128]{3,2,1,0:T(8,128)(2,1)}, bf16[2,3,3,64,128]{4,3,2,1,0:T(8,128)(2,1)S(1)}, f32[8,128]{1,0:T(8,128)S(1)}) custom-call(bf16[62,64,128]{2,1,0:T(8,128)(2,1)S(1)} %all_gather.9.near_ref, bf16[62,64,128]{2,1,0:T(8,128)(2,1)S(1)} %all_gather.10.far_ref, bf16[60,64,128]{2,1,0:T(8,128)(2,1)S(1)} %all_gather.11.rim_ref, ...), custom_call_target="tpu_custom_call" | custom-call | tf_op jit(solution)/shard_map/conv_rim/pallas_call | solution.py:262
  38.6 0.1 fusion.3
  38.7 11.5 %all_to_all.15 = bf16[16,80,128]{2,1,0:T(8,128)(2,1)S(1)} all-to-all(bf16[16,80,128]{2,1,0:T(8,128)(2,1)S(1)} %pad_maximum_fusion.1), channel_id=1, replica_groups=mesh['xlo'=2,'y'=4,'zhi'=8,'zlo'=2,'xhi'=2,'core'=2] {'xlo','y','zlo'}, dimensions={0} | all-to-all | bytes 655360 | tf_op jit(solution)/shard_map/all_to_all | solution.py:294
  50.2 0.1 convert_reduce_fusion
  50.3 0.1 fusion.4
  50.4 24.6 %all_to_all.16 = bf16[8,80,128]{2,1,0:T(8,128)(2,1)S(1)} all-to-all(bf16[8,80,128]{2,1,0:T(8,128)(2,1)S(1)} %pad_maximum_fusion.5), channel_id=1, replica_groups=mesh['xlo'=2,'y'=4,'zhi'=8,'zlo'=2,'xhi'=2,'core'=2] {'zhi'}, dimensions={0} | all-to-all | bytes 327680 | tf_op jit(solution)/shard_map/all_to_all | solution.py:294
  75.1 10.4 %all_to_all.17 = bf16[16,72,128]{2,1,0:T(8,128)(2,1)S(1)} all-to-all(bf16[16,72,128]{2,1,0:T(8,128)(2,1)S(1)} %broadcast_in_dim.30), channel_id=1, replica_groups=mesh['xlo'=2,'y'=4,'zhi'=8,'zlo'=2,'xhi'=2,'core'=2] {'xlo','y','zlo'}, dimensions={0} | all-to-all | bytes 589824 | tf_op jit(solution)/shard_map/all_to_all | solution.py:294
  85.6 0.9 %widen.1 = (f32[3,3,64,256]{3,2,1,0:T(8,128)}, f32[1,1]{1,0:T(1,128)}) custom-call(bf16[2,3,3,64,128]{4,3,2,1,0:T(8,128)(2,1)S(1)} %bitcast.31, f32[4,128]{1,0:T(4,128)S(1)} %slice_add_fusion.value_ref), custom_call_target="tpu_custom_call" | custom-call | tf_op jit(solution)/shard_map/widen/pallas_call | solution.py:309
  (23 shorter events, 0.3 us)
Async XLA Ops:
  0.6 11.9 %copy-start.1 = (bf16[3,3,64,256]{3,2,1,0:T(8,128)(2,1)S(1)}, bf16[3,3,64,256]{3,2,1,0:T(8,128)(2,1)}, u32[]{:S(2)}) copy-start(bf16[3,3,64,256]{3,2,1,0:T(8,128)(2,1)} %w_ref.1) | copy-start | bytes 884740
  1.7 13.4 %collective-permute-start = (bf16[16,64,128]{2,1,0:T(8,128)(2,1)S(1)}, bf16[16,64,128]{2,1,0:T(8,128)(2,1)S(1)}, u32[]{:S(2)}, u32[]{:S(2)}) collective-permute-start(bf16[16,64,128]{2,1,0:T(8,128)(2,1)S(1)} %pad_maximum_fusion.2.pack_ref), channel_id=1, source_target_pairs={{0,2},{2,0},{1,3},{3,1},{4,6},{6,4},{5,7},{7,5},{8,10},{10,8},{9,1... | collective-permute-start | bytes 786440 | tf_op jit(solution)/shard_map/ppermute | solution.py:185
  5.0 24.4 %collective-permute-start.1 = (bf16[3,3,64,256]{3,2,1,0:T(8,128)(2,1)}, bf16[3,3,64,256]{3,2,1,0:T(8,128)(2,1)S(1)}, u32[]{:S(2)}, u32[]{:S(2)}) collective-permute-start(bf16[3,3,64,256]{3,2,1,0:T(8,128)(2,1)} %w_ref.1), channel_id=1, source_target_pairs={{0,258},{2,256},{256,2},{258,0},{1,259},{3,257},{257,3},{259,1},{4... | collective-permute-start | bytes 884744 | tf_op jit(solution)/shard_map/ppermute | solution.py:185
  11.5 1.0 %copy-start = (bf16[3,3,64,256]{3,2,1,0:T(8,128)(2,1)S(1)}, bf16[3,3,64,256]{3,2,1,0:T(8,128)(2,1)}, u32[]{:S(2)}) copy-start(bf16[3,3,64,256]{3,2,1,0:T(8,128)(2,1)} %w_ref.1) | copy-start | bytes 884740
  15.2 18.5 %collective-permute-start.2 = (bf16[12,64,128]{2,1,0:T(8,128)(2,1)S(1)}, bf16[12,64,128]{2,1,0:T(8,128)(2,1)S(1)}, u32[]{:S(2)}, u32[]{:S(2)}) collective-permute-start(bf16[12,64,128]{2,1,0:T(8,128)(2,1)S(1)} %pad_maximum_fusion.3), channel_id=1, source_target_pairs={{0,4},{4,8},{8,12},{12,16},{16,20},{20,24},{24,28},{28,32},{32,36}... | collective-permute-start | bytes 589832 | tf_op jit(solution)/shard_map/ppermute | solution.py:185
  17.2 16.5 %collective-permute-start.3 = (bf16[12,64,128]{2,1,0:T(8,128)(2,1)S(1)}, bf16[12,64,128]{2,1,0:T(8,128)(2,1)S(1)}, u32[]{:S(2)}, u32[]{:S(2)}) collective-permute-start(bf16[12,64,128]{2,1,0:T(8,128)(2,1)S(1)} %pad_maximum_fusion.4), channel_id=1, source_target_pairs={{0,508},{4,0},{8,4},{12,8},{16,12},{20,16},{24,20},{28,24},{32,28}... | collective-permute-start | bytes 589832 | tf_op jit(solution)/shard_map/ppermute | solution.py:185

commit v8 on v7

--- a/solution.py
+++ b/solution.py
@@ -80,7 +80,7 @@
 
 def late_kernel(
     early, near_ref, far_ref, rim_ref, wt_ref, xs_ref, part_ref, wown_ref, cos_ref,
-    gi_ref, wg_ref, loss_ref, xh_ref, tg_ref, cot_ref, grad_ref, sem,
+    gi_ref, wg_ref, loss_ref, xh_ref, tg_ref, cot_ref,
 ):
     xhi, core = lax.axis_index("xhi"), lax.axis_index("core")
     batch, cols, chans, lat = gi_ref.shape
@@ -150,9 +150,7 @@
                 + part[chans : 2 * chans]
                 + shift_lanes(part[2 * chans :], -1)
             )
-            grad_ref[b, j] = grad.astype(BF16)
-    leaving = pltpu.make_async_copy(grad_ref, gi_ref, sem)
-    leaving.start()
+            gi_ref[b, j] = grad.astype(BF16)
 
     mine = pl.ds(pl.multiple_of(core * 3 * chans, chans), 3 * chans)
     half = wg_ref.shape[-1]
@@ -171,7 +169,6 @@
             at = (q * 3 + p) * chans
             for h in range(2):
                 wg_ref[h, p, q] = total[at : at + chans, h * half : (h + 1) * half].astype(BF16)
-    leaving.wait()
 
 
 def last_kernel(scale, halves_ref, value_ref, wg_ref, loss_ref):
@@ -267,13 +264,11 @@
             jax.ShapeDtypeStruct((8, 128), F32),
         ),
         in_specs=[vmem] * 8,
-        out_specs=(pl.BlockSpec(memory_space=pl.ANY), vmem, vmem),
+        out_specs=(vmem, vmem, vmem),
         scratch_shapes=[
             pltpu.VMEM((3 * channels, 4 * wide), BF16),
             pltpu.VMEM((channels, (cols + 2) * wide), BF16),
             pltpu.VMEM((channels, (cols + 2) * wide), BF16),
-            pltpu.VMEM((batch, cols, chans, lat), BF16),
-            pltpu.SemaphoreType.DMA,
         ],
         compiler_params=pltpu.CompilerParams(vmem_limit_bytes=16 * 1024 * 1024),
         name="conv_rim",

time: 86.8 us -> 86.8 us (level)
  no operation moved by 1% of the time
where the time goes in v8:
time: 86.8 us; the launch traced here: 86.4 us
  blocking collectives  54.2 us (62%)
  starting transfers between devices  23.9 us (28%)
  Pallas kernels  4.9 us (6%)
  other arithmetic  1.52 us (2%)
  local copies, waits for them, and re-layouts  1.11 us (1%)
  between operations  0.88 us (1%)
    all_to_all x3, blocking collectives, everyone(): return lax.all_to_all(a, axes, 0, 0, tiled=True)  46.6 us
    ppermute x4, starting transfers between devices, exchange(): return lax.ppermute(a, axes, [(i, to(i)) for i in range(count)])  23.9 us
    all_gather x3, blocking collectives, gathered(): return lax.all_gather(a, 'core', axis=0, tiled=True)  7.58 us
    pallas_call x1, Pallas kernels, local(): pl.pallas_call(functools.partial(late_kernel, early), out_shape=(jax.Shap...  2.28 us
  transfers between devices with their start and end apart: 4, of which 0 were waited for; matrix products, arithmetic and copies ran while one was open for 0% of the time, Pallas kernels for 2%

profile of v8, /device:TPU:6, one launch (start us, length us, event | category | flops | bytes accessed | tf_op | source)
XLA Modules:
  0.0 86.4 jit_solution(11446457337155999048)
XLA Ops:
  0.6 0.0 copy-start.1
  0.6 1.0 %pad_maximum_fusion.2.pack_ref = bf16[16,64,128]{2,1,0:T(8,128)(2,1)S(1)} fusion(bf16[8,64,128]{2,1,0:T(8,128)(2,1)} %bitcast.39, bf16[8,64,128]{2,1,0:T(8,128)(2,1)} %bitcast.40), kind=kLoop, calls=%fused_computation.4 | loop fusion | flops 131072 | bytes 524288 | tf_op jit(solution)/shard_map/concatenate | solution.py:195
  1.7 3.3 %collective-permute-start = (bf16[16,64,128]{2,1,0:T(8,128)(2,1)S(1)}, bf16[16,64,128]{2,1,0:T(8,128)(2,1)S(1)}, u32[]{:S(2)}, u32[]{:S(2)}) collective-permute-start(bf16[16,64,128]{2,1,0:T(8,128)(2,1)S(1)} %pad_maximum_fusion.2.pack_ref), channel_id=1, source_target_pairs={{0,2},{2,0},{1,3},{3,1},{4,6},{6,4},{5,7},{7,5},{8,10},{10,8},{9,1... | collective-permute-start | bytes 786440 | tf_op jit(solution)/shard_map/ppermute | solution.py:182
  5.0 6.4 %collective-permute-start.1 = (bf16[3,3,64,256]{3,2,1,0:T(8,128)(2,1)}, bf16[3,3,64,256]{3,2,1,0:T(8,128)(2,1)S(1)}, u32[]{:S(2)}, u32[]{:S(2)}) collective-permute-start(bf16[3,3,64,256]{3,2,1,0:T(8,128)(2,1)} %w_ref.1), channel_id=1, source_target_pairs={{0,258},{2,256},{256,2},{258,0},{1,259},{3,257},{257,3},{259,1},{4... | collective-permute-start | bytes 884744 | tf_op jit(solution)/shard_map/ppermute | solution.py:182
  11.5 0.0 copy-start
  11.5 1.0 %copy-done = bf16[3,3,64,256]{3,2,1,0:T(8,128)(2,1)S(1)} copy-done((bf16[3,3,64,256]{3,2,1,0:T(8,128)(2,1)S(1)}, bf16[3,3,64,256]{3,2,1,0:T(8,128)(2,1)}, u32[]{:S(2)}) %copy-start) | copy-done | bytes 294936
  12.5 0.1 pack.2
  12.5 0.0 copy-done.1
  12.6 2.5 %all_gather.9.near_ref = bf16[62,64,128]{2,1,0:T(8,128)(2,1)S(1)} all-gather(bf16[31,64,128]{2,1,0:T(8,128)(2,1)S(1)} %get-tuple-element.17), channel_id=1, replica_groups=mesh['xlo'=2,'y'=4,'zhi'=8,'zlo'=2,'xhi'=2,'core'=2] {'core'}, dimensions={0}, use_global_device_ids=true | all-gather | bytes 1523712 | tf_op jit(solution)/shard_map/all_gather | solution.py:193
  15.1 0.0 collective-permute-done.pack_ref
  15.2 2.0 %collective-permute-start.2 = (bf16[12,64,128]{2,1,0:T(8,128)(2,1)S(1)}, bf16[12,64,128]{2,1,0:T(8,128)(2,1)S(1)}, u32[]{:S(2)}, u32[]{:S(2)}) collective-permute-start(bf16[12,64,128]{2,1,0:T(8,128)(2,1)S(1)} %pad_maximum_fusion.3), channel_id=1, source_target_pairs={{0,4},{4,8},{8,12},{12,16},{16,20},{20,24},{24,28},{28,32},{32,36}... | collective-permute-start | bytes 589832 | tf_op jit(solution)/shard_map/ppermute | solution.py:182
  17.2 12.2 %collective-permute-start.3 = (bf16[12,64,128]{2,1,0:T(8,128)(2,1)S(1)}, bf16[12,64,128]{2,1,0:T(8,128)(2,1)S(1)}, u32[]{:S(2)}, u32[]{:S(2)}) collective-permute-start(bf16[12,64,128]{2,1,0:T(8,128)(2,1)S(1)} %pad_maximum_fusion.4), channel_id=1, source_target_pairs={{0,508},{4,0},{8,4},{12,8},{16,12},{20,16},{24,20},{28,24},{32,28}... | collective-permute-start | bytes 589832 | tf_op jit(solution)/shard_map/ppermute | solution.py:182
  29.4 0.0 collective-permute-done.1.w_ref
  29.4 0.1 pack.3
  29.5 2.5 %all_gather.10.far_ref = bf16[62,64,128]{2,1,0:T(8,128)(2,1)S(1)} all-gather(bf16[31,64,128]{2,1,0:T(8,128)(2,1)S(1)} %get-tuple-element.18), channel_id=1, replica_groups=mesh['xlo'=2,'y'=4,'zhi'=8,'zlo'=2,'xhi'=2,'core'=2] {'core'}, dimensions={0}, use_global_device_ids=true | all-gather | bytes 1523712 | tf_op jit(solution)/shard_map/all_gather | solution.py:193
  32.0 1.6 %conv_tile.1 = (bf16[3,256,768]{2,1,0:T(8,128)(2,1)S(1)}, bf16[768,1024]{1,0:T(8,128)(2,1)S(1)}, f32[256,1536]{1,0:T(8,128)S(1)}) custom-call(bf16[62,64,128]{2,1,0:T(8,128)(2,1)S(1)} %all_gather.9.near_ref, bf16[62,64,128]{2,1,0:T(8,128)(2,1)S(1)} %all_gather.10.far_ref), custom_call_target="tpu_custom_call" | custom-call | flops 1207959552 | bytes 6291456 | tf_op jit(solution)/shard_map/conv_tile/pallas_call | solution.py:244
  33.6 0.0 collective-permute-done.2
  33.6 0.0 collective-permute-done.3
  33.7 0.1 pad_maximum_fusion
  33.7 2.5 %all_gather.11.rim_ref = bf16[60,64,128]{2,1,0:T(8,128)(2,1)S(1)} all-gather(bf16[30,64,128]{2,1,0:T(8,128)(2,1)S(1)} %pad_maximum_fusion), channel_id=1, replica_groups=mesh['xlo'=2,'y'=4,'zhi'=8,'zlo'=2,'xhi'=2,'core'=2] {'core'}, dimensions={0}, use_global_device_ids=true | all-gather | bytes 1474560 | tf_op jit(solution)/shard_map/all_gather | solution.py:193
  36.3 2.3 %conv_rim.1 = (bf16[2,4,64,128]{3,2,1,0:T(8,128)(2,1)}, bf16[2,3,3,64,128]{4,3,2,1,0:T(8,128)(2,1)S(1)}, f32[8,128]{1,0:T(8,128)S(1)}) custom-call(bf16[62,64,128]{2,1,0:T(8,128)(2,1)S(1)} %all_gather.9.near_ref, bf16[62,64,128]{2,1,0:T(8,128)(2,1)S(1)} %all_gather.10.far_ref, bf16[60,64,128]{2,1,0:T(8,128)(2,1)S(1)} %all_gather.11.rim_ref, ...), custom_call_target="tpu_custom_call" | custom-call | tf_op jit(solution)/shard_map/conv_rim/pallas_call | solution.py:259
  38.5 0.1 fusion.3
  38.7 11.5 %all_to_all.15 = bf16[16,80,128]{2,1,0:T(8,128)(2,1)S(1)} all-to-all(bf16[16,80,128]{2,1,0:T(8,128)(2,1)S(1)} %pad_maximum_fusion.1), channel_id=1, replica_groups=mesh['xlo'=2,'y'=4,'zhi'=8,'zlo'=2,'xhi'=2,'core'=2] {'xlo','y','zlo'}, dimensions={0} | all-to-all | bytes 655360 | tf_op jit(solution)/shard_map/all_to_all | solution.py:289
  50.2 0.1 convert_reduce_fusion
  50.3 0.1 fusion.4
  50.4 24.6 %all_to_all.16 = bf16[8,80,128]{2,1,0:T(8,128)(2,1)S(1)} all-to-all(bf16[8,80,128]{2,1,0:T(8,128)(2,1)S(1)} %pad_maximum_fusion.5), channel_id=1, replica_groups=mesh['xlo'=2,'y'=4,'zhi'=8,'zlo'=2,'xhi'=2,'core'=2] {'zhi'}, dimensions={0} | all-to-all | bytes 327680 | tf_op jit(solution)/shard_map/all_to_all | solution.py:289
  75.1 10.4 %all_to_all.17 = bf16[16,72,128]{2,1,0:T(8,128)(2,1)S(1)} all-to-all(bf16[16,72,128]{2,1,0:T(8,128)(2,1)S(1)} %broadcast_in_dim.30), channel_id=1, replica_groups=mesh['xlo'=2,'y'=4,'zhi'=8,'zlo'=2,'xhi'=2,'core'=2] {'xlo','y','zlo'}, dimensions={0} | all-to-all | bytes 589824 | tf_op jit(solution)/shard_map/all_to_all | solution.py:289
  85.6 0.9 %widen.1 = (f32[3,3,64,256]{3,2,1,0:T(8,128)}, f32[1,1]{1,0:T(1,128)}) custom-call(bf16[2,3,3,64,128]{4,3,2,1,0:T(8,128)(2,1)S(1)} %bitcast.31, f32[4,128]{1,0:T(4,128)S(1)} %slice_add_fusion.value_ref), custom_call_target="tpu_custom_call" | custom-call | tf_op jit(solution)/shard_map/widen/pallas_call | solution.py:304
  (23 shorter events, 0.3 us)
Async XLA Ops:
  0.6 11.9 %copy-start.1 = (bf16[3,3,64,256]{3,2,1,0:T(8,128)(2,1)S(1)}, bf16[3,3,64,256]{3,2,1,0:T(8,128)(2,1)}, u32[]{:S(2)}) copy-start(bf16[3,3,64,256]{3,2,1,0:T(8,128)(2,1)} %w_ref.1) | copy-start | bytes 884740
  1.7 13.4 %collective-permute-start = (bf16[16,64,128]{2,1,0:T(8,128)(2,1)S(1)}, bf16[16,64,128]{2,1,0:T(8,128)(2,1)S(1)}, u32[]{:S(2)}, u32[]{:S(2)}) collective-permute-start(bf16[16,64,128]{2,1,0:T(8,128)(2,1)S(1)} %pad_maximum_fusion.2.pack_ref), channel_id=1, source_target_pairs={{0,2},{2,0},{1,3},{3,1},{4,6},{6,4},{5,7},{7,5},{8,10},{10,8},{9,1... | collective-permute-start | bytes 786440 | tf_op jit(solution)/shard_map/ppermute | solution.py:182
  5.0 24.4 %collective-permute-start.1 = (bf16[3,3,64,256]{3,2,1,0:T(8,128)(2,1)}, bf16[3,3,64,256]{3,2,1,0:T(8,128)(2,1)S(1)}, u32[]{:S(2)}, u32[]{:S(2)}) collective-permute-start(bf16[3,3,64,256]{3,2,1,0:T(8,128)(2,1)} %w_ref.1), channel_id=1, source_target_pairs={{0,258},{2,256},{256,2},{258,0},{1,259},{3,257},{257,3},{259,1},{4... | collective-permute-start | bytes 884744 | tf_op jit(solution)/shard_map/ppermute | solution.py:182
  11.5 1.0 %copy-start = (bf16[3,3,64,256]{3,2,1,0:T(8,128)(2,1)S(1)}, bf16[3,3,64,256]{3,2,1,0:T(8,128)(2,1)}, u32[]{:S(2)}) copy-start(bf16[3,3,64,256]{3,2,1,0:T(8,128)(2,1)} %w_ref.1) | copy-start | bytes 884740
  15.2 18.5 %collective-permute-start.2 = (bf16[12,64,128]{2,1,0:T(8,128)(2,1)S(1)}, bf16[12,64,128]{2,1,0:T(8,128)(2,1)S(1)}, u32[]{:S(2)}, u32[]{:S(2)}) collective-permute-start(bf16[12,64,128]{2,1,0:T(8,128)(2,1)S(1)} %pad_maximum_fusion.3), channel_id=1, source_target_pairs={{0,4},{4,8},{8,12},{12,16},{16,20},{20,24},{24,28},{28,32},{32,36}... | collective-permute-start | bytes 589832 | tf_op jit(solution)/shard_map/ppermute | solution.py:182
  17.2 16.5 %collective-permute-start.3 = (bf16[12,64,128]{2,1,0:T(8,128)(2,1)S(1)}, bf16[12,64,128]{2,1,0:T(8,128)(2,1)S(1)}, u32[]{:S(2)}, u32[]{:S(2)}) collective-permute-start(bf16[12,64,128]{2,1,0:T(8,128)(2,1)S(1)} %pad_maximum_fusion.4), channel_id=1, source_target_pairs={{0,508},{4,0},{8,4},{12,8},{16,12},{20,16},{24,20},{28,24},{32,28}... | collective-permute-start | bytes 589832 | tf_op jit(solution)/shard_map/ppermute | solution.py:182

commit v9 on v8

--- a/solution.py
+++ b/solution.py
@@ -212,7 +212,7 @@
     right = exchange(to_left, SPACE, tiles, lambda i: (i - 1) % tiles)
 
     half = channels // 2
-    tile, early = batch * cols, 5
+    tile, early = batch * cols, 6
 
     keep = tile + early
     vmem = pl.BlockSpec(memory_space=pltpu.VMEM)

time: 86.8 us -> 125 us (1.44)
  waiting for transfers between devices: 0.01 us -> 18 us
  between operations: 0.88 us -> 14.3 us
  local copies, waits for them, and re-layouts: 1.11 us -> 3.56 us
  starting transfers between devices: 23.9 us -> 25.8 us
  Pallas kernels: 4.9 us -> 6.48 us
    ppermute x4, waiting for transfers between devices: 0.01 us -> 12.2 us  [exchange(): return lax.ppermute(a, axes, [(i, to(i)) for i in range(count)])]
    all_to_all x3, blocking collectives: 46.6 us -> 52.5 us  [everyone(): return lax.all_to_all(a, axes, 0, 0, tiled=True)]
    all_gather x0 -> x2, waiting for transfers between devices: none -> 5.7 us  [gathered(): return lax.all_gather(a, 'core', axis=0, tiled=True)]
    all_gather x3 -> x1, blocking collectives: 7.58 us -> 2.46 us  [gathered(): return lax.all_gather(a, 'core', axis=0, tiled=True)]
    unnamed x4 -> x8, local copies, waits for them, and re-layouts: 0.96 us -> 3.41 us
    ppermute x4, starting transfers between devices: 23.9 us -> 25.7 us  [exchange(): return lax.ppermute(a, axes, [(i, to(i)) for i in range(count)])]
    pallas_call x2, Pallas kernels: 0.14 us -> 1.74 us  [with_weights(): pl.pallas_call(functools.partial(pack_kernel, keep), out_shape=(jax.Shape...]
  transfers between devices with their start and end apart: 4 -> 6, of which waited for: 0 -> 5; matrix products, arithmetic and copies ran while one was open for 0% -> 0% of each run, Pallas kernels for 2% -> 1%
where the time goes in v9:
time: 125 us
  blocking collectives  55 us (44%)
  starting transfers between devices  25.8 us (21%)
  waiting for transfers between devices  18 us (14%)
  between operations  14.3 us (11%)
  Pallas kernels  6.48 us (5%)
  local copies, waits for them, and re-layouts  3.56 us (3%)
  other arithmetic  1.5 us (1%)
    all_to_all x3, blocking collectives, everyone(): return lax.all_to_all(a, axes, 0, 0, tiled=True)  52.5 us
    ppermute x4, starting transfers between devices, exchange(): return lax.ppermute(a, axes, [(i, to(i)) for i in range(count)])  25.7 us
    ppermute x4, waiting for transfers between devices, exchange(): return lax.ppermute(a, axes, [(i, to(i)) for i in range(count)])  12.2 us
    all_gather x2, waiting for transfers between devices, gathered(): return lax.all_gather(a, 'core', axis=0, tiled=True)  5.7 us
    unnamed x8, local copies, waits for them, and re-layouts  3.41 us
  transfers between devices with their start and end apart: 6, of which 5 were waited for; matrix products, arithmetic and copies ran while one was open for 0% of the time, Pallas kernels for 1%

profile of v9, /device:TPU:6, one launch (start us, length us, event | category | flops | bytes accessed | tf_op | source)
XLA Modules:
  0.0 124.6 jit_solution(10454038800779559402)
XLA Ops:
  7.2 0.0 copy-start.1
  7.2 0.0 all-gather.3.cloned.1.call-start
  7.2 1.0 pad_maximum_fusion.2.pack_ref
  8.3 0.0 copy-start
  8.3 1.0 copy-done
  9.2 0.9 pack.2
  10.1 0.0 all-gather.3.cloned.1.call-update
  10.1 0.0 all-gather.5.cloned.1.call-start
  10.2 3.3 %collective-permute-start = (bf16[16,64,128]{2,1,0:T(8,128)(2,1)S(1)}, bf16[16,64,128]{2,1,0:T(8,128)(2,1)S(1)}, u32[]{:S(2)}, u32[]{:S(2)}) collective-permute-start(bf16[16,64,128]{2,1,0:T(8,128)(2,1)S(1)} %pad_maximum_fusion.2.pack_ref), channel_id=1, source_target_pairs={{0,2},{2,0},{1,3},{3,1},{4,6},{6,4},{5,7},{7,5},{8,10},{10,8},{9,1... | collective-permute-start | bytes 786440 | tf_op jit(solution)/shard_map/ppermute | solution.py:182
  13.5 6.4 %collective-permute-start.1 = (bf16[3,3,64,256]{3,2,1,0:T(8,128)(2,1)S(1)}, bf16[3,3,64,256]{3,2,1,0:T(8,128)(2,1)S(1)}, u32[]{:S(2)}, u32[]{:S(2)}) collective-permute-start(bf16[3,3,64,256]{3,2,1,0:T(8,128)(2,1)S(1)} %copy-done.1), channel_id=1, source_target_pairs={{0,258},{2,256},{256,2},{258,0},{1,259},{3,257},{257,3},{259,1},{4... | collective-permute-start | bytes 884744 | tf_op jit(solution)/shard_map/ppermute | solution.py:182
  20.0 1.7 %collective-permute-done.pack_ref = bf16[16,64,128]{2,1,0:T(8,128)(2,1)S(1)} collective-permute-done((bf16[16,64,128]{2,1,0:T(8,128)(2,1)S(1)}, bf16[16,64,128]{2,1,0:T(8,128)(2,1)S(1)}, u32[]{:S(2)}, u32[]{:S(2)}) %collective-permute-start) | collective-permute-done | bytes 262176 | tf_op jit(solution)/shard_map/ppermute | solution.py:182
  21.7 6.2 %collective-permute-done.1.w_ref = bf16[3,3,64,256]{3,2,1,0:T(8,128)(2,1)S(1)} collective-permute-done((bf16[3,3,64,256]{3,2,1,0:T(8,128)(2,1)S(1)}, bf16[3,3,64,256]{3,2,1,0:T(8,128)(2,1)S(1)}, u32[]{:S(2)}, u32[]{:S(2)}) %collective-permute-start.1) | collective-permute-done | bytes 294944 | tf_op jit(solution)/shard_map/ppermute | solution.py:182
  27.9 0.9 pack.3
  28.8 0.0 all-gather.5.cloned.1.call-update
  28.9 3.8 %collective-permute-start.2 = (bf16[12,64,128]{2,1,0:T(8,128)(2,1)S(1)}, bf16[12,64,128]{2,1,0:T(8,128)(2,1)S(1)}, u32[]{:S(2)}, u32[]{:S(2)}) collective-permute-start(bf16[12,64,128]{2,1,0:T(8,128)(2,1)S(1)} %pad_maximum_fusion.3), channel_id=1, source_target_pairs={{0,4},{4,8},{8,12},{12,16},{16,20},{20,24},{24,28},{28,32},{32,36}... | collective-permute-start | bytes 589832 | tf_op jit(solution)/shard_map/ppermute | solution.py:182
  32.8 12.2 %collective-permute-start.3 = (bf16[12,64,128]{2,1,0:T(8,128)(2,1)S(1)}, bf16[12,64,128]{2,1,0:T(8,128)(2,1)S(1)}, u32[]{:S(2)}, u32[]{:S(2)}) collective-permute-start(bf16[12,64,128]{2,1,0:T(8,128)(2,1)S(1)} %pad_maximum_fusion.4), channel_id=1, source_target_pairs={{0,508},{4,0},{8,4},{12,8},{16,12},{20,16},{24,20},{28,24},{32,28}... | collective-permute-start | bytes 589832 | tf_op jit(solution)/shard_map/ppermute | solution.py:182
  45.0 3.1 %collective-permute-done.2 = bf16[12,64,128]{2,1,0:T(8,128)(2,1)S(1)} collective-permute-done((bf16[12,64,128]{2,1,0:T(8,128)(2,1)S(1)}, bf16[12,64,128]{2,1,0:T(8,128)(2,1)S(1)}, u32[]{:S(2)}, u32[]{:S(2)}) %collective-permute-start.2) | collective-permute-done | bytes 196640 | tf_op jit(solution)/shard_map/ppermute | solution.py:182
  48.1 1.2 collective-permute-done.3
  49.3 0.1 pad_maximum_fusion
  49.4 2.5 %all_gather.11.rim_ref = bf16[56,64,128]{2,1,0:T(8,128)(2,1)S(1)} all-gather(bf16[28,64,128]{2,1,0:T(8,128)(2,1)S(1)} %pad_maximum_fusion), channel_id=1, replica_groups=mesh['xlo'=2,'y'=4,'zhi'=8,'zlo'=2,'xhi'=2,'core'=2] {'core'}, dimensions={0}, use_global_device_ids=true | all-gather | bytes 1376256 | tf_op jit(solution)/shard_map/all_gather | solution.py:193
  51.9 5.7 %all-gather.5.cloned.1.call-done.far_ref = bf16[64,64,128]{2,1,0:T(8,128)(2,1)} async-done(((bf16[32,64,128]{2,1,0:T(8,128)(2,1)}), bf16[64,64,128]{2,1,0:T(8,128)(2,1)}) %all-gather.5.cloned.1.call-update) | async-done | bytes 1048592 | tf_op jit(solution)/shard_map/all_gather | solution.py:193
  57.6 1.2 copy-done.2
  58.8 1.2 copy-done.3
  60.0 1.6 %conv_tile.1 = (bf16[3,256,768]{2,1,0:T(8,128)(2,1)S(1)}, bf16[768,1024]{1,0:T(8,128)(2,1)S(1)}, f32[256,1536]{1,0:T(8,128)S(1)}) custom-call(bf16[64,64,128]{2,1,0:T(8,128)(2,1)S(1)} %copy-done.2, bf16[64,64,128]{2,1,0:T(8,128)(2,1)S(1)} %copy-done.3), custom_call_target="tpu_custom_call" | custom-call | flops 1207959552 | bytes 6291456 | tf_op jit(solution)/shard_map/conv_tile/pallas_call | solution.py:244
  61.6 2.3 %conv_rim.1 = (bf16[2,4,64,128]{3,2,1,0:T(8,128)(2,1)}, bf16[2,3,3,64,128]{4,3,2,1,0:T(8,128)(2,1)S(1)}, f32[8,128]{1,0:T(8,128)S(1)}) custom-call(bf16[64,64,128]{2,1,0:T(8,128)(2,1)S(1)} %copy-done.2, bf16[64,64,128]{2,1,0:T(8,128)(2,1)S(1)} %copy-done.3, bf16[56,64,128]{2,1,0:T(8,128)(2,1)S(1)} %all_gather.11.rim_ref, ...), custom_call_target="tpu_custom_call" | custom-call | tf_op jit(solution)/shard_map/conv_rim/pallas_call | solution.py:259
  63.9 0.1 fusion.3
  64.0 14.3 %all_to_all.15 = bf16[16,80,128]{2,1,0:T(8,128)(2,1)S(1)} all-to-all(bf16[16,80,128]{2,1,0:T(8,128)(2,1)S(1)} %pad_maximum_fusion.1), channel_id=1, replica_groups=mesh['xlo'=2,'y'=4,'zhi'=8,'zlo'=2,'xhi'=2,'core'=2] {'xlo','y','zlo'}, dimensions={0} | all-to-all | bytes 655360 | tf_op jit(solution)/shard_map/all_to_all | solution.py:289
  78.3 0.1 convert_reduce_fusion
  78.4 0.1 fusion.4
  78.5 27.8 %all_to_all.16 = bf16[8,80,128]{2,1,0:T(8,128)(2,1)S(1)} all-to-all(bf16[8,80,128]{2,1,0:T(8,128)(2,1)S(1)} %pad_maximum_fusion.5), channel_id=1, replica_groups=mesh['xlo'=2,'y'=4,'zhi'=8,'zlo'=2,'xhi'=2,'core'=2] {'zhi'}, dimensions={0} | all-to-all | bytes 327680 | tf_op jit(solution)/shard_map/all_to_all | solution.py:289
  106.5 10.4 %all_to_all.17 = bf16[16,72,128]{2,1,0:T(8,128)(2,1)S(1)} all-to-all(bf16[16,72,128]{2,1,0:T(8,128)(2,1)S(1)} %broadcast_in_dim.30), channel_id=1, replica_groups=mesh['xlo'=2,'y'=4,'zhi'=8,'zlo'=2,'xhi'=2,'core'=2] {'xlo','y','zlo'}, dimensions={0} | all-to-all | bytes 589824 | tf_op jit(solution)/shard_map/all_to_all | solution.py:289
  116.8 0.9 widen.1
  (27 shorter events, 0.4 us)
Async XLA Ops:
  7.2 6.3 %copy-start.1 = (bf16[3,3,64,256]{3,2,1,0:T(8,128)(2,1)S(1)}, bf16[3,3,64,256]{3,2,1,0:T(8,128)(2,1)}, u32[]{:S(2)}) copy-start(bf16[3,3,64,256]{3,2,1,0:T(8,128)(2,1)} %w_ref.1) | copy-start | bytes 884740
  7.2 44.7 %all-gather.3.cloned.1.call-start = ((), (), s32[]{:S(2)}) async-start(), calls=%async_computation.3 | async-start | bytes 1572864 | tf_op jit(solution)/shard_map/all_gather | solution.py:193
  8.3 1.0 copy-start
  10.1 47.4 %all-gather.5.cloned.1.call-start = ((), (), s32[]{:S(2)}) async-start(), calls=%async_computation.4 | async-start | bytes 1572864 | tf_op jit(solution)/shard_map/all_gather | solution.py:193
  10.2 11.5 %collective-permute-start = (bf16[16,64,128]{2,1,0:T(8,128)(2,1)S(1)}, bf16[16,64,128]{2,1,0:T(8,128)(2,1)S(1)}, u32[]{:S(2)}, u32[]{:S(2)}) collective-permute-start(bf16[16,64,128]{2,1,0:T(8,128)(2,1)S(1)} %pad_maximum_fusion.2.pack_ref), channel_id=1, source_target_pairs={{0,2},{2,0},{1,3},{3,1},{4,6},{6,4},{5,7},{7,5},{8,10},{10,8},{9,1... | collective-permute-start | bytes 786440 | tf_op jit(solution)/shard_map/ppermute | solution.py:182
  13.5 14.4 %collective-permute-start.1 = (bf16[3,3,64,256]{3,2,1,0:T(8,128)(2,1)S(1)}, bf16[3,3,64,256]{3,2,1,0:T(8,128)(2,1)S(1)}, u32[]{:S(2)}, u32[]{:S(2)}) collective-permute-start(bf16[3,3,64,256]{3,2,1,0:T(8,128)(2,1)S(1)} %copy-done.1), channel_id=1, source_target_pairs={{0,258},{2,256},{256,2},{258,0},{1,259},{3,257},{257,3},{259,1},{4... | collective-permute-start | bytes 884744 | tf_op jit(solution)/shard_map/ppermute | solution.py:182
  28.9 19.2 %collective-permute-start.2 = (bf16[12,64,128]{2,1,0:T(8,128)(2,1)S(1)}, bf16[12,64,128]{2,1,0:T(8,128)(2,1)S(1)}, u32[]{:S(2)}, u32[]{:S(2)}) collective-permute-start(bf16[12,64,128]{2,1,0:T(8,128)(2,1)S(1)} %pad_maximum_fusion.3), channel_id=1, source_target_pairs={{0,4},{4,8},{8,12},{12,16},{16,20},{20,24},{24,28},{28,32},{32,36}... | collective-permute-start | bytes 589832 | tf_op jit(solution)/shard_map/ppermute | solution.py:182
  32.8 16.5 %collective-permute-start.3 = (bf16[12,64,128]{2,1,0:T(8,128)(2,1)S(1)}, bf16[12,64,128]{2,1,0:T(8,128)(2,1)S(1)}, u32[]{:S(2)}, u32[]{:S(2)}) collective-permute-start(bf16[12,64,128]{2,1,0:T(8,128)(2,1)S(1)} %pad_maximum_fusion.4), channel_id=1, source_target_pairs={{0,508},{4,0},{8,4},{12,8},{16,12},{20,16},{24,20},{28,24},{32,28}... | collective-permute-start | bytes 589832 | tf_op jit(solution)/shard_map/ppermute | solution.py:182
  57.6 1.2 copy-start.2
  58.8 1.2 copy-start.3
Sparse Core Ops, SparseCore 0:
  10.7 23.8 all-gather.2
  36.7 20.8 all-gather.4
